TPU v7x, 32 devices: a whole 2x2x4 slice. The times are simulated.
32 devices in a mesh: dp: 8 (over y, x, core), mp: 4 (over z).
Axes of the slice: x: 2, y: 2, z: 4, core: 2. Of those that a mesh axis runs over, the one named last changes fastest.
Arguments:
- pooled: bfloat16 [4096, 512], P('dp', 'mp')
- delta: bfloat16 [4096, 2048], P('dp')
- w_first: bfloat16 [512, 2048], P('mp'), may hold values from -0.25 to 0.25
- lookup_slot: int32 [4096, 4, 8], P('dp', 'mp'), may hold values from 0 to 1023, as said below
- row_ids: int32 [8, 4, 1024], P('dp', 'mp'), may hold values from 0 to 511, as said below
- send_counts: int32 [8, 4, 4], P('dp', 'mp'), may hold values from 32 to 256, as said below
Outputs:
- dense_grad: float32 [512, 2048], P('mp')
- table_grad: float32 [8, 4, 2048, 128], P('dp', None, 'mp')
Inputs may be any that keep to these rules, and one draw needn't show every extreme that they name: `lookup_slot`: within one block (d, t), every entry k below the sum of send_counts[d, t, :] is named by at least one lookup of that block's examples, and no lookup names a larger entry. `row_ids`: within one block and one owner's entries the row numbers are distinct; entries past the block's total are 0. `send_counts`: in every block (d, t) some owner gets exactly 256 entries.
All inputs are finite; a program needn't handle non-finite values.
Results may differ from a plain program's by a relative error of at most 0.0028.
Values sent between devices are 32-bit elements; how exact they have to be, the bound alone decides.
No kernel may reach another device: no remote copies, remote signals or barrier semaphores. Data moves between devices by JAX's collectives and lax.ppermute only.
A program may use at most 64 MiB of HBM per device.

v0:
```python
import jax
import jax.numpy as jnp
from jax import lax
from jax.sharding import PartitionSpec as P

CAP = 256
ROWS_DEV = 512


CLIP_NORM = 8.0
EPSILON = 1e-06


def on_device(pooled, delta, w_first, lookup_slot, row_ids, send_counts):
    owners = lax.axis_size("mp")
    width_emb = pooled.shape[1]
    xgrad = lax.dot_general(
        delta, w_first, (((1,), (1,)), ((), ())), preferred_element_type=jnp.float32
    )
    slots = lookup_slot[:, 0, :]
    repeats = jnp.sum((slots[:, :, None] == slots[:, None, :]).astype(jnp.float32), axis=(1, 2))
    pooled_wide = pooled.astype(jnp.float32)
    local_sq = jnp.sum(pooled_wide * pooled_wide, axis=1)
    embed_sq = repeats * jnp.sum(xgrad * xgrad, axis=1)
    total_sq, total_embed = lax.psum((local_sq, embed_sq), "mp")
    delta_wide = delta.astype(jnp.float32)
    delta_sq = jnp.sum(delta_wide * delta_wide, axis=1)
    norm_sq = delta_sq * total_sq + total_embed
    clip = jnp.minimum(1.0, CLIP_NORM / jnp.sqrt(norm_sq + EPSILON))
    scaled = (pooled_wide * clip[:, None]).astype(jnp.bfloat16)
    local_dense = lax.dot_general(
        scaled, delta, (((0,), (0,)), ((), ())), preferred_element_type=jnp.float32
    )
    dense_grad = lax.psum(local_dense, "dp")
    contrib = xgrad * clip[:, None]
    empty = jnp.zeros((owners, ROWS_DEV, width_emb), jnp.float32)
    width = row_ids.shape[-1]
    per_look = slots.shape[1]
    unique = jax.ops.segment_sum(
        jnp.repeat(contrib, per_look, axis=0), slots.reshape(-1), num_segments=width
    )
    counts = send_counts[0, 0]
    offsets = jnp.cumsum(counts) - counts
    places = jnp.arange(CAP, dtype=jnp.int32)
    valid = places[None, :] < counts[:, None]
    index = jnp.minimum(offsets[:, None] + places[None, :], width - 1)
    packed = jnp.where(valid[:, :, None], unique[index], 0.0)
    targets = jnp.where(valid, row_ids[0, 0][index], 0)
    arrived, arrived_ids = (
        lax.all_to_all(packed, "mp", split_axis=0, concat_axis=0, tiled=True),
        lax.all_to_all(targets, "mp", split_axis=0, concat_axis=0, tiled=True),
    )
    sources = jnp.broadcast_to(jnp.arange(owners, dtype=jnp.int32)[:, None], arrived_ids.shape)
    table_grad = empty.at[sources, arrived_ids].add(arrived)
    return (dense_grad, table_grad[None])


def solution(mesh):
    placed = (
        P("dp", "mp"),
        P("dp", None),
        P("mp", None),
        P("dp", "mp", None),
        P("dp", "mp", None),
        P("dp", "mp", None),
    )
    return jax.shard_map(
        on_device,
        mesh=mesh,
        in_specs=placed,
        out_specs=(P("mp", None), P("dp", None, "mp", None)),
        check_vma=False,
    )
```

profile of v0, /device:TPU:0, one launch (start us, length us, event | category | flops | bytes accessed | tf_op | source)
XLA Modules:
  0.0 139.2 jit_solution(13803483939607723858)
XLA Ops:
  7.2 0.0 copy-start
  7.2 0.0 copy-start.1
  7.2 0.9 reduce-window.8
  8.1 0.7 bitcast_subtract_fusion
  8.7 0.1 fusion.11
  8.8 0.0 copy-done.1
  8.8 0.0 copy-start.5
  8.8 0.0 copy-start.4
  8.9 0.0 copy-start.3
  8.9 0.0 copy-start.2
  8.9 4.5 %gather_fusion = s32[1024]{0:T(1024)S(1)} fusion(s32[1024]{0:T(1024)S(1)} %bitcast.28, s32[1024]{0:T(1024)S(1)} %broadcast_clamp_fusion), kind=kCustom, calls=%fused_computation | custom fusion | bytes 12288 | tf_op jit(solution)/shard_map/gather | solution.py:48
  13.4 0.0 copy-done.5
  13.4 0.7 compare_select_fusion
  14.1 6.3 %all-to-all-start = ((s32[4,1,256]{2,1,0:T(1,128)}), s32[4,1,256]{2,1,0:T(1,128)S(1)}, u32[]{:S(2)}, u32[]{:S(2)}) async-start(s32[4,1,256]{2,1,0:T(1,128)} %compare_select_fusion), calls=%async_computation | async-start | bytes 8192 | tf_op jit(solution)/shard_map/all_to_all | solution.py:51
  20.4 0.1 iota_compare_fusion
  20.5 0.0 copy-done.4
  20.5 0.1 copy.22
  20.6 0.0 copy-done.3
  20.6 0.1 copy.23
  20.8 0.0 copy-done.2
  20.8 0.5 multiply_reduce_fusion
  21.3 0.0 copy-done
  21.3 0.8 multiply_reduce_fusion.1
  22.2 0.8 reshape.216
  22.9 12.2 %all-reduce = (f32[512]{0:T(512)S(1)}, f32[512]{0:T(512)S(1)}) all-reduce(f32[512]{0:T(512)S(1)} %mul.33, f32[512]{0:T(512)S(1)} %fusion.5), channel_id=1, replica_groups=mesh['dp'=8,'mp'=4] {'mp'}, use_global_device_ids=true, to_apply=%region_5.0 | all-reduce | flops 1024 | bytes 8192 | tf_op jit(solution)/shard_map/psum | solution.py:25
  35.1 0.1 copy.24
  35.3 22.6 %scatter_custom_fusion = f32[1024,128]{1,0:T(8,128)S(1)} fusion(s32[4096]{0:T(1024)} %reshape.216, f32[512,128]{1,0:T(8,128)S(1)} %copy.24, f32[]{:T(128)} %constant.9.clone.1), kind=kCustom, calls=%fused_computation.5 | custom fusion | flops 524288 | bytes 786944 | tf_op jit(solution)/shard_map/scatter-add | solution.py:39
  57.9 4.0 %gather_fusion.1 = f32[1024,128]{1,0:T(8,128)} fusion(f32[1024,128]{1,0:T(8,128)S(1)} %scatter_custom_fusion, s32[1024]{0:T(1024)S(1)} %broadcast_clamp_fusion), kind=kCustom, calls=%fused_computation.1 | custom fusion | bytes 1052672 | tf_op jit(solution)/shard_map/gather | solution.py:47
  61.9 2.0 %broadcast_select_fusion = f32[4,256,128]{2,1,0:T(8,128)} fusion(f32[4,256,128]{2,1,0:T(8,128)} %bitcast.29, pred[4,256]{1,0:T(4,128)(4,1)S(1)} %iota_compare_fusion), kind=kLoop, calls=%fused_computation.14 | loop fusion | flops 131072 | bytes 1049600 | tf_op jit(solution)/shard_map/jit(_where)/select_n | solution.py:47
  64.0 0.0 all-to-all-done
  64.0 3.5 %all-to-all-start.1 = ((f32[4,256,128]{2,1,0:T(8,128)}), f32[4,256,128]{2,1,0:T(8,128)S(1)}, u32[]{:S(2)}, u32[]{:S(2)}) async-start(f32[4,256,128]{2,1,0:T(8,128)} %broadcast_select_fusion), calls=%async_computation.1 | async-start | bytes 1048576 | tf_op jit(solution)/shard_map/all_to_all | solution.py:50
  67.5 0.0 copy-start.7
  67.5 0.0 copy-start.6
  67.5 0.0 all-reduce.3.cloned.1.call-start
  67.5 1.4 %fusion.8 = f32[128,2048]{1,0:T(8,128)} fusion(bf16[512,2048]{1,0:T(8,128)(2,1)S(1)} %copy-done.2, bf16[512,128]{0,1:T(8,128)(2,1)S(1)} %copy.22, f32[512]{0:T(512)S(1)} %multiply_minimum_fusion), kind=kOutput, calls=%fused_computation.17 | convolution fusion | flops 268632064 | bytes 3278848 | tf_op jit(solution)/shard_map/dot_general | solution.py:31
  69.0 0.0 all-reduce.3.cloned.1.call-update
  69.0 0.0 copy-done.7
  69.0 0.1 multiply_reduce_fusion.2
  69.1 0.0 copy-done.6
  69.1 0.1 and_reduce_fusion
  69.2 10.4 %all-to-all-done.1 = f32[4,256,128]{2,1,0:T(8,128)S(1)} async-done(((f32[4,256,128]{2,1,0:T(8,128)}), f32[4,256,128]{2,1,0:T(8,128)S(1)}, u32[]{:S(2)}, u32[]{:S(2)}) %all-to-all-start.1) | async-done | bytes 524320 | tf_op jit(solution)/shard_map/all_to_all | solution.py:50
  79.6 7.6 %scatter_custom_fusion.1 = f32[2048,128]{1,0:T(8,128)} fusion(s32[1024]{0:T(1024)S(1)} %bitcast.35, f32[1024,128]{1,0:T(8,128)S(1)} %bitcast.31, f32[]{:T(128)} %constant.9.clone.1), kind=kCustom, calls=%fused_computation.8 | custom fusion | flops 131072 | bytes 1048580
  87.2 42.9 %all-reduce.3.cloned.1.call-done = f32[128,2048]{1,0:T(8,128)} async-done(((f32[128,2048]{1,0:T(8,128)}), f32[128,2048]{1,0:T(8,128)}) %all-reduce.3.cloned.1.call-update) | async-done | bytes 1048592 | tf_op jit(solution)/shard_map/psum | solution.py:34
  130.1 2.3 %copy.30 = f32[128,2048]{1,0:T(8,128)} copy(f32[128,2048]{1,0:T(8,128)} %all-reduce.3.cloned.1.call-done) | data formatting | bytes 2097152
  (11 shorter events, 0.2 us)
Async XLA Ops:
  7.2 14.1 %copy-start = (bf16[128,2048]{1,0:T(8,128)(2,1)S(1)}, bf16[128,2048]{1,0:T(8,128)(2,1)}, u32[]{:S(2)}) copy-start(bf16[128,2048]{1,0:T(8,128)(2,1)} %param.8) | copy-start | bytes 1572868
  7.2 1.6 %copy-start.1 = (s32[1,1,1024]{2,1,0:T(1,128)S(1)}, s32[1,1,1024]{2,1,0:T(1,128)}, u32[]{:S(2)}) copy-start(s32[1,1,1024]{2,1,0:T(1,128)} %param.10) | copy-start | bytes 12292
  8.8 4.6 %copy-start.5 = (s32[1,1,4]{2,1,0:T(1,128)S(1)}, s32[1,1,4]{2,1,0:T(1,128)}, u32[]{:S(2)}) copy-start(s32[1,1,4]{2,1,0:T(1,128)} %param.11) | copy-start | bytes 52
  8.8 11.6 %copy-start.4 = (bf16[512,128]{1,0:T(8,128)(2,1)S(1)}, bf16[512,128]{1,0:T(8,128)(2,1)}, u32[]{:S(2)}) copy-start(bf16[512,128]{1,0:T(8,128)(2,1)} %param.6) | copy-start | bytes 393220
  8.9 11.8 %copy-start.3 = (s32[512,1,8]{0,2,1:T(8,128)S(1)}, s32[512,1,8]{0,2,1:T(8,128)}, u32[]{:S(2)}) copy-start(s32[512,1,8]{0,2,1:T(8,128)} %param.9) | copy-start | bytes 49156
  8.9 11.9 %copy-start.2 = (bf16[512,2048]{1,0:T(8,128)(2,1)S(1)}, bf16[512,2048]{1,0:T(8,128)(2,1)}, u32[]{:S(2)}) copy-start(bf16[512,2048]{1,0:T(8,128)(2,1)} %param.7) | copy-start | bytes 6291460
  14.1 49.9 %all-to-all-start = ((s32[4,1,256]{2,1,0:T(1,128)}), s32[4,1,256]{2,1,0:T(1,128)S(1)}, u32[]{:S(2)}, u32[]{:S(2)}) async-start(s32[4,1,256]{2,1,0:T(1,128)} %compare_select_fusion), calls=%async_computation | async-start | bytes 8192 | tf_op jit(solution)/shard_map/all_to_all | solution.py:51
  64.0 15.6 %all-to-all-start.1 = ((f32[4,256,128]{2,1,0:T(8,128)}), f32[4,256,128]{2,1,0:T(8,128)S(1)}, u32[]{:S(2)}, u32[]{:S(2)}) async-start(f32[4,256,128]{2,1,0:T(8,128)} %broadcast_select_fusion), calls=%async_computation.1 | async-start | bytes 1048576 | tf_op jit(solution)/shard_map/all_to_all | solution.py:50
  67.5 1.5 %copy-start.7 = (s32[2]{0:T(128)S(1)}, s32[2]{0:T(128)}, u32[]{:S(2)}) copy-start(s32[2]{0:T(128)} %constant.27) | copy-start | bytes 28
  67.5 1.6 %copy-start.6 = (s32[2]{0:T(128)S(1)}, s32[2]{0:T(128)}, u32[]{:S(2)}) copy-start(s32[2]{0:T(128)} %constant.30) | copy-start | bytes 28
  67.5 62.6 %all-reduce.3.cloned.1.call-start = ((), (), s32[]{:S(2)}) async-start(), calls=%async_computation.2 | async-start | bytes 2097152 | tf_op jit(solution)/shard_map/psum | solution.py:34
Sparse Core Ops, SparseCore 0:
  72.1 57.9 all-reduce.2
where the time goes:
time: 140 us; the launch traced here: 139 us
  waiting for transfers between devices  53.3 us (38%)
  other arithmetic  35.4 us (25%)
  between operations  14.2 us (10%)
  blocking collectives  12.2 us (9%)
  local copies, waits for them, and re-layouts  12 us (9%)
  starting transfers between devices  9.83 us (7%)
  matrix products  2.27 us (2%)
    psum x1, waiting for transfers between devices, on_device(): dense_grad = lax.psum(local_dense, 'dp')  42.9 us
    scatter-add x1, other arithmetic, on_device(): jax.ops.segment_sum(jnp.repeat(contrib, per_look, axis=0), slots.reshape(...  22.6 us
    psum x1, blocking collectives, on_device(): total_sq, total_embed = lax.psum((local_sq, embed_sq), 'mp')  12.2 us
    all_to_all x1, waiting for transfers between devices, on_device(): lax.all_to_all(packed, 'mp', split_axis=0, concat_axis=0, tiled=True)  10.4 us
    unnamed x5, other arithmetic  7.81 us
    all_to_all x1, starting transfers between devices, on_device(): lax.all_to_all(targets, 'mp', split_axis=0, concat_axis=0, tiled=True)  6.32 us
    gather x1, local copies, waits for them, and re-layouts, on_device(): targets = jnp.where(valid, row_ids[0, 0][index], 0)  4.53 us
    gather x1, local copies, waits for them, and re-layouts, on_device(): packed = jnp.where(valid[:, :, None], unique[index], 0.0)  4.04 us
  transfers between devices with their start and end apart: 3, of which 2 were waited for; matrix products, arithmetic and copies ran while one was open for 29% of the time, Pallas kernels for 0%

commit v1 on v0

v1 whole, which is shorter than its diff:
```python
import jax
import jax.numpy as jnp
from jax import lax
from jax.sharding import PartitionSpec as P

ROWS_DEV = 512
CLIP_NORM = 8.0
EPSILON = 1e-06


def peers(n):
    if n & (n - 1) == 0:
        return [[(i, i ^ s) for i in range(n)] for s in range(1, n)]
    return [[(i, (i + s) % n) for i in range(n)] for s in range(1, n)]


def peer_to(me, s, n):
    return me ^ s if n & (n - 1) == 0 else lax.rem(me + s, n)


def peer_from(me, s, n):
    return me ^ s if n & (n - 1) == 0 else lax.rem(me + n - s, n)


def split(x):
    hi = lax.reduce_precision(x, 8, 7)
    return hi.astype(jnp.bfloat16), (x - hi).astype(jnp.bfloat16)


def dense_sum(local, n_dp):
    if n_dp != 8:
        return lax.psum(local, "dp")
    rows = local.shape[0]
    half, part = rows // 2, rows // 8
    me = lax.axis_index("dp")
    core, chip = me & 1, me >> 1
    swap = [(i, i ^ 1) for i in range(8)]
    theirs = lax.dynamic_slice_in_dim(local, (1 - core) * half, half, 0)
    mine = lax.dynamic_slice_in_dim(local, core * half, half, 0)
    mine = mine + lax.ppermute(theirs, "dp", swap)
    total = lax.dynamic_slice_in_dim(mine, chip * part, part, 0)
    got = []
    for s in (1, 2, 3):
        piece = lax.dynamic_slice_in_dim(mine, (chip ^ s) * part, part, 0)
        got.append(lax.ppermute(piece, "dp", [(i, i ^ (2 * s)) for i in range(8)]))
    total = total + got[0] + got[1] + got[2]
    own = jnp.zeros((half, local.shape[1]), jnp.float32)
    own = lax.dynamic_update_slice_in_dim(own, total, chip * part, 0)
    for s in (1, 2, 3):
        piece = lax.ppermute(total, "dp", [(i, i ^ (2 * s)) for i in range(8)])
        own = lax.dynamic_update_slice_in_dim(own, piece, (chip ^ s) * part, 0)
    other = lax.ppermute(own, "dp", swap)
    out = jnp.zeros(local.shape, jnp.float32)
    out = lax.dynamic_update_slice_in_dim(out, own, core * half, 0)
    return lax.dynamic_update_slice_in_dim(out, other, (1 - core) * half, 0)


def on_device(pooled, delta, w_first, lookup_slot, row_ids, send_counts):
    owners = lax.axis_size("mp")
    n_dp = lax.axis_size("dp")
    me = lax.axis_index("mp")
    width = row_ids.shape[-1]
    cap = width // owners
    xgrad = lax.dot_general(
        w_first, delta, (((1,), (1,)), ((), ())), preferred_element_type=jnp.float32
    )
    slots = lookup_slot[:, 0, :].T
    looks = slots.shape[0]
    pairs = jnp.zeros(slots.shape[1:], jnp.float32)
    for a in range(looks):
        for b in range(a):
            pairs = pairs + (slots[a] == slots[b]).astype(jnp.float32)
    repeats = looks + 2.0 * pairs
    pooled_t = pooled.astype(jnp.float32).T
    delta_wide = delta.astype(jnp.float32)
    partial = jnp.sum(delta_wide * delta_wide, axis=1) * jnp.sum(pooled_t * pooled_t, axis=0)
    partial = partial + repeats * jnp.sum(xgrad * xgrad, axis=0)

    counts = send_counts[0, 0]
    order = jnp.arange(owners, dtype=jnp.int32)
    ids = jnp.pad(row_ids[0, 0], (0, cap))
    place = jnp.arange(cap, dtype=jnp.int32)
    names, targets = [], []
    for s in range(owners):
        owner = peer_to(me, s, owners)
        start = jnp.sum(jnp.where(order < owner, counts, 0))
        count = jnp.sum(jnp.where(order == owner, counts, 0))
        names.append(jnp.where(place < count, start + place, -1))
        targets.append(jnp.where(place < count, lax.dynamic_slice_in_dim(ids, start, cap, 0), -1))
    perms = peers(owners)
    norm_sq, rows = partial, [targets[0]]
    arrived = []
    for s in range(1, owners):
        message = jnp.concatenate([partial, targets[s].astype(jnp.float32)])
        arrived.append(lax.ppermute(message, "mp", perms[s - 1]))
    for message in arrived:
        norm_sq = norm_sq + message[: partial.shape[0]]
        rows.append(message[partial.shape[0]:].astype(jnp.int32))
    names = jnp.concatenate(names)
    named = jnp.zeros((width, slots.shape[1]), jnp.float32)
    for a in range(looks):
        named = named + (slots[a][None, :] == names[:, None]).astype(jnp.float32)
    named = named.astype(jnp.bfloat16)

    clip = jnp.minimum(1.0, CLIP_NORM / jnp.sqrt(norm_sq + EPSILON))
    scaled = (pooled_t * clip[None, :]).astype(jnp.bfloat16)
    local_dense = jnp.dot(scaled, delta, preferred_element_type=jnp.float32)
    hi, lo = split(xgrad * clip[None, :])
    both = lax.dot_general(
        named, jnp.concatenate([hi, lo]), (((1,), (1,)), ((), ())),
        preferred_element_type=jnp.float32,
    )
    emb = hi.shape[0]
    unique = both[:, :emb] + both[:, emb:]
    dense_grad = dense_sum(local_dense, n_dp)

    received = [unique[:cap]]
    for s in range(1, owners):
        received.append(lax.ppermute(unique[s * cap:(s + 1) * cap], "mp", perms[s - 1]))
    row = jnp.arange(ROWS_DEV, dtype=jnp.int32)
    table_grad = jnp.zeros((owners, ROWS_DEV, emb), jnp.float32)
    for s in range(owners):
        hi, lo = split(received[s])
        hot = (row[:, None] == rows[s][None, :]).astype(jnp.bfloat16)
        placed = jnp.dot(hot, jnp.concatenate([hi, lo], axis=1), preferred_element_type=jnp.float32)
        placed = placed[:, :emb] + placed[:, emb:]
        table_grad = lax.dynamic_update_slice_in_dim(
            table_grad, placed[None], peer_from(me, s, owners), 0
        )
    return (dense_grad, table_grad[None])


def solution(mesh):
    placed = (
        P("dp", "mp"),
        P("dp", None),
        P("mp", None),
        P("dp", "mp", None),
        P("dp", "mp", None),
        P("dp", "mp", None),
    )
    return jax.shard_map(
        on_device,
        mesh=mesh,
        in_specs=placed,
        out_specs=(P("mp", None), P("dp", None, "mp", None)),
        check_vma=False,
    )
```

time: 140 us -> 65.8 us (0.47)
  waiting for transfers between devices: 53.3 us -> 20.5 us
  other arithmetic: 35.4 us -> 12.1 us
  blocking collectives: 12.2 us -> 0 us
  local copies, waits for them, and re-layouts: 12 us -> 2.42 us
  starting transfers between devices: 9.83 us -> 17.4 us
  between operations: 14.2 us -> 8.41 us
  matrix products: 2.27 us -> 4.41 us
    psum x1 -> x0, waiting for transfers between devices: 42.9 us -> none  [on_device(): dense_grad = lax.psum(local_dense, 'dp')]
    scatter-add x1 -> x0, other arithmetic: 22.6 us -> none  [on_device(): jax.ops.segment_sum(jnp.repeat(contrib, per_look, axis=0), slots.reshape(...]
    ppermute x0 -> x14, waiting for transfers between devices: none -> 20.5 us  [the longest x3 8.6 us: on_device(): lax.ppermute(unique[s * cap:(s + 1) * cap], 'mp', perms[s - 1])]
    ppermute x0 -> x14, starting transfers between devices: none -> 17.4 us  [the longest x3 5.68 us: on_device(): arrived.append(lax.ppermute(message, 'mp', perms[s - 1]))]
    psum x1 -> x0, blocking collectives: 12.2 us -> none  [on_device(): total_sq, total_embed = lax.psum((local_sq, embed_sq), 'mp')]
    all_to_all x2 -> x0, waiting for transfers between devices: 10.4 us -> none  [the longest x1 10.4 us: on_device(): lax.all_to_all(packed, 'mp', split_axis=0, concat_axis=0, tiled=True)]
    all_to_all x2 -> x0, starting transfers between devices: 9.79 us -> none  [the longest x1 6.32 us: on_device(): lax.all_to_all(targets, 'mp', split_axis=0, concat_axis=0, tiled=True)]
    gather x2 -> x0, local copies, waits for them, and re-layouts: 8.56 us -> none  [the longest x1 4.53 us: on_device(): targets = jnp.where(valid, row_ids[0, 0][index], 0)]
  transfers between devices with their start and end apart: 3 -> 14, of which waited for: 2 -> 10; matrix products, arithmetic and copies ran while one was open for 29% -> 10% of each run, Pallas kernels for 0% -> 0%
where the time goes in v1:
time: 65.8 us; the launch traced here: 65.3 us
  waiting for transfers between devices  20.5 us (31%)
  starting transfers between devices  17.4 us (26%)
  other arithmetic  12.1 us (18%)
  between operations  8.41 us (13%)
  matrix products  4.41 us (7%)
  local copies, waits for them, and re-layouts  2.42 us (4%)
    ppermute x3, waiting for transfers between devices, on_device(): lax.ppermute(unique[s * cap:(s + 1) * cap], 'mp', perms[s - 1])  8.6 us
    ppermute x3, waiting for transfers between devices, dense_sum(): got.append(lax.ppermute(piece, 'dp', [(i, i ^ 2 * s) for i in range(8)]))  6.63 us
    ppermute x3, starting transfers between devices, on_device(): arrived.append(lax.ppermute(message, 'mp', perms[s - 1]))  5.68 us
    select_n x2, other arithmetic, on_device(): names.append(jnp.where(place < count, start + place, -1))  5.03 us
    ppermute x3, starting transfers between devices, on_device(): lax.ppermute(unique[s * cap:(s + 1) * cap], 'mp', perms[s - 1])  4.45 us
    ppermute x3, starting transfers between devices, dense_sum(): piece = lax.ppermute(total, 'dp', [(i, i ^ 2 * s) for i in range(8)])  3.62 us
    ppermute x3, starting transfers between devices, dense_sum(): got.append(lax.ppermute(piece, 'dp', [(i, i ^ 2 * s) for i in range(8)]))  3.55 us
    ppermute x3, waiting for transfers between devices, dense_sum(): piece = lax.ppermute(total, 'dp', [(i, i ^ 2 * s) for i in range(8)])  3.38 us
  transfers between devices with their start and end apart: 14, of which 10 were waited for; matrix products, arithmetic and copies ran while one was open for 10% of the time, Pallas kernels for 0%

profile of v1, /device:TPU:0, one launch (start us, length us, event | category | flops | bytes accessed | tf_op | source)
XLA Modules:
  0.0 65.3 jit_solution(1849951825541864859)
XLA Ops:
  0.6 0.0 copy-start
  0.6 0.0 copy-start.1
  0.7 1.6 %fusion.64 = (s32[]{:T(128)}, s32[]{:T(128)}, s32[]{:T(128)}, s32[]{:T(128)}, s32[]{:T(128)}, /*index=5*/s32[]{:T(128)}, s32[]{:T(128)}, s32[]{:T(128)}) fusion(s32[1,1,4]{2,1,0:T(1,128)} %param.11, s32[]{:T(128)S(6)} %axis_index.22, s32[]{:T(128)S(6)} %xor.24, s32[]{:T(128)S(6)} %xor.25, s32[]{:T(128)S(6)} %xor.26), kind=kLoop, calls=%fused_computation.128 | loop fusion | flops 88 | bytes 64 | tf_op jit(solution)/shard_map/reduce_sum | solution.py:87
  7.2 1.0 %fusion.72 = (s32[1,512]{1,0:T(1,128)S(1)}, s32[1,512]{1,0:T(1,128)S(1)}, s32[1,512]{1,0:T(1,128)S(1)}, s32[1,512]{1,0:T(1,128)S(1)}, s32[1,512]{1,0:T(1,128)S(1...) fusion(s32[8,512]{1,0:T(8,128)} %bitcast.40), kind=kLoop, calls=%fused_computation.136 | loop fusion | bytes 32768 | tf_op jit(solution)/shard_map/slice | solution.py:72
  8.3 0.0 copy-start.4
  8.3 0.0 copy-start.5
  8.3 2.1 %multiply_reduce_fusion = f32[512]{0:T(512)S(1)} fusion(bf16[512,2048]{1,0:T(8,128)(2,1)} %param.7), kind=kLoop, calls=%fused_computation | loop fusion | flops 3145216 | bytes 2099200 | tf_op jit(solution)/shard_map/reduce_sum | solution.py:76
  10.4 0.0 copy-done
  10.4 0.0 copy-done.1
  10.4 0.8 %multiply_reduce_fusion.1 = (f32[512]{0:T(512)S(1)}, f32[128,512]{1,0:T(8,128)S(1)}) fusion(bf16[128,2048]{1,0:T(8,128)(2,1)S(1)} %copy-done, bf16[512,2048]{1,0:T(8,128)(2,1)S(1)} %copy-done.1), kind=kOutput, calls=%fused_computation.48 | convolution fusion | flops 268566016 | bytes 2885632 | tf_op jit(solution)/shard_map/dot_general | solution.py:64
  11.2 0.0 copy-done.4
  11.3 0.1 fusion.14
  13.9 0.0 copy-done.5
  13.9 2.7 %fusion.57 = (s32[256]{0:T(256)S(1)}, f32[256]{0:T(256)S(1)}, f32[256]{0:T(256)S(1)}, f32[256]{0:T(256)S(1)}) fusion(s32[]{:T(128)S(6)} %select_n.118, s32[1024]{0:T(1024)S(1)} %bitcast.57, s32[]{:T(128)} %get-tuple-element.2, s32[]{:T(128)S(6)} %select_n.104, s32[]{:T(128)} %get-tuple-element.4, s32[]{:T(128)S(6)} %select_n.108, s32[]{:T(128)} %get-tuple-element.6, ...), kind=kLoop, calls=%fused_computation.110 | loop fusion | flops 2816 | bytes 8224 | tf_op jit(solution)/shard_map/jit(_where)/select_n | solution.py:89
  16.6 3.1 %collective-permute-start = (f32[768]{0:T(1024)S(1)}, f32[768]{0:T(1024)S(1)}, u32[]{:S(2)}, u32[]{:S(2)}) collective-permute-start(f32[768]{0:T(1024)S(1)} %get-tuple-element.40), channel_id=1, source_target_pairs={{0,1},{1,0},{2,3},{3,2},{4,5},{5,4},{6,7},{7,6},{8,9},{9,8},{10,11... | collective-permute-start | bytes 9224 | tf_op jit(solution)/shard_map/ppermute | solution.py:95
  19.7 2.6 %collective-permute-start.1 = (f32[768]{0:T(1024)S(1)}, f32[768]{0:T(1024)S(1)}, u32[]{:S(2)}, u32[]{:S(2)}) collective-permute-start(f32[768]{0:T(1024)S(1)} %get-tuple-element.41), channel_id=1, source_target_pairs={{0,2},{1,3},{2,0},{3,1},{4,6},{5,7},{6,4},{7,5},{8,10},{9,11},{10,... | collective-permute-start | bytes 9224 | tf_op jit(solution)/shard_map/ppermute | solution.py:95
  22.3 0.0 collective-permute-start.2
  22.3 2.5 %add_select_fusion = (s32[256]{0:T(256)S(1)}, s32[256]{0:T(256)S(1)}) fusion(s32[]{:T(128)} %get-tuple-element.7, s32[]{:T(128)} %get-tuple-element.6, s32[]{:T(128)} %get-tuple-element.5, s32[]{:T(128)} %get-tuple-element.4), kind=kLoop, calls=%fused_computation.114 | loop fusion | flops 1536 | bytes 2064 | tf_op jit(solution)/shard_map/jit(_where)/select_n | solution.py:88
  24.8 2.5 %add_select_fusion.2 = (s32[256]{0:T(256)S(1)}, s32[256]{0:T(256)S(1)}) fusion(s32[]{:T(128)} %get-tuple-element.3, s32[]{:T(128)} %get-tuple-element.9, s32[]{:T(128)} %get-tuple-element.8, s32[]{:T(128)} %get-tuple-element.2), kind=kLoop, calls=%fused_computation.116 | loop fusion | flops 1536 | bytes 2064 | tf_op jit(solution)/shard_map/jit(_where)/select_n | solution.py:88
  27.4 0.0 collective-permute-done
  27.4 0.0 collective-permute-done.1
  27.4 0.3 collective-permute-done.2
  27.7 0.6 fusion.36
  28.3 1.9 %fusion = f32[1024,256]{0,1:T(8,128)S(1)} fusion(s32[512]{0:T(512)S(1)} %bitcast.44, s32[512]{0:T(512)S(1)} %bitcast.46, s32[512]{0:T(512)S(1)} %bitcast.48, s32[512]{0:T(512)S(1)} %bitcast.50, s32[512]{0:T(512)S(1)} %bitcast.52, s32[512]{0:T(512)S(1)} %bitcast.54, s32[512]{0:T(512)S(1)} %bitcast.56, s32[512]{0:T(512)S(1)} %bitcast.42, ...), kind=kOutput, calls=%fused_computation.2 | convolution fusion | flops 281542656 | bytes 1331200 | tf_op jit(solution)/shard_map/dot_general | solution.py:109
  30.2 0.1 slice_add_fusion
  30.3 0.7 %collective-permute-start.11 = (f32[256,128]{0,1:T(8,128)S(1)}, f32[256,128]{0,1:T(8,128)S(1)}, u32[]{:S(2)}, u32[]{:S(2)}) collective-permute-start(f32[256,128]{0,1:T(8,128)S(1)} %get-tuple-element.15), channel_id=1, source_target_pairs={{0,1},{1,0},{2,3},{3,2},{4,5},{5,4},{6,7},{7,6},{8,9},{9,8},{10,11... | collective-permute-start | bytes 393224 | tf_op jit(solution)/shard_map/ppermute | solution.py:119
  31.0 3.5 %collective-permute-start.12 = (f32[256,128]{0,1:T(8,128)S(1)}, f32[256,128]{0,1:T(8,128)S(1)}, u32[]{:S(2)}, u32[]{:S(2)}) collective-permute-start(f32[256,128]{0,1:T(8,128)S(1)} %get-tuple-element.14), channel_id=1, source_target_pairs={{0,2},{1,3},{2,0},{3,1},{4,6},{5,7},{6,4},{7,5},{8,10},{9,11},{10,... | collective-permute-start | bytes 393224 | tf_op jit(solution)/shard_map/ppermute | solution.py:119
  34.5 0.3 collective-permute-start.13
  34.8 0.1 collective-permute-start.3
  34.9 0.3 fusion.10
  35.2 0.1 broadcast_in_dim.66
  35.3 1.6 %collective-permute-done.11 = f32[256,128]{0,1:T(8,128)S(1)} collective-permute-done((f32[256,128]{0,1:T(8,128)S(1)}, f32[256,128]{0,1:T(8,128)S(1)}, u32[]{:S(2)}, u32[]{:S(2)}) %collective-permute-start.11) | collective-permute-done | bytes 131104 | tf_op jit(solution)/shard_map/ppermute | solution.py:119
  37.0 7.0 %collective-permute-done.12 = f32[256,128]{0,1:T(8,128)S(1)} collective-permute-done((f32[256,128]{0,1:T(8,128)S(1)}, f32[256,128]{0,1:T(8,128)S(1)}, u32[]{:S(2)}, u32[]{:S(2)}) %collective-permute-start.12) | collective-permute-done | bytes 131104 | tf_op jit(solution)/shard_map/ppermute | solution.py:119
  44.0 0.0 collective-permute-done.13
  44.0 0.3 fusion.11
  44.3 0.3 fusion.12
  44.6 0.0 collective-permute-done.3
  44.6 0.1 dynamic-slice_add_fusion
  44.7 1.6 %collective-permute-start.4 = (f32[16,2048]{1,0:T(8,128)S(1)}, f32[16,2048]{1,0:T(8,128)S(1)}, u32[]{:S(2)}, u32[]{:S(2)}) collective-permute-start(f32[16,2048]{1,0:T(8,128)S(1)} %get-tuple-element.17), channel_id=1, source_target_pairs={{0,8},{4,12},{8,0},{12,4},{16,24},{20,28},{24,16},{28,20},{1,9},{5... | collective-permute-start | bytes 393224 | tf_op jit(solution)/shard_map/ppermute | solution.py:45
  46.2 1.5 %collective-permute-start.5 = (f32[16,2048]{1,0:T(8,128)S(1)}, f32[16,2048]{1,0:T(8,128)S(1)}, u32[]{:S(2)}, u32[]{:S(2)}) collective-permute-start(f32[16,2048]{1,0:T(8,128)S(1)} %get-tuple-element.19), channel_id=1, source_target_pairs={{0,16},{4,20},{8,24},{12,28},{16,0},{20,4},{24,8},{28,12},{1,17},{... | collective-permute-start | bytes 393224 | tf_op jit(solution)/shard_map/ppermute | solution.py:45
  47.8 0.5 collective-permute-start.6
  48.2 0.3 fusion.13
  48.5 1.2 %collective-permute-done.4 = f32[16,2048]{1,0:T(8,128)S(1)} collective-permute-done((f32[16,2048]{1,0:T(8,128)S(1)}, f32[16,2048]{1,0:T(8,128)S(1)}, u32[]{:S(2)}, u32[]{:S(2)}) %collective-permute-start.4) | collective-permute-done | bytes 131104 | tf_op jit(solution)/shard_map/ppermute | solution.py:45
  49.7 1.5 %collective-permute-done.5 = f32[16,2048]{1,0:T(8,128)S(1)} collective-permute-done((f32[16,2048]{1,0:T(8,128)S(1)}, f32[16,2048]{1,0:T(8,128)S(1)}, u32[]{:S(2)}, u32[]{:S(2)}) %collective-permute-start.5) | collective-permute-done | bytes 131104 | tf_op jit(solution)/shard_map/ppermute | solution.py:45
  51.2 3.9 %collective-permute-done.6 = f32[16,2048]{1,0:T(8,128)S(1)} collective-permute-done((f32[16,2048]{1,0:T(8,128)S(1)}, f32[16,2048]{1,0:T(8,128)S(1)}, u32[]{:S(2)}, u32[]{:S(2)}) %collective-permute-start.6) | collective-permute-done | bytes 131104 | tf_op jit(solution)/shard_map/ppermute | solution.py:45
  55.2 0.6 collective-permute-start.7
  55.8 0.5 collective-permute-start.8
  56.3 2.5 %collective-permute-start.9 = (f32[16,2048]{1,0:T(8,128)S(1)}, f32[16,2048]{1,0:T(8,128)S(1)}, u32[]{:S(2)}, u32[]{:S(2)}) collective-permute-start(f32[16,2048]{1,0:T(8,128)S(1)} %get-tuple-element.11), channel_id=1, source_target_pairs={{0,24},{4,28},{8,16},{12,20},{16,8},{20,12},{24,0},{28,4},{1,25},{... | collective-permute-start | bytes 393224 | tf_op jit(solution)/shard_map/ppermute | solution.py:50
  58.9 1.4 %collective-permute-done.7 = f32[16,2048]{1,0:T(8,128)S(1)} collective-permute-done((f32[16,2048]{1,0:T(8,128)S(1)}, f32[16,2048]{1,0:T(8,128)S(1)}, u32[]{:S(2)}, u32[]{:S(2)}) %collective-permute-start.7) | collective-permute-done | bytes 131104 | tf_op jit(solution)/shard_map/ppermute | solution.py:50
  60.3 0.6 collective-permute-done.8
  60.9 1.4 %collective-permute-done.9 = f32[16,2048]{1,0:T(8,128)S(1)} collective-permute-done((f32[16,2048]{1,0:T(8,128)S(1)}, f32[16,2048]{1,0:T(8,128)S(1)}, u32[]{:S(2)}, u32[]{:S(2)}) %collective-permute-start.9) | collective-permute-done | bytes 131104 | tf_op jit(solution)/shard_map/ppermute | solution.py:50
  62.3 0.1 collective-permute-start.10
  62.5 0.0 copy-start.2
  62.5 0.1 broadcast_in_dim.62
  62.6 1.7 %collective-permute-done.10 = f32[64,2048]{1,0:T(8,128)S(1)} collective-permute-done((f32[64,2048]{1,0:T(8,128)S(1)}, f32[64,2048]{1,0:T(8,128)S(1)}, u32[]{:S(2)}, u32[]{:S(2)}) %collective-permute-start.10) | collective-permute-done | bytes 524320 | tf_op jit(solution)/shard_map/ppermute | solution.py:52
  64.3 0.0 copy-done.2
  64.3 0.0 copy-start.3
  64.3 1.0 %copy-done.3 = f32[128,2048]{1,0:T(8,128)} copy-done((f32[128,2048]{1,0:T(8,128)}, f32[128,2048]{1,0:T(8,128)S(1)}, u32[]{:S(2)}) %copy-start.3) | copy-done | bytes 1048600
  (25 shorter events, 0.6 us)
Async XLA Ops:
  0.6 9.8 %copy-start = (bf16[128,2048]{1,0:T(8,128)(2,1)S(1)}, bf16[128,2048]{1,0:T(8,128)(2,1)}, u32[]{:S(2)}) copy-start(bf16[128,2048]{1,0:T(8,128)(2,1)} %param.8) | copy-start | bytes 1572868
  0.6 9.7 %copy-start.1 = (bf16[512,2048]{1,0:T(8,128)(2,1)S(1)}, bf16[512,2048]{1,0:T(8,128)(2,1)}, u32[]{:S(2)}) copy-start(bf16[512,2048]{1,0:T(8,128)(2,1)} %param.7) | copy-start | bytes 6291460
  8.3 3.0 %copy-start.4 = (bf16[512,128]{1,0:T(8,128)(2,1)S(1)}, bf16[512,128]{1,0:T(8,128)(2,1)}, u32[]{:S(2)}) copy-start(bf16[512,128]{1,0:T(8,128)(2,1)} %param.6) | copy-start | bytes 393220
  8.3 5.6 %copy-start.5 = (s32[1,1,1024]{2,1,0:T(1,128)S(1)}, s32[1,1,1024]{2,1,0:T(1,128)}, u32[]{:S(2)}) copy-start(s32[1,1,1024]{2,1,0:T(1,128)} %param.10) | copy-start | bytes 12292
  16.6 10.8 %collective-permute-start = (f32[768]{0:T(1024)S(1)}, f32[768]{0:T(1024)S(1)}, u32[]{:S(2)}, u32[]{:S(2)}) collective-permute-start(f32[768]{0:T(1024)S(1)} %get-tuple-element.40), channel_id=1, source_target_pairs={{0,1},{1,0},{2,3},{3,2},{4,5},{5,4},{6,7},{7,6},{8,9},{9,8},{10,11... | collective-permute-start | bytes 9224 | tf_op jit(solution)/shard_map/ppermute | solution.py:95
  19.7 7.7 %collective-permute-start.1 = (f32[768]{0:T(1024)S(1)}, f32[768]{0:T(1024)S(1)}, u32[]{:S(2)}, u32[]{:S(2)}) collective-permute-start(f32[768]{0:T(1024)S(1)} %get-tuple-element.41), channel_id=1, source_target_pairs={{0,2},{1,3},{2,0},{3,1},{4,6},{5,7},{6,4},{7,5},{8,10},{9,11},{10,... | collective-permute-start | bytes 9224 | tf_op jit(solution)/shard_map/ppermute | solution.py:95
  22.3 5.4 %collective-permute-start.2 = (f32[768]{0:T(1024)S(1)}, f32[768]{0:T(1024)S(1)}, u32[]{:S(2)}, u32[]{:S(2)}) collective-permute-start(f32[768]{0:T(1024)S(1)} %get-tuple-element.42), channel_id=1, source_target_pairs={{0,3},{1,2},{2,1},{3,0},{4,7},{5,6},{6,5},{7,4},{8,11},{9,10},{10,... | collective-permute-start | bytes 9224 | tf_op jit(solution)/shard_map/ppermute | solution.py:95
  30.3 6.6 %collective-permute-start.11 = (f32[256,128]{0,1:T(8,128)S(1)}, f32[256,128]{0,1:T(8,128)S(1)}, u32[]{:S(2)}, u32[]{:S(2)}) collective-permute-start(f32[256,128]{0,1:T(8,128)S(1)} %get-tuple-element.15), channel_id=1, source_target_pairs={{0,1},{1,0},{2,3},{3,2},{4,5},{5,4},{6,7},{7,6},{8,9},{9,8},{10,11... | collective-permute-start | bytes 393224 | tf_op jit(solution)/shard_map/ppermute | solution.py:119
  31.0 12.9 %collective-permute-start.12 = (f32[256,128]{0,1:T(8,128)S(1)}, f32[256,128]{0,1:T(8,128)S(1)}, u32[]{:S(2)}, u32[]{:S(2)}) collective-permute-start(f32[256,128]{0,1:T(8,128)S(1)} %get-tuple-element.14), channel_id=1, source_target_pairs={{0,2},{1,3},{2,0},{3,1},{4,6},{5,7},{6,4},{7,5},{8,10},{9,11},{10,... | collective-permute-start | bytes 393224 | tf_op jit(solution)/shard_map/ppermute | solution.py:119
  34.5 9.4 %collective-permute-start.13 = (f32[256,128]{0,1:T(8,128)S(1)}, f32[256,128]{0,1:T(8,128)S(1)}, u32[]{:S(2)}, u32[]{:S(2)}) collective-permute-start(f32[256,128]{0,1:T(8,128)S(1)} %get-tuple-element.12), channel_id=1, source_target_pairs={{0,3},{1,2},{2,1},{3,0},{4,7},{5,6},{6,5},{7,4},{8,11},{9,10},{10,... | collective-permute-start | bytes 393224 | tf_op jit(solution)/shard_map/ppermute | solution.py:119
  34.8 9.7 %collective-permute-start.3 = (f32[64,2048]{1,0:T(8,128)S(1)}, f32[64,2048]{1,0:T(8,128)S(1)}, u32[]{:S(2)}, u32[]{:S(2)}) collective-permute-start(f32[64,2048]{1,0:T(8,128)S(1)} %constant_dynamic-slice_fusion.3), channel_id=1, source_target_pairs={{0,4},{4,0},{8,12},{12,8},{16,20},{20,16},{24,28},{28,24},{1,5},{5... | collective-permute-start | bytes 1572872 | tf_op jit(solution)/shard_map/ppermute | solution.py:40
  44.7 5.0 %collective-permute-start.4 = (f32[16,2048]{1,0:T(8,128)S(1)}, f32[16,2048]{1,0:T(8,128)S(1)}, u32[]{:S(2)}, u32[]{:S(2)}) collective-permute-start(f32[16,2048]{1,0:T(8,128)S(1)} %get-tuple-element.17), channel_id=1, source_target_pairs={{0,8},{4,12},{8,0},{12,4},{16,24},{20,28},{24,16},{28,20},{1,9},{5... | collective-permute-start | bytes 393224 | tf_op jit(solution)/shard_map/ppermute | solution.py:45
  46.2 5.0 %collective-permute-start.5 = (f32[16,2048]{1,0:T(8,128)S(1)}, f32[16,2048]{1,0:T(8,128)S(1)}, u32[]{:S(2)}, u32[]{:S(2)}) collective-permute-start(f32[16,2048]{1,0:T(8,128)S(1)} %get-tuple-element.19), channel_id=1, source_target_pairs={{0,16},{4,20},{8,24},{12,28},{16,0},{20,4},{24,8},{28,12},{1,17},{... | collective-permute-start | bytes 393224 | tf_op jit(solution)/shard_map/ppermute | solution.py:45
  47.8 7.4 %collective-permute-start.6 = (f32[16,2048]{1,0:T(8,128)S(1)}, f32[16,2048]{1,0:T(8,128)S(1)}, u32[]{:S(2)}, u32[]{:S(2)}) collective-permute-start(f32[16,2048]{1,0:T(8,128)S(1)} %get-tuple-element.18), channel_id=1, source_target_pairs={{0,24},{4,28},{8,16},{12,20},{16,8},{20,12},{24,0},{28,4},{1,25},{... | collective-permute-start | bytes 393224 | tf_op jit(solution)/shard_map/ppermute | solution.py:45
  55.2 5.0 %collective-permute-start.7 = (f32[16,2048]{1,0:T(8,128)S(1)}, f32[16,2048]{1,0:T(8,128)S(1)}, u32[]{:S(2)}, u32[]{:S(2)}) collective-permute-start(f32[16,2048]{1,0:T(8,128)S(1)} %get-tuple-element.11), channel_id=1, source_target_pairs={{0,8},{4,12},{8,0},{12,4},{16,24},{20,28},{24,16},{28,20},{1,9},{5... | collective-permute-start | bytes 393224 | tf_op jit(solution)/shard_map/ppermute | solution.py:50
  55.8 5.0 %collective-permute-start.8 = (f32[16,2048]{1,0:T(8,128)S(1)}, f32[16,2048]{1,0:T(8,128)S(1)}, u32[]{:S(2)}, u32[]{:S(2)}) collective-permute-start(f32[16,2048]{1,0:T(8,128)S(1)} %get-tuple-element.11), channel_id=1, source_target_pairs={{0,16},{4,20},{8,24},{12,28},{16,0},{20,4},{24,8},{28,12},{1,17},{... | collective-permute-start | bytes 393224 | tf_op jit(solution)/shard_map/ppermute | solution.py:50
  56.3 5.9 %collective-permute-start.9 = (f32[16,2048]{1,0:T(8,128)S(1)}, f32[16,2048]{1,0:T(8,128)S(1)}, u32[]{:S(2)}, u32[]{:S(2)}) collective-permute-start(f32[16,2048]{1,0:T(8,128)S(1)} %get-tuple-element.11), channel_id=1, source_target_pairs={{0,24},{4,28},{8,16},{12,20},{16,8},{20,12},{24,0},{28,4},{1,25},{... | collective-permute-start | bytes 393224 | tf_op jit(solution)/shard_map/ppermute | solution.py:50
  62.3 2.0 %collective-permute-start.10 = (f32[64,2048]{1,0:T(8,128)S(1)}, f32[64,2048]{1,0:T(8,128)S(1)}, u32[]{:S(2)}, u32[]{:S(2)}) collective-permute-start(f32[64,2048]{1,0:T(8,128)S(1)} %constant_dynamic-update-slice_fusion.2), channel_id=1, source_target_pairs={{0,4},{4,0},{8,12},{12,8},{16,20},{20,16},{24,28},{28,24},{1,5},{5... | collective-permute-start | bytes 1572872 | tf_op jit(solution)/shard_map/ppermute | solution.py:52
  62.5 1.9 %copy-start.2 = (f32[1,4,512,128]{3,2,1,0:T(8,128)}, f32[1,4,512,128]{3,2,1,0:T(8,128)S(1)}, u32[]{:S(2)}) copy-start(f32[1,4,512,128]{3,2,1,0:T(8,128)S(1)} %fusion.18) | copy-start | bytes 3145732
  64.3 1.0 %copy-start.3 = (f32[128,2048]{1,0:T(8,128)}, f32[128,2048]{1,0:T(8,128)S(1)}, u32[]{:S(2)}) copy-start(f32[128,2048]{1,0:T(8,128)S(1)} %constant_dynamic-update-slice_fusion) | copy-start | bytes 3145732

commit v2 on v0

v2 whole, which is shorter than its diff:
```python
import functools

import jax
import jax.numpy as jnp
from jax import lax
from jax.experimental import pallas as pl
from jax.experimental.pallas import tpu as pltpu
from jax.sharding import PartitionSpec as P

ROWS_DEV = 512
CLIP_NORM = 8.0
EPSILON = 1e-06

VMEM = pl.BlockSpec(memory_space=pltpu.VMEM)
SMEM = pl.BlockSpec(memory_space=pltpu.SMEM)
HBM = pl.BlockSpec(memory_space=pltpu.HBM)
ANY = pl.BlockSpec(memory_space=pl.ANY)
CHUNK = 256
F32, BF16, I32 = jnp.float32, jnp.bfloat16, jnp.int32


def pairings(n):
    if n & (n - 1) == 0:
        return [[(i, i ^ s) for i in range(n)] for s in range(1, n)]
    return [[(i, (i + s) % n) for i in range(n)] for s in range(1, n)]


def peer_to(me, s, n):
    return me ^ s if n & (n - 1) == 0 else lax.rem(me + s, n)


def peer_from(me, s, n):
    return me ^ s if n & (n - 1) == 0 else lax.rem(me + n - s, n)


def call(kernel, outs, flops, *args, specs=None, out_specs=None, scratch=(), aliases=None):
    size = sum(a.size * a.dtype.itemsize for a in args)
    return list(pl.pallas_call(
        kernel,
        out_shape=[jax.ShapeDtypeStruct(shape, dtype) for shape, dtype in outs],
        in_specs=specs or [VMEM] * len(args),
        out_specs=out_specs or [VMEM] * len(outs),
        scratch_shapes=list(scratch),
        input_output_aliases=aliases or {},
        compiler_params=pltpu.CompilerParams(vmem_limit_bytes=16 * 2**20),
        cost_estimate=pl.CostEstimate(flops=flops, bytes_accessed=size, transcendentals=0),
    )(*args))


def window(counts_ref, me, s, owners):
    owner = peer_to(me, s, owners)
    start, count = jnp.int32(0), jnp.int32(0)
    for o in range(owners):
        here = counts_ref[0, o]
        start = start + jnp.where(o < owner, here, 0)
        count = count + jnp.where(o == owner, here, 0)
    return start, count


def first_kernel(owners, counts_hbm, delta_hbm, w_hbm, pooled_hbm, slots_hbm, ids_hbm, *refs):
    xgrad_ref, delta_ref, pooled_ref, slots_ref, *rest = refs
    message_refs, (w_ref, ids_ref, counts_ref, sems) = rest[:owners], rest[owners:]
    examples, emb = pooled_ref.shape
    hid = delta_ref.shape[1]
    looks = slots_ref.shape[0]
    width = ids_ref.shape[1]
    cap = width // owners
    blocks = list(range(0, examples, CHUNK))
    pairs = [(w_hbm, w_ref)]
    pairs += [(delta_hbm.at[pl.ds(r, CHUNK)], delta_ref.at[pl.ds(r, CHUNK)]) for r in blocks]
    pairs += [(counts_hbm, counts_ref), (slots_hbm, slots_ref), (ids_hbm, ids_ref), (pooled_hbm, pooled_ref)]
    copies = [pltpu.make_async_copy(a, b, sems.at[i]) for i, (a, b) in enumerate(pairs)]
    for copy in copies:
        copy.start()
    me = lax.axis_index("mp")
    n = len(blocks)
    copies[0].wait()
    norms = []
    for i, r in enumerate(blocks):
        copies[1 + i].wait()
        xgrad = lax.dot_general(
            w_ref[...], delta_ref[r:r + CHUNK, :], (((1,), (1,)), ((), ())),
            preferred_element_type=F32,
        )
        xgrad_ref[:, r:r + CHUNK] = xgrad
        sums = []
        for q in range(r, r + CHUNK, 128):
            total = jnp.zeros((128, 128), F32)
            for c in range(0, hid, 128):
                piece = delta_ref[q:q + 128, c:c + 128].astype(F32)
                total = total + piece * piece
            sums.append(jnp.sum(total.T, axis=0, keepdims=True))
        norms.append((jnp.sum(xgrad * xgrad, axis=0, keepdims=True), jnp.concatenate(sums, axis=1)))
    for copy in copies[1 + n:]:
        copy.wait()
    slots = slots_ref[...]
    same = jnp.full(slots.shape, 1.0, F32)
    for shift in range(1, looks):
        same = same + jnp.where(slots == pltpu.roll(slots, shift, 0), 1.0, 0.0)
    repeats = jnp.sum(same, axis=0, keepdims=True)
    for i, r in enumerate(blocks):
        xgrad_sq, delta_sq = norms[i]
        sums = []
        for q in range(r, r + CHUNK, 128):
            piece = pooled_ref[q:q + 128, :].astype(F32)
            sums.append(jnp.sum((piece * piece).T, axis=0, keepdims=True))
        partial = delta_sq * jnp.concatenate(sums, axis=1) + repeats[:, r:r + CHUNK] * xgrad_sq
        for message in message_refs:
            message[:, r:r + CHUNK] = partial
    ids = jnp.broadcast_to(ids_ref[...], (8, width))
    place = lax.broadcasted_iota(I32, (1, cap), 1)
    for s in range(owners):
        start, count = window(counts_ref, me, s, owners)
        mine = pltpu.roll(ids, lax.rem(width - start, width), 1)[0:1, :cap]
        message_refs[s][:, examples:] = jnp.where(place < count, mine, -1).astype(F32)


def named_kernel(owners, counts_ref, slots_ref, named_ref):
    width = named_ref.shape[0]
    looks, examples = slots_ref.shape
    cap = width // owners
    me = lax.axis_index("mp")
    for s in range(owners):
        start, count = window(counts_ref, me, s, owners)
        for r in range(0, cap, 64):
            place = lax.broadcasted_iota(I32, (64, 128), 0) + r
            name = jnp.where(place < count, place + start, -1)
            for c in range(0, examples, 128):
                total = jnp.zeros((64, 128), F32)
                for l in range(looks):
                    total = total + jnp.where(slots_ref[l:l + 1, c:c + 128] == name, 1.0, 0.0)
                named_ref[s * cap + r:s * cap + r + 64, c:c + 128] = total.astype(BF16)


def clip_kernel(owners, *refs):
    messages = refs[:owners]
    pooled_ref, delta_ref, _, clip_ref, scaled_ref, theirs_ref, wide_ref = refs[owners:]
    examples, emb = pooled_ref.shape
    half = theirs_ref.shape[0]
    core = lax.rem(lax.axis_index("dp"), 2)
    norm_sq = messages[0][:, :examples]
    for message in messages[1:]:
        norm_sq = norm_sq + message[:, :examples]
    clip = jnp.minimum(1.0, CLIP_NORM / jnp.sqrt(norm_sq + EPSILON))
    clip_ref[...] = clip
    wide_ref[...] = pooled_ref[...].astype(F32).T * clip
    other = wide_ref[pl.ds((1 - core) * half, half), :].astype(BF16)
    theirs_ref[...] = jnp.dot(other, delta_ref[...], preferred_element_type=F32)
    scaled_ref[...] = wide_ref[pl.ds(core * half, half), :].astype(BF16)


def mine_kernel(scaled_ref, delta_ref, mine_ref):
    mine_ref[...] = jnp.dot(scaled_ref[...], delta_ref[...], preferred_element_type=F32)


def unique_kernel(owners, named_ref, xgrad_ref, clip_ref, gate_ref, *out_refs):
    del gate_ref
    emb = xgrad_ref.shape[0]
    cap = named_ref.shape[0] // owners
    wide = xgrad_ref[...] * clip_ref[...]
    hi = wide.astype(BF16)
    lo = (wide - hi.astype(F32)).astype(BF16)
    terms = jnp.concatenate([hi, lo], axis=0)
    for s in range(owners):
        both = lax.dot_general(
            named_ref[s * cap:(s + 1) * cap, :], terms, (((1,), (1,)), ((), ())),
            preferred_element_type=F32,
        )
        out_refs[s][...] = both[:, :emb] + both[:, emb:]


def place_kernel(owners, *refs):
    pieces, messages = refs[:owners], refs[owners:2 * owners]
    own_ref, table_ref, dense_ref, rows_ref, sems = refs[2 * owners:]
    cap, emb = pieces[0].shape
    half = own_ref.shape[0]
    me, core = lax.axis_index("mp"), lax.rem(lax.axis_index("dp"), 2)
    copy = pltpu.make_async_copy(own_ref, dense_ref.at[pl.ds(core * half, half)], sems.at[owners])
    copy.start()
    copies = [copy]
    row = lax.broadcasted_iota(I32, (ROWS_DEV, cap), 0).astype(F32)
    for s in range(owners):
        ids = messages[s][:, messages[s].shape[1] - cap:]
        hot = jnp.where(row == ids, 1.0, 0.0).astype(BF16)
        wide = pieces[s][...]
        hi = wide.astype(BF16)
        lo = (wide - hi.astype(F32)).astype(BF16)
        both = jnp.dot(hot, jnp.concatenate([hi, lo], axis=1), preferred_element_type=F32)
        rows_ref[s] = both[:, :emb] + both[:, emb:]
        copy = pltpu.make_async_copy(
            rows_ref.at[s], table_ref.at[peer_from(me, s, owners)], sems.at[s]
        )
        copy.start()
        copies.append(copy)
    for copy in copies:
        copy.wait()


def finish_kernel(_, other_ref, dense_ref, sem):
    half = other_ref.shape[0]
    core = lax.rem(lax.axis_index("dp"), 2)
    copy = pltpu.make_async_copy(other_ref, dense_ref.at[pl.ds((1 - core) * half, half)], sem)
    copy.start()
    copy.wait()


def on_device(pooled, delta, w_first, lookup_slot, row_ids, send_counts):
    owners, n_dp = lax.axis_size("mp"), lax.axis_size("dp")
    examples, emb = pooled.shape
    hid = delta.shape[1]
    width = row_ids.shape[-1]
    cap = width // owners
    slots = lookup_slot[:, 0, :].T
    looks = slots.shape[0]
    counts, ids = send_counts[0], row_ids[0]
    half, part = emb // 2, emb // 8

    xgrad, delta, pooled, slots, *messages = call(
        functools.partial(first_kernel, owners),
        [((emb, examples), F32), (delta.shape, BF16), (pooled.shape, BF16), (slots.shape, I32)]
        + [((1, examples + cap), F32)] * owners,
        2 * emb * examples * hid,
        *[pltpu.with_memory_space_constraint(a, pltpu.HBM) for a in (counts, delta, w_first, pooled, slots, ids)],
        specs=[HBM] * 6,
        scratch=[
            pltpu.VMEM(w_first.shape, BF16), pltpu.VMEM(ids.shape, I32),
            pltpu.SMEM(counts.shape, I32), pltpu.SemaphoreType.DMA((5 + examples // CHUNK,)),
        ],
    )
    steps = pairings(owners)
    for s in range(1, owners):
        messages[s] = lax.ppermute(messages[s], "mp", steps[s - 1])
    (named,) = call(
        functools.partial(named_kernel, owners), [((width, examples), BF16)],
        8 * width * examples * looks, counts, slots, specs=[SMEM, VMEM],
    )
    clip, scaled, theirs = call(
        functools.partial(clip_kernel, owners),
        [((1, examples), F32), ((half, examples), BF16), ((half, hid), F32)],
        2 * half * examples * hid,
        *messages, pooled, delta, named,
        specs=[VMEM] * (owners + 2) + [ANY],
        scratch=[pltpu.VMEM((emb, examples), F32)],
    )
    me = lax.axis_index("dp")
    core, chip = me & 1, me >> 1
    swap = [(i, i ^ 1) for i in range(n_dp)]
    came = lax.ppermute(theirs, "dp", swap)
    (mine,) = call(mine_kernel, [((half, hid), F32)], 2 * half * examples * hid, scaled, delta)
    mine = mine + came

    def chips(piece, s):
        return lax.ppermute(piece, "dp", [(i, i ^ (2 * s)) for i in range(n_dp)])

    unique = call(
        functools.partial(unique_kernel, owners), [((cap, emb), F32)] * owners,
        4 * width * examples * emb, named, xgrad, clip, mine, specs=[VMEM] * 3 + [ANY],
    )
    if n_dp == 8:
        got = {}
        for s in (3, 1, 2):
            got[s] = chips(lax.dynamic_slice_in_dim(mine, (chip ^ s) * part, part, 0), s)
        got, _ = lax.optimization_barrier((got, unique[0]))
        total = lax.dynamic_slice_in_dim(mine, chip * part, part, 0) + got[1] + got[2] + got[3]
        own = lax.dynamic_update_slice_in_dim(jnp.zeros((half, hid), F32), total, chip * part, 0)
        for s in (3, 1, 2):
            own = lax.dynamic_update_slice_in_dim(own, chips(total, s), (chip ^ s) * part, 0)
    else:
        own = lax.psum(mine, "dp", axis_index_groups=[list(range(c, n_dp, 2)) for c in (0, 1)])
    for s in range(1, owners):
        unique[s] = lax.ppermute(unique[s], "mp", steps[s - 1])
    own, *unique = lax.optimization_barrier((own, *unique))
    other = lax.ppermute(own, "dp", swap)
    table_grad, dense_grad = call(
        functools.partial(place_kernel, owners),
        [((owners, ROWS_DEV, emb), F32), ((emb, hid), F32)],
        4 * owners * ROWS_DEV * cap * emb, *unique, *messages, own, out_specs=[HBM, HBM],
        scratch=[pltpu.VMEM((owners, ROWS_DEV, emb), F32), pltpu.SemaphoreType.DMA((owners + 1,))],
    )
    (dense_grad,) = call(
        finish_kernel, [((emb, hid), F32)], 0, dense_grad, other, specs=[HBM, VMEM],
        out_specs=[HBM], scratch=[pltpu.SemaphoreType.DMA(())], aliases={0: 0},
    )
    return (dense_grad, table_grad[None])


def solution(mesh):
    placed = (
        P("dp", "mp"),
        P("dp", None),
        P("mp", None),
        P("dp", "mp", None),
        P("dp", "mp", None),
        P("dp", "mp", None),
    )
    return jax.shard_map(
        on_device,
        mesh=mesh,
        in_specs=placed,
        out_specs=(P("mp", None), P("dp", None, "mp", None)),
        check_vma=False,
    )
```

time: 140 us -> 46 us (0.33)
  waiting for transfers between devices: 53.3 us -> 16.8 us
  other arithmetic: 35.4 us -> 1.13 us
  between operations: 14.2 us -> 0.74 us
  blocking collectives: 12.2 us -> 0 us
  local copies, waits for them, and re-layouts: 12 us -> 0.11 us
  Pallas kernels: 0 us -> 9.89 us
  starting transfers between devices: 9.83 us -> 17.2 us
  matrix products: 2.27 us -> 0 us
    psum x1 -> x0, waiting for transfers between devices: 42.9 us -> none  [on_device(): dense_grad = lax.psum(local_dense, 'dp')]
    scatter-add x1 -> x0, other arithmetic: 22.6 us -> none  [on_device(): jax.ops.segment_sum(jnp.repeat(contrib, per_look, axis=0), slots.reshape(...]
    ppermute x0 -> x14, starting transfers between devices: none -> 17.2 us  [the longest x6 7.11 us: chips(): return lax.ppermute(piece, 'dp', [(i, i ^ 2 * s) for i in range(n_dp)])]
    ppermute x0 -> x14, waiting for transfers between devices: none -> 16.8 us  [the longest x6 10 us: chips(): return lax.ppermute(piece, 'dp', [(i, i ^ 2 * s) for i in range(n_dp)])]
    psum x1 -> x0, blocking collectives: 12.2 us -> none  [on_device(): total_sq, total_embed = lax.psum((local_sq, embed_sq), 'mp')]
    all_to_all x2 -> x0, waiting for transfers between devices: 10.4 us -> none  [the longest x1 10.4 us: on_device(): lax.all_to_all(packed, 'mp', split_axis=0, concat_axis=0, tiled=True)]
    pallas_call x0 -> x7, Pallas kernels: none -> 9.89 us  [call(): pl.pallas_call(kernel, out_shape=[jax.ShapeDtypeStruct(shape, dtype) for...]
    all_to_all x2 -> x0, starting transfers between devices: 9.79 us -> none  [the longest x1 6.32 us: on_device(): lax.all_to_all(targets, 'mp', split_axis=0, concat_axis=0, tiled=True)]
  transfers between devices with their start and end apart: 3 -> 14, of which waited for: 2 -> 8; matrix products, arithmetic and copies ran while one was open for 29% -> 0% of each run, Pallas kernels for 0% -> 10%
where the time goes in v2:
time: 46 us; the launch traced here: 45.8 us
  starting transfers between devices  17.2 us (37%)
  waiting for transfers between devices  16.8 us (37%)
  Pallas kernels  9.89 us (22%)
  other arithmetic  1.13 us (2%)
  between operations  0.74 us (2%)
    ppermute x6, waiting for transfers between devices, chips(): return lax.ppermute(piece, 'dp', [(i, i ^ 2 * s) for i in range(n_dp)])  10 us
    pallas_call x7, Pallas kernels, call(): pl.pallas_call(kernel, out_shape=[jax.ShapeDtypeStruct(shape, dtype) for...  9.89 us
    ppermute x6, starting transfers between devices, chips(): return lax.ppermute(piece, 'dp', [(i, i ^ 2 * s) for i in range(n_dp)])  7.11 us
    ppermute x3, starting transfers between devices, on_device(): messages[s] = lax.ppermute(messages[s], 'mp', steps[s - 1])  5.68 us
    ppermute x3, starting transfers between devices, on_device(): unique[s] = lax.ppermute(unique[s], 'mp', steps[s - 1])  4.39 us
    ppermute x3, waiting for transfers between devices, on_device(): messages[s] = lax.ppermute(messages[s], 'mp', steps[s - 1])  3.13 us
    ppermute x1, waiting for transfers between devices, on_device(): came = lax.ppermute(theirs, 'dp', swap)  1.77 us
    ppermute x3, waiting for transfers between devices, on_device(): unique[s] = lax.ppermute(unique[s], 'mp', steps[s - 1])  1.26 us
  transfers between devices with their start and end apart: 14, of which 8 were waited for; matrix products, arithmetic and copies ran while one was open for 0% of the time, Pallas kernels for 10%

profile of v2, /device:TPU:0, one launch (start us, length us, event | category | flops | bytes accessed | tf_op | source)
XLA Modules:
  0.0 45.8 jit_solution(17874433727614702193)
XLA Ops:
  0.6 0.0 copy-start
  0.6 3.2 %shard_map.77 = (f32[128,512]{1,0:T(8,128)S(1)}, bf16[512,2048]{1,0:T(8,128)(2,1)S(1)}, bf16[512,128]{1,0:T(8,128)(2,1)S(1)}, s32[8,512]{1,0:T(8,128)S(1)}, f32[...) custom-call(s32[1,4]{1,0:T(1,128)} %bitcast.6, ...), custom_call_target="tpu_custom_call" | custom-call | flops 268435456 | bytes 2773008 | tf_op jit(solution)/shard_map/pallas_call | solution.py:38
  3.9 3.1 %collective-permute-start = (f32[1,768]{1,0:T(1,128)S(1)}, f32[1,768]{1,0:T(1,128)S(1)}, u32[]{:S(2)}, u32[]{:S(2)}) collective-permute-start(f32[1,768]{1,0:T(1,128)S(1)} %get-tuple-element.28), channel_id=1, source_target_pairs={{0,1},{1,0},{2,3},{3,2},{4,5},{5,4},{6,7},{7,6},{8,9},{9,8},{10,11... | collective-permute-start | bytes 9224 | tf_op jit(solution)/shard_map/ppermute | solution.py:232
  7.0 2.6 %collective-permute-start.1 = (f32[1,768]{1,0:T(1,128)S(1)}, f32[1,768]{1,0:T(1,128)S(1)}, u32[]{:S(2)}, u32[]{:S(2)}) collective-permute-start(f32[1,768]{1,0:T(1,128)S(1)} %get-tuple-element.29), channel_id=1, source_target_pairs={{0,2},{1,3},{2,0},{3,1},{4,6},{5,7},{6,4},{7,5},{8,10},{9,11},{10,... | collective-permute-start | bytes 9224 | tf_op jit(solution)/shard_map/ppermute | solution.py:232
  9.6 0.0 collective-permute-start.2
  9.6 0.0 copy-done
  9.6 2.2 %shard_map.78.refs_6_.named_ref = bf16[1024,512]{1,0:T(8,128)(2,1)S(1)} custom-call(s32[1,4]{1,0:T(1,128)S(1)} %bitcast.7, s32[8,512]{1,0:T(8,128)S(1)} %get-tuple-element.33.slots_ref), custom_call_target="tpu_custom_call" | custom-call | flops 33554432 | bytes 16400 | tf_op jit(solution)/shard_map/pallas_call | solution.py:38
  11.8 0.0 collective-permute-done.refs_1_.refs_5_
  11.8 0.0 collective-permute-done.1.refs_2_.refs_6_
  11.8 3.1 %collective-permute-done.2.refs_3_.refs_7_ = f32[1,768]{1,0:T(1,128)S(1)} collective-permute-done((f32[1,768]{1,0:T(1,128)S(1)}, f32[1,768]{1,0:T(1,128)S(1)}, u32[]{:S(2)}, u32[]{:S(2)}) %collective-permute-start.2) | collective-permute-done | bytes 3104 | tf_op jit(solution)/shard_map/ppermute | solution.py:232
  15.0 1.4 %shard_map.79 = (f32[1,512]{1,0:T(1,128)S(1)}, bf16[64,512]{1,0:T(8,128)(2,1)S(1)}, f32[64,2048]{1,0:T(8,128)}) custom-call(f32[1,768]{1,0:T(1,128)S(1)} %get-tuple-element.27.refs_0_.refs_4_, f32[1,768]{1,0:T(1,128)S(1)} %collective-permute-done.refs_1_.refs_5_, f32[1,768]{1,0:T(1,128)S(1)} %collective-permute-done.1.refs_2_.refs_6_, ...), custom_call_target="tpu_custom_call" | custom-call | flops 134217728 | bytes 3289088 | tf_op jit(solution)/shard_map/pallas_call | solution.py:38
  16.3 0.0 collective-permute-start.3
  16.3 0.5 %shard_map.80 = f32[64,2048]{1,0:T(8,128)S(1)} custom-call(bf16[64,512]{1,0:T(8,128)(2,1)S(1)} %get-tuple-element.34.scaled_ref, bf16[512,2048]{1,0:T(8,128)(2,1)S(1)} %get-tuple-element.32.refs_5_.delta_ref), custom_call_target="tpu_custom_call" | custom-call | flops 134217728 | bytes 2162688 | tf_op jit(solution)/shard_map/pallas_call | solution.py:38
  16.8 1.8 %collective-permute-done.3 = f32[64,2048]{1,0:T(8,128)} collective-permute-done((f32[64,2048]{1,0:T(8,128)}, f32[64,2048]{1,0:T(8,128)}, u32[]{:S(2)}, u32[]{:S(2)}) %collective-permute-start.3) | collective-permute-done | bytes 524320 | tf_op jit(solution)/shard_map/ppermute | solution.py:248
  18.6 1.1 %add.28.gate_ref = f32[64,2048]{1,0:T(8,128)S(1)} add(f32[64,2048]{1,0:T(8,128)S(1)} %shard_map.80, f32[64,2048]{1,0:T(8,128)} %collective-permute-done.3) | non-fusion elementwise | flops 131072 | bytes 1572864 | tf_op jit(solution)/shard_map/add | solution.py:250
  19.7 1.6 %collective-permute-start.4 = (f32[16,2048]{1,0:T(8,128)S(1)}, f32[16,2048]{1,0:T(8,128)S(1)}, u32[]{:S(2)}, u32[]{:S(2)}) collective-permute-start(f32[16,2048]{1,0:T(8,128)S(1)} %get-tuple-element.56), channel_id=1, source_target_pairs={{0,8},{4,12},{8,0},{12,4},{16,24},{20,28},{24,16},{28,20},{1,9},{5... | collective-permute-start | bytes 393224 | tf_op jit(solution)/shard_map/ppermute | solution.py:253
  21.3 1.5 %collective-permute-start.5 = (f32[16,2048]{1,0:T(8,128)S(1)}, f32[16,2048]{1,0:T(8,128)S(1)}, u32[]{:S(2)}, u32[]{:S(2)}) collective-permute-start(f32[16,2048]{1,0:T(8,128)S(1)} %get-tuple-element.55), channel_id=1, source_target_pairs={{0,16},{4,20},{8,24},{12,28},{16,0},{20,4},{24,8},{28,12},{1,17},{... | collective-permute-start | bytes 393224 | tf_op jit(solution)/shard_map/ppermute | solution.py:253
  22.8 0.5 %collective-permute-start.6 = (f32[16,2048]{1,0:T(8,128)S(1)}, f32[16,2048]{1,0:T(8,128)S(1)}, u32[]{:S(2)}, u32[]{:S(2)}) collective-permute-start(f32[16,2048]{1,0:T(8,128)S(1)} %get-tuple-element.54), channel_id=1, source_target_pairs={{0,24},{4,28},{8,16},{12,20},{16,8},{20,12},{24,0},{28,4},{1,25},{... | collective-permute-start | bytes 393224 | tf_op jit(solution)/shard_map/ppermute | solution.py:253
  23.3 0.5 %shard_map.81 = (f32[256,128]{1,0:T(8,128)S(1)}, f32[256,128]{1,0:T(8,128)S(1)}, f32[256,128]{1,0:T(8,128)S(1)}, f32[256,128]{1,0:T(8,128)S(1)}) custom-call(bf16[1024,512]{1,0:T(8,128)(2,1)S(1)} %shard_map.78.refs_6_.named_ref, f32[128,512]{1,0:T(8,128)S(1)} %get-tuple-element.36.xgrad_ref, f32[1,512]{1,0:T(1,128)S(1)} %get-tuple-element.37.clip_ref, ...), custom_call_target="tpu_custom_call" | custom-call | flops 268435456 | bytes 1837056 | tf_op jit(solution)/shard_map/pallas_call | solution.py:38
  23.7 1.9 %collective-permute-done.4 = f32[16,2048]{1,0:T(8,128)S(1)} collective-permute-done((f32[16,2048]{1,0:T(8,128)S(1)}, f32[16,2048]{1,0:T(8,128)S(1)}, u32[]{:S(2)}, u32[]{:S(2)}) %collective-permute-start.4) | collective-permute-done | bytes 131104 | tf_op jit(solution)/shard_map/ppermute | solution.py:253
  25.7 3.7 %collective-permute-done.5 = f32[16,2048]{1,0:T(8,128)S(1)} collective-permute-done((f32[16,2048]{1,0:T(8,128)S(1)}, f32[16,2048]{1,0:T(8,128)S(1)}, u32[]{:S(2)}, u32[]{:S(2)}) %collective-permute-start.5) | collective-permute-done | bytes 131104 | tf_op jit(solution)/shard_map/ppermute | solution.py:253
  29.3 0.0 collective-permute-done.6
  29.4 1.6 %collective-permute-start.7 = (f32[16,2048]{1,0:T(8,128)S(1)}, f32[16,2048]{1,0:T(8,128)S(1)}, u32[]{:S(2)}, u32[]{:S(2)}) collective-permute-start(f32[16,2048]{1,0:T(8,128)S(1)} %get-tuple-element.53), channel_id=1, source_target_pairs={{0,24},{4,28},{8,16},{12,20},{16,8},{20,12},{24,0},{28,4},{1,25},{... | collective-permute-start | bytes 393224 | tf_op jit(solution)/shard_map/ppermute | solution.py:253
  31.0 0.0 collective-permute-start.10
  31.0 1.3 %collective-permute-start.11 = (f32[256,128]{1,0:T(8,128)S(1)}, f32[256,128]{1,0:T(8,128)S(1)}, u32[]{:S(2)}, u32[]{:S(2)}) collective-permute-start(f32[256,128]{1,0:T(8,128)S(1)} %get-tuple-element.43), channel_id=1, source_target_pairs={{0,2},{1,3},{2,0},{3,1},{4,6},{5,7},{6,4},{7,5},{8,10},{9,11},{10,... | collective-permute-start | bytes 393224 | tf_op jit(solution)/shard_map/ppermute | solution.py:271
  32.3 3.1 %collective-permute-start.12 = (f32[256,128]{1,0:T(8,128)S(1)}, f32[256,128]{1,0:T(8,128)S(1)}, u32[]{:S(2)}, u32[]{:S(2)}) collective-permute-start(f32[256,128]{1,0:T(8,128)S(1)} %get-tuple-element.44), channel_id=1, source_target_pairs={{0,3},{1,2},{2,1},{3,0},{4,7},{5,6},{6,5},{7,4},{8,11},{9,10},{10,... | collective-permute-start | bytes 393224 | tf_op jit(solution)/shard_map/ppermute | solution.py:271
  35.4 1.5 %collective-permute-start.8 = (f32[16,2048]{1,0:T(8,128)S(1)}, f32[16,2048]{1,0:T(8,128)S(1)}, u32[]{:S(2)}, u32[]{:S(2)}) collective-permute-start(f32[16,2048]{1,0:T(8,128)S(1)} %get-tuple-element.53), channel_id=1, source_target_pairs={{0,8},{4,12},{8,0},{12,4},{16,24},{20,28},{24,16},{28,20},{1,9},{5... | collective-permute-start | bytes 393224 | tf_op jit(solution)/shard_map/ppermute | solution.py:253
  36.9 0.0 collective-permute-done.7
  36.9 0.5 %collective-permute-start.9 = (f32[16,2048]{1,0:T(8,128)S(1)}, f32[16,2048]{1,0:T(8,128)S(1)}, u32[]{:S(2)}, u32[]{:S(2)}) collective-permute-start(f32[16,2048]{1,0:T(8,128)S(1)} %get-tuple-element.53), channel_id=1, source_target_pairs={{0,16},{4,20},{8,24},{12,28},{16,0},{20,4},{24,8},{28,12},{1,17},{... | collective-permute-start | bytes 393224 | tf_op jit(solution)/shard_map/ppermute | solution.py:253
  37.4 3.0 %collective-permute-done.8 = f32[16,2048]{1,0:T(8,128)S(1)} collective-permute-done((f32[16,2048]{1,0:T(8,128)S(1)}, f32[16,2048]{1,0:T(8,128)S(1)}, u32[]{:S(2)}, u32[]{:S(2)}) %collective-permute-start.8) | collective-permute-done | bytes 131104 | tf_op jit(solution)/shard_map/ppermute | solution.py:253
  40.4 1.5 %collective-permute-done.9 = f32[16,2048]{1,0:T(8,128)S(1)} collective-permute-done((f32[16,2048]{1,0:T(8,128)S(1)}, f32[16,2048]{1,0:T(8,128)S(1)}, u32[]{:S(2)}, u32[]{:S(2)}) %collective-permute-start.9) | collective-permute-done | bytes 131104 | tf_op jit(solution)/shard_map/ppermute | solution.py:253
  41.9 0.0 collective-permute-done.10.refs_1_
  41.9 1.3 %collective-permute-done.11.refs_2_ = f32[256,128]{1,0:T(8,128)S(1)} collective-permute-done((f32[256,128]{1,0:T(8,128)S(1)}, f32[256,128]{1,0:T(8,128)S(1)}, u32[]{:S(2)}, u32[]{:S(2)}) %collective-permute-start.11) | collective-permute-done | bytes 131104 | tf_op jit(solution)/shard_map/ppermute | solution.py:271
  43.1 0.0 collective-permute-done.12.refs_3_
  43.1 0.0 collective-permute-start.13
  43.1 1.3 %shard_map.82 = (f32[4,512,128]{2,1,0:T(8,128)}, f32[128,2048]{1,0:T(8,128)}) custom-call(f32[256,128]{1,0:T(8,128)S(1)} %get-tuple-element.45.refs_0_, f32[256,128]{1,0:T(8,128)S(1)} %collective-permute-done.10.refs_1_, f32[256,128]{1,0:T(8,128)S(1)} %collective-permute-done.11.refs_2_, f32[256,128]{1,0:T(8,128)S(1)} %collective-permute-done.12.refs_3_, ...), custom_call_target="tpu_custom_call" | custom-call | flops 268435456 | bytes 1060864 | tf_op jit(solution)/shard_map/pallas_call | solution.py:38
  44.4 0.6 %collective-permute-done.13.other_ref = f32[64,2048]{1,0:T(8,128)S(1)} collective-permute-done((f32[64,2048]{1,0:T(8,128)S(1)}, f32[64,2048]{1,0:T(8,128)S(1)}, u32[]{:S(2)}, u32[]{:S(2)}) %collective-permute-start.13) | collective-permute-done | bytes 524320 | tf_op jit(solution)/shard_map/ppermute | solution.py:273
  45.0 0.8 %shard_map.83 = f32[128,2048]{1,0:T(8,128)} custom-call(f32[128,2048]{1,0:T(8,128)} %get-tuple-element.50._, f32[64,2048]{1,0:T(8,128)S(1)} %collective-permute-done.13.other_ref), custom_call_target="tpu_custom_call", output_to_operand_aliasing={{}: (0, {})} | custom-call | bytes 1572864 | tf_op jit(solution)/shard_map/pallas_call | solution.py:38
  (6 shorter events, 0.1 us)
Async XLA Ops:
  0.6 8.9 %copy-start = (s32[1,1,4]{2,1,0:T(1,128)S(1)}, s32[1,1,4]{2,1,0:T(1,128)}, u32[]{:S(2)}) copy-start(s32[1,1,4]{2,1,0:T(1,128)} %param.11) | copy-start | bytes 52
  3.9 7.9 %collective-permute-start = (f32[1,768]{1,0:T(1,128)S(1)}, f32[1,768]{1,0:T(1,128)S(1)}, u32[]{:S(2)}, u32[]{:S(2)}) collective-permute-start(f32[1,768]{1,0:T(1,128)S(1)} %get-tuple-element.28), channel_id=1, source_target_pairs={{0,1},{1,0},{2,3},{3,2},{4,5},{5,4},{6,7},{7,6},{8,9},{9,8},{10,11... | collective-permute-start | bytes 9224 | tf_op jit(solution)/shard_map/ppermute | solution.py:232
  7.0 4.9 %collective-permute-start.1 = (f32[1,768]{1,0:T(1,128)S(1)}, f32[1,768]{1,0:T(1,128)S(1)}, u32[]{:S(2)}, u32[]{:S(2)}) collective-permute-start(f32[1,768]{1,0:T(1,128)S(1)} %get-tuple-element.29), channel_id=1, source_target_pairs={{0,2},{1,3},{2,0},{3,1},{4,6},{5,7},{6,4},{7,5},{8,10},{9,11},{10,... | collective-permute-start | bytes 9224 | tf_op jit(solution)/shard_map/ppermute | solution.py:232
  9.6 5.4 %collective-permute-start.2 = (f32[1,768]{1,0:T(1,128)S(1)}, f32[1,768]{1,0:T(1,128)S(1)}, u32[]{:S(2)}, u32[]{:S(2)}) collective-permute-start(f32[1,768]{1,0:T(1,128)S(1)} %get-tuple-element.30), channel_id=1, source_target_pairs={{0,3},{1,2},{2,1},{3,0},{4,7},{5,6},{6,5},{7,4},{8,11},{9,10},{10,... | collective-permute-start | bytes 9224 | tf_op jit(solution)/shard_map/ppermute | solution.py:232
  16.3 2.3 %collective-permute-start.3 = (f32[64,2048]{1,0:T(8,128)}, f32[64,2048]{1,0:T(8,128)}, u32[]{:S(2)}, u32[]{:S(2)}) collective-permute-start(f32[64,2048]{1,0:T(8,128)} %get-tuple-element.35), channel_id=1, source_target_pairs={{0,4},{4,0},{8,12},{12,8},{16,20},{20,16},{24,28},{28,24},{1,5},{5... | collective-permute-start | bytes 1572872 | tf_op jit(solution)/shard_map/ppermute | solution.py:248
  19.7 5.9 %collective-permute-start.4 = (f32[16,2048]{1,0:T(8,128)S(1)}, f32[16,2048]{1,0:T(8,128)S(1)}, u32[]{:S(2)}, u32[]{:S(2)}) collective-permute-start(f32[16,2048]{1,0:T(8,128)S(1)} %get-tuple-element.56), channel_id=1, source_target_pairs={{0,8},{4,12},{8,0},{12,4},{16,24},{20,28},{24,16},{28,20},{1,9},{5... | collective-permute-start | bytes 393224 | tf_op jit(solution)/shard_map/ppermute | solution.py:253
  21.3 8.1 %collective-permute-start.5 = (f32[16,2048]{1,0:T(8,128)S(1)}, f32[16,2048]{1,0:T(8,128)S(1)}, u32[]{:S(2)}, u32[]{:S(2)}) collective-permute-start(f32[16,2048]{1,0:T(8,128)S(1)} %get-tuple-element.55), channel_id=1, source_target_pairs={{0,16},{4,20},{8,24},{12,28},{16,0},{20,4},{24,8},{28,12},{1,17},{... | collective-permute-start | bytes 393224 | tf_op jit(solution)/shard_map/ppermute | solution.py:253
  22.8 6.6 %collective-permute-start.6 = (f32[16,2048]{1,0:T(8,128)S(1)}, f32[16,2048]{1,0:T(8,128)S(1)}, u32[]{:S(2)}, u32[]{:S(2)}) collective-permute-start(f32[16,2048]{1,0:T(8,128)S(1)} %get-tuple-element.54), channel_id=1, source_target_pairs={{0,24},{4,28},{8,16},{12,20},{16,8},{20,12},{24,0},{28,4},{1,25},{... | collective-permute-start | bytes 393224 | tf_op jit(solution)/shard_map/ppermute | solution.py:253
  29.4 7.4 %collective-permute-start.7 = (f32[16,2048]{1,0:T(8,128)S(1)}, f32[16,2048]{1,0:T(8,128)S(1)}, u32[]{:S(2)}, u32[]{:S(2)}) collective-permute-start(f32[16,2048]{1,0:T(8,128)S(1)} %get-tuple-element.53), channel_id=1, source_target_pairs={{0,24},{4,28},{8,16},{12,20},{16,8},{20,12},{24,0},{28,4},{1,25},{... | collective-permute-start | bytes 393224 | tf_op jit(solution)/shard_map/ppermute | solution.py:253
  31.0 10.9 %collective-permute-start.10 = (f32[256,128]{1,0:T(8,128)S(1)}, f32[256,128]{1,0:T(8,128)S(1)}, u32[]{:S(2)}, u32[]{:S(2)}) collective-permute-start(f32[256,128]{1,0:T(8,128)S(1)} %get-tuple-element.42), channel_id=1, source_target_pairs={{0,1},{1,0},{2,3},{3,2},{4,5},{5,4},{6,7},{7,6},{8,9},{9,8},{10,11... | collective-permute-start | bytes 393224 | tf_op jit(solution)/shard_map/ppermute | solution.py:271
  31.0 12.1 %collective-permute-start.11 = (f32[256,128]{1,0:T(8,128)S(1)}, f32[256,128]{1,0:T(8,128)S(1)}, u32[]{:S(2)}, u32[]{:S(2)}) collective-permute-start(f32[256,128]{1,0:T(8,128)S(1)} %get-tuple-element.43), channel_id=1, source_target_pairs={{0,2},{1,3},{2,0},{3,1},{4,6},{5,7},{6,4},{7,5},{8,10},{9,11},{10,... | collective-permute-start | bytes 393224 | tf_op jit(solution)/shard_map/ppermute | solution.py:271
  32.3 10.9 %collective-permute-start.12 = (f32[256,128]{1,0:T(8,128)S(1)}, f32[256,128]{1,0:T(8,128)S(1)}, u32[]{:S(2)}, u32[]{:S(2)}) collective-permute-start(f32[256,128]{1,0:T(8,128)S(1)} %get-tuple-element.44), channel_id=1, source_target_pairs={{0,3},{1,2},{2,1},{3,0},{4,7},{5,6},{6,5},{7,4},{8,11},{9,10},{10,... | collective-permute-start | bytes 393224 | tf_op jit(solution)/shard_map/ppermute | solution.py:271
  35.4 5.0 %collective-permute-start.8 = (f32[16,2048]{1,0:T(8,128)S(1)}, f32[16,2048]{1,0:T(8,128)S(1)}, u32[]{:S(2)}, u32[]{:S(2)}) collective-permute-start(f32[16,2048]{1,0:T(8,128)S(1)} %get-tuple-element.53), channel_id=1, source_target_pairs={{0,8},{4,12},{8,0},{12,4},{16,24},{20,28},{24,16},{28,20},{1,9},{5... | collective-permute-start | bytes 393224 | tf_op jit(solution)/shard_map/ppermute | solution.py:253
  36.9 5.0 %collective-permute-start.9 = (f32[16,2048]{1,0:T(8,128)S(1)}, f32[16,2048]{1,0:T(8,128)S(1)}, u32[]{:S(2)}, u32[]{:S(2)}) collective-permute-start(f32[16,2048]{1,0:T(8,128)S(1)} %get-tuple-element.53), channel_id=1, source_target_pairs={{0,16},{4,20},{8,24},{12,28},{16,0},{20,4},{24,8},{28,12},{1,17},{... | collective-permute-start | bytes 393224 | tf_op jit(solution)/shard_map/ppermute | solution.py:253
  43.1 1.9 %collective-permute-start.13 = (f32[64,2048]{1,0:T(8,128)S(1)}, f32[64,2048]{1,0:T(8,128)S(1)}, u32[]{:S(2)}, u32[]{:S(2)}) collective-permute-start(f32[64,2048]{1,0:T(8,128)S(1)} %constant_dynamic-update-slice_fusion.refs_8_), channel_id=1, source_target_pairs={{0,4},{4,0},{8,12},{12,8},{16,20},{20,16},{24,28},{28,24},{1,5},{5... | collective-permute-start | bytes 1572872 | tf_op jit(solution)/shard_map/ppermute | solution.py:273

commit v3 on v2

--- a/solution.py
+++ b/solution.py
@@ -115,7 +115,8 @@
         message_refs[s][:, examples:] = jnp.where(place < count, mine, -1).astype(F32)
 
 
-def named_kernel(owners, counts_ref, slots_ref, named_ref):
+def named_kernel(owners, counts_ref, slots_ref, pooled_ref, named_ref, turned_ref):
+    turned_ref[...] = pooled_ref[...].astype(F32).T
     width = named_ref.shape[0]
     looks, examples = slots_ref.shape
     cap = width // owners
@@ -134,8 +135,8 @@
 
 def clip_kernel(owners, *refs):
     messages = refs[:owners]
-    pooled_ref, delta_ref, _, clip_ref, scaled_ref, theirs_ref, wide_ref = refs[owners:]
-    examples, emb = pooled_ref.shape
+    turned_ref, delta_ref, _, clip_ref, scaled_ref, theirs_ref, wide_ref = refs[owners:]
+    examples = turned_ref.shape[1]
     half = theirs_ref.shape[0]
     core = lax.rem(lax.axis_index("dp"), 2)
     norm_sq = messages[0][:, :examples]
@@ -143,7 +144,7 @@
         norm_sq = norm_sq + message[:, :examples]
     clip = jnp.minimum(1.0, CLIP_NORM / jnp.sqrt(norm_sq + EPSILON))
     clip_ref[...] = clip
-    wide_ref[...] = pooled_ref[...].astype(F32).T * clip
+    wide_ref[...] = turned_ref[...] * clip
     other = wide_ref[pl.ds((1 - core) * half, half), :].astype(BF16)
     theirs_ref[...] = jnp.dot(other, delta_ref[...], preferred_element_type=F32)
     scaled_ref[...] = wide_ref[pl.ds(core * half, half), :].astype(BF16)
@@ -151,6 +152,14 @@
 
 def mine_kernel(scaled_ref, delta_ref, mine_ref):
     mine_ref[...] = jnp.dot(scaled_ref[...], delta_ref[...], preferred_element_type=F32)
+
+
+def split_kernel(steps, mine_ref, came_ref, *part_refs):
+    part = part_refs[0].shape[0]
+    chip = lax.axis_index("dp") // 2
+    for step, out_ref in zip(steps, part_refs):
+        rows = pl.ds((chip ^ step) * part, part)
+        out_ref[...] = mine_ref[rows, :] + came_ref[rows, :]
 
 
 def unique_kernel(owners, named_ref, xgrad_ref, clip_ref, gate_ref, *out_refs):
@@ -230,46 +239,52 @@
     steps = pairings(owners)
     for s in range(1, owners):
         messages[s] = lax.ppermute(messages[s], "mp", steps[s - 1])
-    (named,) = call(
-        functools.partial(named_kernel, owners), [((width, examples), BF16)],
-        8 * width * examples * looks, counts, slots, specs=[SMEM, VMEM],
+    named, turned = call(
+        functools.partial(named_kernel, owners),
+        [((width, examples), BF16), ((emb, examples), F32)],
+        8 * width * examples * looks, counts, slots, pooled, specs=[SMEM, VMEM, VMEM],
     )
     clip, scaled, theirs = call(
         functools.partial(clip_kernel, owners),
         [((1, examples), F32), ((half, examples), BF16), ((half, hid), F32)],
         2 * half * examples * hid,
-        *messages, pooled, delta, named,
+        *messages, turned, delta, named,
         specs=[VMEM] * (owners + 2) + [ANY],
         scratch=[pltpu.VMEM((emb, examples), F32)],
     )
     me = lax.axis_index("dp")
-    core, chip = me & 1, me >> 1
+    chip = me >> 1
     swap = [(i, i ^ 1) for i in range(n_dp)]
     came = lax.ppermute(theirs, "dp", swap)
     (mine,) = call(mine_kernel, [((half, hid), F32)], 2 * half * examples * hid, scaled, delta)
-    mine = mine + came
 
     def chips(piece, s):
         return lax.ppermute(piece, "dp", [(i, i ^ (2 * s)) for i in range(n_dp)])
 
+    hops = (0, 3, 1, 2)
+    if n_dp == 8:
+        parts = call(
+            functools.partial(split_kernel, hops), [((part, hid), F32)] * 4, half * hid, mine, came
+        )
+    else:
+        parts = [mine + came]
     unique = call(
         functools.partial(unique_kernel, owners), [((cap, emb), F32)] * owners,
-        4 * width * examples * emb, named, xgrad, clip, mine, specs=[VMEM] * 3 + [ANY],
-    )
+        4 * width * examples * emb, named, xgrad, clip, parts[0], specs=[VMEM] * 3 + [ANY],
+    )
+    for s in range(1, owners):
+        unique[s] = lax.ppermute(unique[s], "mp", steps[s - 1])
     if n_dp == 8:
-        got = {}
-        for s in (3, 1, 2):
-            got[s] = chips(lax.dynamic_slice_in_dim(mine, (chip ^ s) * part, part, 0), s)
-        got, _ = lax.optimization_barrier((got, unique[0]))
-        total = lax.dynamic_slice_in_dim(mine, chip * part, part, 0) + got[1] + got[2] + got[3]
+        got = [chips(piece, s) for piece, s in zip(parts[1:], hops[1:])]
+        got, unique[0] = lax.optimization_barrier((got, unique[0]))
+        total = parts[0] + got[0] + got[1] + got[2]
         own = lax.dynamic_update_slice_in_dim(jnp.zeros((half, hid), F32), total, chip * part, 0)
-        for s in (3, 1, 2):
+        own, *unique = lax.optimization_barrier((own, *unique))
+        for s in hops[1:]:
             own = lax.dynamic_update_slice_in_dim(own, chips(total, s), (chip ^ s) * part, 0)
     else:
-        own = lax.psum(mine, "dp", axis_index_groups=[list(range(c, n_dp, 2)) for c in (0, 1)])
-    for s in range(1, owners):
-        unique[s] = lax.ppermute(unique[s], "mp", steps[s - 1])
-    own, *unique = lax.optimization_barrier((own, *unique))
+        groups = [list(range(c, n_dp, 2)) for c in (0, 1)]
+        own = lax.psum(parts[0], "dp", axis_index_groups=groups)
     other = lax.ppermute(own, "dp", swap)
     table_grad, dense_grad = call(
         functools.partial(place_kernel, owners),

time: 46 us -> 39.1 us (0.85)
  waiting for transfers between devices: 16.8 us -> 13.5 us
  starting transfers between devices: 17.2 us -> 15.5 us
  other arithmetic: 1.13 us -> 0.05 us
  Pallas kernels: 9.89 us -> 9.14 us
    ppermute x6, waiting for transfers between devices: 10 us -> 4.77 us  [chips(): return lax.ppermute(piece, 'dp', [(i, i ^ 2 * s) for i in range(n_dp)])]
    ppermute x3, waiting for transfers between devices: 1.26 us -> 3.64 us  [on_device(): unique[s] = lax.ppermute(unique[s], 'mp', steps[s - 1])]
    ppermute x3, starting transfers between devices: 4.39 us -> 2.55 us  [on_device(): unique[s] = lax.ppermute(unique[s], 'mp', steps[s - 1])]
    add x1 -> x0, other arithmetic: 1.1 us -> none  [on_device(): mine = mine + came]
    pallas_call x7 -> x8, Pallas kernels: 9.89 us -> 9.14 us  [call(): pl.pallas_call(kernel, out_shape=[jax.ShapeDtypeStruct(shape, dtype) for...]
  transfers between devices with their start and end apart: 14 -> 14, of which waited for: 8 -> 8; matrix products, arithmetic and copies ran while one was open for 0% -> 0% of each run, Pallas kernels for 10% -> 12%
where the time goes in v3:
time: 39.1 us; the launch traced here: 39 us
  starting transfers between devices  15.5 us (40%)
  waiting for transfers between devices  13.5 us (35%)
  Pallas kernels  9.14 us (23%)
  between operations  0.76 us (2%)
    pallas_call x8, Pallas kernels, call(): pl.pallas_call(kernel, out_shape=[jax.ShapeDtypeStruct(shape, dtype) for...  9.14 us
    ppermute x6, starting transfers between devices, chips(): return lax.ppermute(piece, 'dp', [(i, i ^ 2 * s) for i in range(n_dp)])  7.11 us
    ppermute x3, starting transfers between devices, on_device(): messages[s] = lax.ppermute(messages[s], 'mp', steps[s - 1])  5.68 us
    ppermute x6, waiting for transfers between devices, chips(): return lax.ppermute(piece, 'dp', [(i, i ^ 2 * s) for i in range(n_dp)])  4.77 us
    ppermute x3, waiting for transfers between devices, on_device(): unique[s] = lax.ppermute(unique[s], 'mp', steps[s - 1])  3.64 us
    ppermute x3, waiting for transfers between devices, on_device(): messages[s] = lax.ppermute(messages[s], 'mp', steps[s - 1])  3.1 us
    ppermute x3, starting transfers between devices, on_device(): unique[s] = lax.ppermute(unique[s], 'mp', steps[s - 1])  2.55 us
    ppermute x1, waiting for transfers between devices, on_device(): came = lax.ppermute(theirs, 'dp', swap)  1.42 us
  transfers between devices with their start and end apart: 14, of which 8 were waited for; matrix products, arithmetic and copies ran while one was open for 0% of the time, Pallas kernels for 12%

profile of v3, /device:TPU:0, one launch (start us, length us, event | category | flops | bytes accessed | tf_op | source)
XLA Modules:
  0.0 39.0 jit_solution(14204409078766754376)
XLA Ops:
  0.6 0.0 copy-start
  0.6 3.2 %shard_map.77 = (f32[128,512]{1,0:T(8,128)S(1)}, bf16[512,2048]{1,0:T(8,128)(2,1)S(1)}, bf16[512,128]{1,0:T(8,128)(2,1)S(1)}, s32[8,512]{1,0:T(8,128)S(1)}, f32[...) custom-call(s32[1,4]{1,0:T(1,128)} %bitcast.6, ...), custom_call_target="tpu_custom_call" | custom-call | flops 268435456 | bytes 2773008 | tf_op jit(solution)/shard_map/pallas_call | solution.py:38
  3.9 3.1 %collective-permute-start = (f32[1,768]{1,0:T(1,128)S(1)}, f32[1,768]{1,0:T(1,128)S(1)}, u32[]{:S(2)}, u32[]{:S(2)}) collective-permute-start(f32[1,768]{1,0:T(1,128)S(1)} %get-tuple-element.35), channel_id=1, source_target_pairs={{0,1},{1,0},{2,3},{3,2},{4,5},{5,4},{6,7},{7,6},{8,9},{9,8},{10,11... | collective-permute-start | bytes 9224 | tf_op jit(solution)/shard_map/ppermute | solution.py:241
  7.0 2.6 %collective-permute-start.1 = (f32[1,768]{1,0:T(1,128)S(1)}, f32[1,768]{1,0:T(1,128)S(1)}, u32[]{:S(2)}, u32[]{:S(2)}) collective-permute-start(f32[1,768]{1,0:T(1,128)S(1)} %get-tuple-element.36), channel_id=1, source_target_pairs={{0,2},{1,3},{2,0},{3,1},{4,6},{5,7},{6,4},{7,5},{8,10},{9,11},{10,... | collective-permute-start | bytes 9224 | tf_op jit(solution)/shard_map/ppermute | solution.py:241
  9.6 0.0 collective-permute-start.2
  9.6 0.0 copy-done
  9.6 2.3 %shard_map.78 = (bf16[1024,512]{1,0:T(8,128)(2,1)S(1)}, f32[128,512]{1,0:T(8,128)S(1)}) custom-call(s32[1,4]{1,0:T(1,128)S(1)} %bitcast.7, s32[8,512]{1,0:T(8,128)S(1)} %get-tuple-element.38.slots_ref, bf16[512,128]{1,0:T(8,128)(2,1)S(1)} %get-tuple-element.39.pooled_ref), custom_call_target="tpu_custom_call" | custom-call | flops 33554432 | bytes 147472 | tf_op jit(solution)/shard_map/pallas_call | solution.py:38
  11.9 0.0 collective-permute-done.refs_1_.refs_5_
  11.9 0.0 collective-permute-done.1.refs_2_.refs_6_
  11.9 3.1 %collective-permute-done.2.refs_3_.refs_7_ = f32[1,768]{1,0:T(1,128)S(1)} collective-permute-done((f32[1,768]{1,0:T(1,128)S(1)}, f32[1,768]{1,0:T(1,128)S(1)}, u32[]{:S(2)}, u32[]{:S(2)}) %collective-permute-start.2) | collective-permute-done | bytes 3104 | tf_op jit(solution)/shard_map/ppermute | solution.py:241
  15.0 0.5 %shard_map.79 = (f32[1,512]{1,0:T(1,128)S(1)}, bf16[64,512]{1,0:T(8,128)(2,1)S(1)}, f32[64,2048]{1,0:T(8,128)S(1)}) custom-call(f32[1,768]{1,0:T(1,128)S(1)} %get-tuple-element.34.refs_0_.refs_4_, f32[1,768]{1,0:T(1,128)S(1)} %collective-permute-done.refs_1_.refs_5_, f32[1,768]{1,0:T(1,128)S(1)} %collective-permute-done.1.refs_2_.refs_6_, ...), custom_call_target="tpu_custom_call" | custom-call | flops 134217728 | bytes 3420160 | tf_op jit(solution)/shard_map/pallas_call | solution.py:38
  15.5 0.1 collective-permute-start.3
  15.6 0.5 %shard_map.80.mine_ref = f32[64,2048]{1,0:T(8,128)S(1)} custom-call(bf16[64,512]{1,0:T(8,128)(2,1)S(1)} %get-tuple-element.43.scaled_ref, bf16[512,2048]{1,0:T(8,128)(2,1)S(1)} %get-tuple-element.41.refs_5_.delta_ref), custom_call_target="tpu_custom_call" | custom-call | flops 134217728 | bytes 2162688 | tf_op jit(solution)/shard_map/pallas_call | solution.py:38
  16.0 1.4 %collective-permute-done.3.came_ref = f32[64,2048]{1,0:T(8,128)S(1)} collective-permute-done((f32[64,2048]{1,0:T(8,128)S(1)}, f32[64,2048]{1,0:T(8,128)S(1)}, u32[]{:S(2)}, u32[]{:S(2)}) %collective-permute-start.3) | collective-permute-done | bytes 524320 | tf_op jit(solution)/shard_map/ppermute | solution.py:258
  17.5 0.1 shard_map.81
  17.5 2.5 %collective-permute-start.4 = (f32[16,2048]{1,0:T(8,128)S(1)}, f32[16,2048]{1,0:T(8,128)S(1)}, u32[]{:S(2)}, u32[]{:S(2)}) collective-permute-start(f32[16,2048]{1,0:T(8,128)S(1)} %get-tuple-element.46), channel_id=1, source_target_pairs={{0,24},{4,28},{8,16},{12,20},{16,8},{20,12},{24,0},{28,4},{1,25},{... | collective-permute-start | bytes 393224 | tf_op jit(solution)/shard_map/ppermute | solution.py:262
  20.0 0.5 %collective-permute-start.5 = (f32[16,2048]{1,0:T(8,128)S(1)}, f32[16,2048]{1,0:T(8,128)S(1)}, u32[]{:S(2)}, u32[]{:S(2)}) collective-permute-start(f32[16,2048]{1,0:T(8,128)S(1)} %get-tuple-element.47), channel_id=1, source_target_pairs={{0,8},{4,12},{8,0},{12,4},{16,24},{20,28},{24,16},{28,20},{1,9},{5... | collective-permute-start | bytes 393224 | tf_op jit(solution)/shard_map/ppermute | solution.py:262
  20.6 0.5 %collective-permute-start.6 = (f32[16,2048]{1,0:T(8,128)S(1)}, f32[16,2048]{1,0:T(8,128)S(1)}, u32[]{:S(2)}, u32[]{:S(2)}) collective-permute-start(f32[16,2048]{1,0:T(8,128)S(1)} %get-tuple-element.48), channel_id=1, source_target_pairs={{0,16},{4,20},{8,24},{12,28},{16,0},{20,4},{24,8},{28,12},{1,17},{... | collective-permute-start | bytes 393224 | tf_op jit(solution)/shard_map/ppermute | solution.py:262
  21.1 0.5 %shard_map.82 = (f32[256,128]{1,0:T(8,128)S(1)}, f32[256,128]{1,0:T(8,128)S(1)}, f32[256,128]{1,0:T(8,128)S(1)}, f32[256,128]{1,0:T(8,128)S(1)}) custom-call(bf16[1024,512]{1,0:T(8,128)(2,1)S(1)} %get-tuple-element.42.refs_6_.named_ref, f32[128,512]{1,0:T(8,128)S(1)} %get-tuple-element.49.xgrad_ref, f32[1,512]{1,0:T(1,128)S(1)} %get-tuple-element.50.clip_ref, ...), custom_call_target="tpu_custom_call" | custom-call | flops 268435456 | bytes 1443840 | tf_op jit(solution)/shard_map/pallas_call | solution.py:38
  21.5 0.1 collective-permute-start.7
  21.6 1.3 %collective-permute-start.8 = (f32[256,128]{1,0:T(8,128)S(1)}, f32[256,128]{1,0:T(8,128)S(1)}, u32[]{:S(2)}, u32[]{:S(2)}) collective-permute-start(f32[256,128]{1,0:T(8,128)S(1)} %get-tuple-element.57), channel_id=1, source_target_pairs={{0,2},{1,3},{2,0},{3,1},{4,6},{5,7},{6,4},{7,5},{8,10},{9,11},{10,... | collective-permute-start | bytes 393224 | tf_op jit(solution)/shard_map/ppermute | solution.py:276
  22.9 1.9 %collective-permute-done.4 = f32[16,2048]{1,0:T(8,128)S(1)} collective-permute-done((f32[16,2048]{1,0:T(8,128)S(1)}, f32[16,2048]{1,0:T(8,128)S(1)}, u32[]{:S(2)}, u32[]{:S(2)}) %collective-permute-start.4) | collective-permute-done | bytes 131104 | tf_op jit(solution)/shard_map/ppermute | solution.py:262
  24.8 1.2 %collective-permute-start.9 = (f32[256,128]{1,0:T(8,128)S(1)}, f32[256,128]{1,0:T(8,128)S(1)}, u32[]{:S(2)}, u32[]{:S(2)}) collective-permute-start(f32[256,128]{1,0:T(8,128)S(1)} %get-tuple-element.58), channel_id=1, source_target_pairs={{0,3},{1,2},{2,1},{3,0},{4,7},{5,6},{6,5},{7,4},{8,11},{9,10},{10,... | collective-permute-start | bytes 393224 | tf_op jit(solution)/shard_map/ppermute | solution.py:276
  26.0 0.9 %collective-permute-done.5 = f32[16,2048]{1,0:T(8,128)S(1)} collective-permute-done((f32[16,2048]{1,0:T(8,128)S(1)}, f32[16,2048]{1,0:T(8,128)S(1)}, u32[]{:S(2)}, u32[]{:S(2)}) %collective-permute-start.5) | collective-permute-done | bytes 131104 | tf_op jit(solution)/shard_map/ppermute | solution.py:262
  26.9 0.0 collective-permute-done.6
  27.0 2.5 %collective-permute-start.10 = (f32[16,2048]{1,0:T(8,128)S(1)}, f32[16,2048]{1,0:T(8,128)S(1)}, u32[]{:S(2)}, u32[]{:S(2)}) collective-permute-start(f32[16,2048]{1,0:T(8,128)S(1)} %get-tuple-element.67), channel_id=1, source_target_pairs={{0,24},{4,28},{8,16},{12,20},{16,8},{20,12},{24,0},{28,4},{1,25},{... | collective-permute-start | bytes 393224 | tf_op jit(solution)/shard_map/ppermute | solution.py:262
  29.4 0.5 %collective-permute-start.11 = (f32[16,2048]{1,0:T(8,128)S(1)}, f32[16,2048]{1,0:T(8,128)S(1)}, u32[]{:S(2)}, u32[]{:S(2)}) collective-permute-start(f32[16,2048]{1,0:T(8,128)S(1)} %get-tuple-element.67), channel_id=1, source_target_pairs={{0,8},{4,12},{8,0},{12,4},{16,24},{20,28},{24,16},{28,20},{1,9},{5... | collective-permute-start | bytes 393224 | tf_op jit(solution)/shard_map/ppermute | solution.py:262
  30.0 0.0 collective-permute-done.7.refs_1_
  30.0 0.6 %collective-permute-start.12 = (f32[16,2048]{1,0:T(8,128)S(1)}, f32[16,2048]{1,0:T(8,128)S(1)}, u32[]{:S(2)}, u32[]{:S(2)}) collective-permute-start(f32[16,2048]{1,0:T(8,128)S(1)} %get-tuple-element.67), channel_id=1, source_target_pairs={{0,16},{4,20},{8,24},{12,28},{16,0},{20,4},{24,8},{28,12},{1,17},{... | collective-permute-start | bytes 393224 | tf_op jit(solution)/shard_map/ppermute | solution.py:262
  30.5 3.6 %collective-permute-done.8.refs_2_ = f32[256,128]{1,0:T(8,128)S(1)} collective-permute-done((f32[256,128]{1,0:T(8,128)S(1)}, f32[256,128]{1,0:T(8,128)S(1)}, u32[]{:S(2)}, u32[]{:S(2)}) %collective-permute-start.8) | collective-permute-done | bytes 131104 | tf_op jit(solution)/shard_map/ppermute | solution.py:276
  34.2 0.0 collective-permute-done.9.refs_3_
  34.2 0.2 collective-permute-done.10
  34.3 1.8 %collective-permute-done.11 = f32[16,2048]{1,0:T(8,128)S(1)} collective-permute-done((f32[16,2048]{1,0:T(8,128)S(1)}, f32[16,2048]{1,0:T(8,128)S(1)}, u32[]{:S(2)}, u32[]{:S(2)}) %collective-permute-start.11) | collective-permute-done | bytes 131104 | tf_op jit(solution)/shard_map/ppermute | solution.py:262
  36.2 0.0 collective-permute-done.12
  36.2 0.1 collective-permute-start.13
  36.3 1.3 %shard_map.83 = (f32[4,512,128]{2,1,0:T(8,128)}, f32[128,2048]{1,0:T(8,128)}) custom-call(f32[256,128]{1,0:T(8,128)S(1)} %get-tuple-element.59.refs_0_, f32[256,128]{1,0:T(8,128)S(1)} %collective-permute-done.7.refs_1_, f32[256,128]{1,0:T(8,128)S(1)} %collective-permute-done.8.refs_2_, f32[256,128]{1,0:T(8,128)S(1)} %collective-permute-done.9.refs_3_, ...), custom_call_target="tpu_custom_call" | custom-call | flops 268435456 | bytes 1060864 | tf_op jit(solution)/shard_map/pallas_call | solution.py:38
  37.6 0.6 %collective-permute-done.13.other_ref = f32[64,2048]{1,0:T(8,128)S(1)} collective-permute-done((f32[64,2048]{1,0:T(8,128)S(1)}, f32[64,2048]{1,0:T(8,128)S(1)}, u32[]{:S(2)}, u32[]{:S(2)}) %collective-permute-start.13) | collective-permute-done | bytes 524320 | tf_op jit(solution)/shard_map/ppermute | solution.py:288
  38.2 0.8 %shard_map.84 = f32[128,2048]{1,0:T(8,128)} custom-call(f32[128,2048]{1,0:T(8,128)} %get-tuple-element.64._, f32[64,2048]{1,0:T(8,128)S(1)} %collective-permute-done.13.other_ref), custom_call_target="tpu_custom_call", output_to_operand_aliasing={{}: (0, {})} | custom-call | bytes 1572864 | tf_op jit(solution)/shard_map/pallas_call | solution.py:38
  (5 shorter events, 0.1 us)
Async XLA Ops:
  0.6 8.9 %copy-start = (s32[1,1,4]{2,1,0:T(1,128)S(1)}, s32[1,1,4]{2,1,0:T(1,128)}, u32[]{:S(2)}) copy-start(s32[1,1,4]{2,1,0:T(1,128)} %param.11) | copy-start | bytes 52
  3.9 8.0 %collective-permute-start = (f32[1,768]{1,0:T(1,128)S(1)}, f32[1,768]{1,0:T(1,128)S(1)}, u32[]{:S(2)}, u32[]{:S(2)}) collective-permute-start(f32[1,768]{1,0:T(1,128)S(1)} %get-tuple-element.35), channel_id=1, source_target_pairs={{0,1},{1,0},{2,3},{3,2},{4,5},{5,4},{6,7},{7,6},{8,9},{9,8},{10,11... | collective-permute-start | bytes 9224 | tf_op jit(solution)/shard_map/ppermute | solution.py:241
  7.0 4.9 %collective-permute-start.1 = (f32[1,768]{1,0:T(1,128)S(1)}, f32[1,768]{1,0:T(1,128)S(1)}, u32[]{:S(2)}, u32[]{:S(2)}) collective-permute-start(f32[1,768]{1,0:T(1,128)S(1)} %get-tuple-element.36), channel_id=1, source_target_pairs={{0,2},{1,3},{2,0},{3,1},{4,6},{5,7},{6,4},{7,5},{8,10},{9,11},{10,... | collective-permute-start | bytes 9224 | tf_op jit(solution)/shard_map/ppermute | solution.py:241
  9.6 5.4 %collective-permute-start.2 = (f32[1,768]{1,0:T(1,128)S(1)}, f32[1,768]{1,0:T(1,128)S(1)}, u32[]{:S(2)}, u32[]{:S(2)}) collective-permute-start(f32[1,768]{1,0:T(1,128)S(1)} %get-tuple-element.37), channel_id=1, source_target_pairs={{0,3},{1,2},{2,1},{3,0},{4,7},{5,6},{6,5},{7,4},{8,11},{9,10},{10,... | collective-permute-start | bytes 9224 | tf_op jit(solution)/shard_map/ppermute | solution.py:241
  15.5 2.0 %collective-permute-start.3 = (f32[64,2048]{1,0:T(8,128)S(1)}, f32[64,2048]{1,0:T(8,128)S(1)}, u32[]{:S(2)}, u32[]{:S(2)}) collective-permute-start(f32[64,2048]{1,0:T(8,128)S(1)} %get-tuple-element.44), channel_id=1, source_target_pairs={{0,4},{4,0},{8,12},{12,8},{16,20},{20,16},{24,28},{28,24},{1,5},{5... | collective-permute-start | bytes 1572872 | tf_op jit(solution)/shard_map/ppermute | solution.py:258
  17.5 7.3 %collective-permute-start.4 = (f32[16,2048]{1,0:T(8,128)S(1)}, f32[16,2048]{1,0:T(8,128)S(1)}, u32[]{:S(2)}, u32[]{:S(2)}) collective-permute-start(f32[16,2048]{1,0:T(8,128)S(1)} %get-tuple-element.46), channel_id=1, source_target_pairs={{0,24},{4,28},{8,16},{12,20},{16,8},{20,12},{24,0},{28,4},{1,25},{... | collective-permute-start | bytes 393224 | tf_op jit(solution)/shard_map/ppermute | solution.py:262
  20.0 6.9 %collective-permute-start.5 = (f32[16,2048]{1,0:T(8,128)S(1)}, f32[16,2048]{1,0:T(8,128)S(1)}, u32[]{:S(2)}, u32[]{:S(2)}) collective-permute-start(f32[16,2048]{1,0:T(8,128)S(1)} %get-tuple-element.47), channel_id=1, source_target_pairs={{0,8},{4,12},{8,0},{12,4},{16,24},{20,28},{24,16},{28,20},{1,9},{5... | collective-permute-start | bytes 393224 | tf_op jit(solution)/shard_map/ppermute | solution.py:262
  20.6 6.3 %collective-permute-start.6 = (f32[16,2048]{1,0:T(8,128)S(1)}, f32[16,2048]{1,0:T(8,128)S(1)}, u32[]{:S(2)}, u32[]{:S(2)}) collective-permute-start(f32[16,2048]{1,0:T(8,128)S(1)} %get-tuple-element.48), channel_id=1, source_target_pairs={{0,16},{4,20},{8,24},{12,28},{16,0},{20,4},{24,8},{28,12},{1,17},{... | collective-permute-start | bytes 393224 | tf_op jit(solution)/shard_map/ppermute | solution.py:262
  21.5 8.4 %collective-permute-start.7 = (f32[256,128]{1,0:T(8,128)S(1)}, f32[256,128]{1,0:T(8,128)S(1)}, u32[]{:S(2)}, u32[]{:S(2)}) collective-permute-start(f32[256,128]{1,0:T(8,128)S(1)} %get-tuple-element.56), channel_id=1, source_target_pairs={{0,1},{1,0},{2,3},{3,2},{4,5},{5,4},{6,7},{7,6},{8,9},{9,8},{10,11... | collective-permute-start | bytes 393224 | tf_op jit(solution)/shard_map/ppermute | solution.py:276
  21.6 12.5 %collective-permute-start.8 = (f32[256,128]{1,0:T(8,128)S(1)}, f32[256,128]{1,0:T(8,128)S(1)}, u32[]{:S(2)}, u32[]{:S(2)}) collective-permute-start(f32[256,128]{1,0:T(8,128)S(1)} %get-tuple-element.57), channel_id=1, source_target_pairs={{0,2},{1,3},{2,0},{3,1},{4,6},{5,7},{6,4},{7,5},{8,10},{9,11},{10,... | collective-permute-start | bytes 393224 | tf_op jit(solution)/shard_map/ppermute | solution.py:276
  24.8 9.3 %collective-permute-start.9 = (f32[256,128]{1,0:T(8,128)S(1)}, f32[256,128]{1,0:T(8,128)S(1)}, u32[]{:S(2)}, u32[]{:S(2)}) collective-permute-start(f32[256,128]{1,0:T(8,128)S(1)} %get-tuple-element.58), channel_id=1, source_target_pairs={{0,3},{1,2},{2,1},{3,0},{4,7},{5,6},{6,5},{7,4},{8,11},{9,10},{10,... | collective-permute-start | bytes 393224 | tf_op jit(solution)/shard_map/ppermute | solution.py:276
  27.0 7.4 %collective-permute-start.10 = (f32[16,2048]{1,0:T(8,128)S(1)}, f32[16,2048]{1,0:T(8,128)S(1)}, u32[]{:S(2)}, u32[]{:S(2)}) collective-permute-start(f32[16,2048]{1,0:T(8,128)S(1)} %get-tuple-element.67), channel_id=1, source_target_pairs={{0,24},{4,28},{8,16},{12,20},{16,8},{20,12},{24,0},{28,4},{1,25},{... | collective-permute-start | bytes 393224 | tf_op jit(solution)/shard_map/ppermute | solution.py:262
  29.4 6.7 %collective-permute-start.11 = (f32[16,2048]{1,0:T(8,128)S(1)}, f32[16,2048]{1,0:T(8,128)S(1)}, u32[]{:S(2)}, u32[]{:S(2)}) collective-permute-start(f32[16,2048]{1,0:T(8,128)S(1)} %get-tuple-element.67), channel_id=1, source_target_pairs={{0,8},{4,12},{8,0},{12,4},{16,24},{20,28},{24,16},{28,20},{1,9},{5... | collective-permute-start | bytes 393224 | tf_op jit(solution)/shard_map/ppermute | solution.py:262
  30.0 6.2 %collective-permute-start.12 = (f32[16,2048]{1,0:T(8,128)S(1)}, f32[16,2048]{1,0:T(8,128)S(1)}, u32[]{:S(2)}, u32[]{:S(2)}) collective-permute-start(f32[16,2048]{1,0:T(8,128)S(1)} %get-tuple-element.67), channel_id=1, source_target_pairs={{0,16},{4,20},{8,24},{12,28},{16,0},{20,4},{24,8},{28,12},{1,17},{... | collective-permute-start | bytes 393224 | tf_op jit(solution)/shard_map/ppermute | solution.py:262
  36.2 2.0 %collective-permute-start.13 = (f32[64,2048]{1,0:T(8,128)S(1)}, f32[64,2048]{1,0:T(8,128)S(1)}, u32[]{:S(2)}, u32[]{:S(2)}) collective-permute-start(f32[64,2048]{1,0:T(8,128)S(1)} %constant_dynamic-update-slice_fusion.refs_8_), channel_id=1, source_target_pairs={{0,4},{4,0},{8,12},{12,8},{16,20},{20,16},{24,28},{28,24},{1,5},{5... | collective-permute-start | bytes 1572872 | tf_op jit(solution)/shard_map/ppermute | solution.py:288

commit v4 on v3

--- a/solution.py
+++ b/solution.py
@@ -23,6 +23,10 @@
     if n & (n - 1) == 0:
         return [[(i, i ^ s) for i in range(n)] for s in range(1, n)]
     return [[(i, (i + s) % n) for i in range(n)] for s in range(1, n)]
+
+
+def rounds(n):
+    return pairings(n)[::-1]
 
 
 def peer_to(me, s, n):
@@ -57,22 +61,18 @@
     return start, count
 
 
-def first_kernel(owners, counts_hbm, delta_hbm, w_hbm, pooled_hbm, slots_hbm, ids_hbm, *refs):
-    xgrad_ref, delta_ref, pooled_ref, slots_ref, *rest = refs
-    message_refs, (w_ref, ids_ref, counts_ref, sems) = rest[:owners], rest[owners:]
+def first_kernel(delta_hbm, w_hbm, pooled_hbm, slots_hbm, *refs):
+    xgrad_ref, delta_ref, pooled_ref, slots_ref, partial_ref, w_ref, sems = refs
     examples, emb = pooled_ref.shape
     hid = delta_ref.shape[1]
     looks = slots_ref.shape[0]
-    width = ids_ref.shape[1]
-    cap = width // owners
     blocks = list(range(0, examples, CHUNK))
     pairs = [(w_hbm, w_ref)]
     pairs += [(delta_hbm.at[pl.ds(r, CHUNK)], delta_ref.at[pl.ds(r, CHUNK)]) for r in blocks]
-    pairs += [(counts_hbm, counts_ref), (slots_hbm, slots_ref), (ids_hbm, ids_ref), (pooled_hbm, pooled_ref)]
+    pairs += [(slots_hbm, slots_ref), (pooled_hbm, pooled_ref)]
     copies = [pltpu.make_async_copy(a, b, sems.at[i]) for i, (a, b) in enumerate(pairs)]
     for copy in copies:
         copy.start()
-    me = lax.axis_index("mp")
     n = len(blocks)
     copies[0].wait()
     norms = []
@@ -105,24 +105,21 @@
             piece = pooled_ref[q:q + 128, :].astype(F32)
             sums.append(jnp.sum((piece * piece).T, axis=0, keepdims=True))
         partial = delta_sq * jnp.concatenate(sums, axis=1) + repeats[:, r:r + CHUNK] * xgrad_sq
-        for message in message_refs:
-            message[:, r:r + CHUNK] = partial
-    ids = jnp.broadcast_to(ids_ref[...], (8, width))
-    place = lax.broadcasted_iota(I32, (1, cap), 1)
-    for s in range(owners):
-        start, count = window(counts_ref, me, s, owners)
-        mine = pltpu.roll(ids, lax.rem(width - start, width), 1)[0:1, :cap]
-        message_refs[s][:, examples:] = jnp.where(place < count, mine, -1).astype(F32)
-
-
-def named_kernel(owners, counts_ref, slots_ref, pooled_ref, named_ref, turned_ref):
+        partial_ref[:, r:r + CHUNK] = partial
+
+
+def named_kernel(owners, counts_ref, slots_ref, pooled_ref, ids_ref, named_ref, turned_ref, targets_ref):
     turned_ref[...] = pooled_ref[...].astype(F32).T
     width = named_ref.shape[0]
+    ids = jnp.broadcast_to(ids_ref[...], (8, width))
     looks, examples = slots_ref.shape
     cap = width // owners
     me = lax.axis_index("mp")
     for s in range(owners):
         start, count = window(counts_ref, me, s, owners)
+        mine = pltpu.roll(ids, lax.rem(width - start, width), 1)[0:1, :cap]
+        inside = lax.broadcasted_iota(I32, (1, cap), 1) < count
+        targets_ref[s] = jnp.where(inside, mine, -1).astype(F32)
         for r in range(0, cap, 64):
             place = lax.broadcasted_iota(I32, (64, 128), 0) + r
             name = jnp.where(place < count, place + start, -1)
@@ -133,15 +130,13 @@
                 named_ref[s * cap + r:s * cap + r + 64, c:c + 128] = total.astype(BF16)
 
 
-def clip_kernel(owners, *refs):
-    messages = refs[:owners]
-    turned_ref, delta_ref, _, clip_ref, scaled_ref, theirs_ref, wide_ref = refs[owners:]
-    examples = turned_ref.shape[1]
+def clip_kernel(*refs):
+    *messages, turned_ref, delta_ref, _, clip_ref, scaled_ref, theirs_ref, wide_ref = refs
     half = theirs_ref.shape[0]
     core = lax.rem(lax.axis_index("dp"), 2)
-    norm_sq = messages[0][:, :examples]
+    norm_sq = messages[0][...]
     for message in messages[1:]:
-        norm_sq = norm_sq + message[:, :examples]
+        norm_sq = norm_sq + message[...]
     clip = jnp.minimum(1.0, CLIP_NORM / jnp.sqrt(norm_sq + EPSILON))
     clip_ref[...] = clip
     wide_ref[...] = turned_ref[...] * clip
@@ -162,8 +157,7 @@
         out_ref[...] = mine_ref[rows, :] + came_ref[rows, :]
 
 
-def unique_kernel(owners, named_ref, xgrad_ref, clip_ref, gate_ref, *out_refs):
-    del gate_ref
+def unique_kernel(owners, named_ref, xgrad_ref, clip_ref, targets_ref, _, *out_refs):
     emb = xgrad_ref.shape[0]
     cap = named_ref.shape[0] // owners
     wide = xgrad_ref[...] * clip_ref[...]
@@ -175,13 +169,16 @@
             named_ref[s * cap:(s + 1) * cap, :], terms, (((1,), (1,)), ((), ())),
             preferred_element_type=F32,
         )
-        out_refs[s][...] = both[:, :emb] + both[:, emb:]
-
-
-def place_kernel(owners, *refs):
-    pieces, messages = refs[:owners], refs[owners:2 * owners]
-    own_ref, table_ref, dense_ref, rows_ref, sems = refs[2 * owners:]
-    cap, emb = pieces[0].shape
+        out_refs[s][:cap, :] = both[:, :emb] + both[:, emb:]
+        out_refs[s][cap:, :] = jnp.zeros((out_refs[s].shape[0] - cap, emb), F32)
+        for q in range(cap // emb):
+            out_refs[s][cap + q:cap + q + 1, :] = targets_ref[s, :, q * emb:(q + 1) * emb]
+
+
+def place_kernel(owners, cap, *refs):
+    pieces = refs[:owners]
+    own_ref, table_ref, dense_ref, rows_ref, sems = refs[owners:]
+    emb = pieces[0].shape[1]
     half = own_ref.shape[0]
     me, core = lax.axis_index("mp"), lax.rem(lax.axis_index("dp"), 2)
     copy = pltpu.make_async_copy(own_ref, dense_ref.at[pl.ds(core * half, half)], sems.at[owners])
@@ -189,9 +186,10 @@
     copies = [copy]
     row = lax.broadcasted_iota(I32, (ROWS_DEV, cap), 0).astype(F32)
     for s in range(owners):
-        ids = messages[s][:, messages[s].shape[1] - cap:]
+        ids = [pieces[s][cap + q:cap + q + 1, :] for q in range(cap // emb)]
+        ids = jnp.concatenate(ids, axis=1)
         hot = jnp.where(row == ids, 1.0, 0.0).astype(BF16)
-        wide = pieces[s][...]
+        wide = pieces[s][:cap, :]
         hi = wide.astype(BF16)
         lo = (wide - hi.astype(F32)).astype(BF16)
         both = jnp.dot(hot, jnp.concatenate([hi, lo], axis=1), preferred_element_type=F32)
@@ -223,35 +221,32 @@
     looks = slots.shape[0]
     counts, ids = send_counts[0], row_ids[0]
     half, part = emb // 2, emb // 8
-
-    xgrad, delta, pooled, slots, *messages = call(
-        functools.partial(first_kernel, owners),
+    tail = -(-cap // (8 * emb)) * 8
+
+    xgrad, delta, pooled, slots, partial = call(
+        first_kernel,
         [((emb, examples), F32), (delta.shape, BF16), (pooled.shape, BF16), (slots.shape, I32)]
-        + [((1, examples + cap), F32)] * owners,
+        + [((1, examples), F32)],
         2 * emb * examples * hid,
-        *[pltpu.with_memory_space_constraint(a, pltpu.HBM) for a in (counts, delta, w_first, pooled, slots, ids)],
-        specs=[HBM] * 6,
-        scratch=[
-            pltpu.VMEM(w_first.shape, BF16), pltpu.VMEM(ids.shape, I32),
-            pltpu.SMEM(counts.shape, I32), pltpu.SemaphoreType.DMA((5 + examples // CHUNK,)),
-        ],
-    )
-    steps = pairings(owners)
-    for s in range(1, owners):
-        messages[s] = lax.ppermute(messages[s], "mp", steps[s - 1])
-    named, turned = call(
+        *[pltpu.with_memory_space_constraint(a, pltpu.HBM) for a in (delta, w_first, pooled, slots)],
+        specs=[HBM] * 4,
+        scratch=[pltpu.VMEM(w_first.shape, BF16), pltpu.SemaphoreType.DMA((3 + examples // CHUNK,))],
+    )
+    norms = [lax.ppermute(partial, "mp", r) for r in rounds(owners)]
+    named, turned, targets = call(
         functools.partial(named_kernel, owners),
-        [((width, examples), BF16), ((emb, examples), F32)],
-        8 * width * examples * looks, counts, slots, pooled, specs=[SMEM, VMEM, VMEM],
+        [((width, examples), BF16), ((emb, examples), F32), ((owners, 1, cap), F32)],
+        8 * width * examples * looks, counts, slots, pooled, ids, specs=[SMEM, VMEM, VMEM, VMEM],
     )
     clip, scaled, theirs = call(
-        functools.partial(clip_kernel, owners),
+        clip_kernel,
         [((1, examples), F32), ((half, examples), BF16), ((half, hid), F32)],
         2 * half * examples * hid,
-        *messages, turned, delta, named,
-        specs=[VMEM] * (owners + 2) + [ANY],
+        *norms, partial, turned, delta, named,
+        specs=[VMEM] * (len(norms) + 3) + [ANY],
         scratch=[pltpu.VMEM((emb, examples), F32)],
     )
+    steps = pairings(owners)
     me = lax.axis_index("dp")
     chip = me >> 1
     swap = [(i, i ^ 1) for i in range(n_dp)]
@@ -269,8 +264,8 @@
     else:
         parts = [mine + came]
     unique = call(
-        functools.partial(unique_kernel, owners), [((cap, emb), F32)] * owners,
-        4 * width * examples * emb, named, xgrad, clip, parts[0], specs=[VMEM] * 3 + [ANY],
+        functools.partial(unique_kernel, owners), [((cap + tail, emb), F32)] * owners,
+        4 * width * examples * emb, named, xgrad, clip, targets, parts[0], specs=[VMEM] * 4 + [ANY],
     )
     for s in range(1, owners):
         unique[s] = lax.ppermute(unique[s], "mp", steps[s - 1])
@@ -287,9 +282,9 @@
         own = lax.psum(parts[0], "dp", axis_index_groups=groups)
     other = lax.ppermute(own, "dp", swap)
     table_grad, dense_grad = call(
-        functools.partial(place_kernel, owners),
+        functools.partial(place_kernel, owners, cap),
         [((owners, ROWS_DEV, emb), F32), ((emb, hid), F32)],
-        4 * owners * ROWS_DEV * cap * emb, *unique, *messages, own, out_specs=[HBM, HBM],
+        4 * owners * ROWS_DEV * cap * emb, *unique, own, out_specs=[HBM, HBM],
         scratch=[pltpu.VMEM((owners, ROWS_DEV, emb), F32), pltpu.SemaphoreType.DMA((owners + 1,))],
     )
     (dense_grad,) = call(

time: 39.1 us -> 37.6 us (0.962)
  waiting for transfers between devices: 13.5 us -> 9.25 us
  starting transfers between devices: 15.5 us -> 18.2 us
    ppermute x6, waiting for transfers between devices: 4.77 us -> 1.94 us  [chips(): return lax.ppermute(piece, 'dp', [(i, i ^ 2 * s) for i in range(n_dp)])]
    ppermute x3, starting transfers between devices: 2.55 us -> 5.18 us  [on_device(): unique[s] = lax.ppermute(unique[s], 'mp', steps[s - 1])]
    ppermute x3, waiting for transfers between devices: 3.1 us -> 1.49 us  [on_device(): norms = [lax.ppermute(partial, 'mp', r) for r in rounds(owners)]]
  transfers between devices with their start and end apart: 14 -> 14, of which waited for: 8 -> 6; matrix products, arithmetic and copies ran while one was open for 0% -> 0% of each run, Pallas kernels for 12% -> 12%
where the time goes in v4:
time: 37.6 us; the launch traced here: 37.5 us
  starting transfers between devices  18.2 us (48%)
  waiting for transfers between devices  9.25 us (25%)
  Pallas kernels  9.14 us (24%)
  between operations  0.76 us (2%)
    pallas_call x8, Pallas kernels, call(): pl.pallas_call(kernel, out_shape=[jax.ShapeDtypeStruct(shape, dtype) for...  9.14 us
    ppermute x6, starting transfers between devices, chips(): return lax.ppermute(piece, 'dp', [(i, i ^ 2 * s) for i in range(n_dp)])  7.11 us
    ppermute x3, starting transfers between devices, on_device(): norms = [lax.ppermute(partial, 'mp', r) for r in rounds(owners)]  5.76 us
    ppermute x3, starting transfers between devices, on_device(): unique[s] = lax.ppermute(unique[s], 'mp', steps[s - 1])  5.18 us
    ppermute x3, waiting for transfers between devices, on_device(): unique[s] = lax.ppermute(unique[s], 'mp', steps[s - 1])  3.83 us
    ppermute x6, waiting for transfers between devices, chips(): return lax.ppermute(piece, 'dp', [(i, i ^ 2 * s) for i in range(n_dp)])  1.94 us
    ppermute x3, waiting for transfers between devices, on_device(): norms = [lax.ppermute(partial, 'mp', r) for r in rounds(owners)]  1.49 us
    ppermute x1, waiting for transfers between devices, on_device(): came = lax.ppermute(theirs, 'dp', swap)  1.42 us
  transfers between devices with their start and end apart: 14, of which 6 were waited for; matrix products, arithmetic and copies ran while one was open for 0% of the time, Pallas kernels for 12%

profile of v4, /device:TPU:0, one launch (start us, length us, event | category | flops | bytes accessed | tf_op | source)
XLA Modules:
  0.0 37.5 jit_solution(11628346251493099814)
XLA Ops:
  0.6 0.0 copy-start.1
  0.6 0.0 copy-start
  0.7 3.2 %shard_map.77 = (f32[128,512]{1,0:T(8,128)S(1)}, bf16[512,2048]{1,0:T(8,128)(2,1)S(1)}, bf16[512,128]{1,0:T(8,128)(2,1)S(1)}, s32[8,512]{1,0:T(8,128)S(1)}, f32[1,512]{1,0:T(1,128)S(1)}) custom-call(bf16[512,2048]{1,0:T(8,128)(2,1)} %delta_hbm.1, bf16[128,2048]{1,0:T(8,128)(2,1)} %w_hbm.1, bf16[512,128]{1,0:T(8,128)(2,1)} %pooled_hbm.1, s32[8,512]{1,0:T(8,128)} %bitcast.8), custom_call_target="tpu_custom_call" | custom-call | flops 268435456 | bytes 2768896 | tf_op jit(solution)/shard_map/pallas_call | solution.py:42
  3.8 5.1 %collective-permute-start = (f32[1,512]{1,0:T(1,128)S(1)}, f32[1,512]{1,0:T(1,128)S(1)}, u32[]{:S(2)}, u32[]{:S(2)}) collective-permute-start(f32[1,512]{1,0:T(1,128)S(1)} %get-tuple-element.32.refs_3_), channel_id=1, source_target_pairs={{0,3},{1,2},{2,1},{3,0},{4,7},{5,6},{6,5},{7,4},{8,11},{9,10},{10,... | collective-permute-start | bytes 6152 | tf_op jit(solution)/shard_map/ppermute | solution.py:235
  8.9 0.0 collective-permute-start.1
  8.9 0.6 %collective-permute-start.2 = (f32[1,512]{1,0:T(1,128)S(1)}, f32[1,512]{1,0:T(1,128)S(1)}, u32[]{:S(2)}, u32[]{:S(2)}) collective-permute-start(f32[1,512]{1,0:T(1,128)S(1)} %get-tuple-element.32.refs_3_), channel_id=1, source_target_pairs={{0,1},{1,0},{2,3},{3,2},{4,5},{5,4},{6,7},{7,6},{8,9},{9,8},{10,11... | collective-permute-start | bytes 6152 | tf_op jit(solution)/shard_map/ppermute | solution.py:235
  9.6 0.0 copy-done.1
  9.6 0.0 copy-done
  9.6 2.3 %shard_map.78 = (bf16[1024,512]{1,0:T(8,128)(2,1)S(1)}, f32[128,512]{1,0:T(8,128)S(1)}, f32[4,1,256]{2,1,0:T(1,128)S(1)}) custom-call(s32[1,4]{1,0:T(1,128)S(1)} %bitcast.7, s32[8,512]{1,0:T(8,128)S(1)} %get-tuple-element.33.slots_ref, bf16[512,128]{1,0:T(8,128)(2,1)S(1)} %get-tuple-element.34.pooled_ref, s32[1,1024]{1,0:T(1,128)S(1)} %bitcast.6), custom_call_target="tpu_custom_call" | custom-call | flops 33554432 | bytes 151568 | tf_op jit(solution)/shard_map/pallas_call | solution.py:42
  11.9 0.0 collective-permute-done.refs_0_
  11.9 1.5 %collective-permute-done.1.refs_1_ = f32[1,512]{1,0:T(1,128)S(1)} collective-permute-done((f32[1,512]{1,0:T(1,128)S(1)}, f32[1,512]{1,0:T(1,128)S(1)}, u32[]{:S(2)}, u32[]{:S(2)}) %collective-permute-start.1) | collective-permute-done | bytes 2080 | tf_op jit(solution)/shard_map/ppermute | solution.py:235
  13.4 0.0 collective-permute-done.2.refs_2_
  13.4 0.5 %shard_map.79 = (f32[1,512]{1,0:T(1,128)S(1)}, bf16[64,512]{1,0:T(8,128)(2,1)S(1)}, f32[64,2048]{1,0:T(8,128)S(1)}) custom-call(f32[1,512]{1,0:T(1,128)S(1)} %collective-permute-done.refs_0_, f32[1,512]{1,0:T(1,128)S(1)} %collective-permute-done.1.refs_1_, f32[1,512]{1,0:T(1,128)S(1)} %collective-permute-done.2.refs_2_, ...), custom_call_target="tpu_custom_call" | custom-call | flops 134217728 | bytes 3416064 | tf_op jit(solution)/shard_map/pallas_call | solution.py:42
  13.9 0.1 collective-permute-start.3
  14.0 0.5 %shard_map.80.mine_ref = f32[64,2048]{1,0:T(8,128)S(1)} custom-call(bf16[64,512]{1,0:T(8,128)(2,1)S(1)} %get-tuple-element.38.scaled_ref, bf16[512,2048]{1,0:T(8,128)(2,1)S(1)} %get-tuple-element.36.refs_5_.delta_ref), custom_call_target="tpu_custom_call" | custom-call | flops 134217728 | bytes 2162688 | tf_op jit(solution)/shard_map/pallas_call | solution.py:42
  14.5 1.4 %collective-permute-done.3.came_ref = f32[64,2048]{1,0:T(8,128)S(1)} collective-permute-done((f32[64,2048]{1,0:T(8,128)S(1)}, f32[64,2048]{1,0:T(8,128)S(1)}, u32[]{:S(2)}, u32[]{:S(2)}) %collective-permute-start.3) | collective-permute-done | bytes 524320 | tf_op jit(solution)/shard_map/ppermute | solution.py:253
  15.9 0.1 shard_map.81
  16.0 2.5 %collective-permute-start.4 = (f32[16,2048]{1,0:T(8,128)S(1)}, f32[16,2048]{1,0:T(8,128)S(1)}, u32[]{:S(2)}, u32[]{:S(2)}) collective-permute-start(f32[16,2048]{1,0:T(8,128)S(1)} %get-tuple-element.41), channel_id=1, source_target_pairs={{0,24},{4,28},{8,16},{12,20},{16,8},{20,12},{24,0},{28,4},{1,25},{... | collective-permute-start | bytes 393224 | tf_op jit(solution)/shard_map/ppermute | solution.py:257
  18.5 0.5 %collective-permute-start.5 = (f32[16,2048]{1,0:T(8,128)S(1)}, f32[16,2048]{1,0:T(8,128)S(1)}, u32[]{:S(2)}, u32[]{:S(2)}) collective-permute-start(f32[16,2048]{1,0:T(8,128)S(1)} %get-tuple-element.42), channel_id=1, source_target_pairs={{0,8},{4,12},{8,0},{12,4},{16,24},{20,28},{24,16},{28,20},{1,9},{5... | collective-permute-start | bytes 393224 | tf_op jit(solution)/shard_map/ppermute | solution.py:257
  19.0 0.5 %collective-permute-start.6 = (f32[16,2048]{1,0:T(8,128)S(1)}, f32[16,2048]{1,0:T(8,128)S(1)}, u32[]{:S(2)}, u32[]{:S(2)}) collective-permute-start(f32[16,2048]{1,0:T(8,128)S(1)} %get-tuple-element.43), channel_id=1, source_target_pairs={{0,16},{4,20},{8,24},{12,28},{16,0},{20,4},{24,8},{28,12},{1,17},{... | collective-permute-start | bytes 393224 | tf_op jit(solution)/shard_map/ppermute | solution.py:257
  19.5 0.5 %shard_map.82 = (f32[264,128]{1,0:T(8,128)S(1)}, f32[264,128]{1,0:T(8,128)S(1)}, f32[264,128]{1,0:T(8,128)S(1)}, f32[264,128]{1,0:T(8,128)S(1)}) custom-call(bf16[1024,512]{1,0:T(8,128)(2,1)S(1)} %get-tuple-element.37.refs_6_.named_ref, f32[128,512]{1,0:T(8,128)S(1)} %get-tuple-element.44.xgrad_ref, f32[1,512]{1,0:T(1,128)S(1)} %get-tuple-element.45.clip_ref, ...), custom_call_target="tpu_custom_call" | custom-call | flops 268435456 | bytes 1447936 | tf_op jit(solution)/shard_map/pallas_call | solution.py:42
  20.0 0.1 collective-permute-start.7
  20.1 2.8 %collective-permute-start.8 = (f32[264,128]{1,0:T(8,128)S(1)}, f32[264,128]{1,0:T(8,128)S(1)}, u32[]{:S(2)}, u32[]{:S(2)}) collective-permute-start(f32[264,128]{1,0:T(8,128)S(1)} %get-tuple-element.53), channel_id=1, source_target_pairs={{0,2},{1,3},{2,0},{3,1},{4,6},{5,7},{6,4},{7,5},{8,10},{9,11},{10,... | collective-permute-start | bytes 405512 | tf_op jit(solution)/shard_map/ppermute | solution.py:271
  22.9 0.4 collective-permute-done.4
  23.3 2.3 %collective-permute-start.9 = (f32[264,128]{1,0:T(8,128)S(1)}, f32[264,128]{1,0:T(8,128)S(1)}, u32[]{:S(2)}, u32[]{:S(2)}) collective-permute-start(f32[264,128]{1,0:T(8,128)S(1)} %get-tuple-element.54), channel_id=1, source_target_pairs={{0,3},{1,2},{2,1},{3,0},{4,7},{5,6},{6,5},{7,4},{8,11},{9,10},{10,... | collective-permute-start | bytes 405512 | tf_op jit(solution)/shard_map/ppermute | solution.py:271
  25.6 0.0 collective-permute-done.5
  25.6 0.0 collective-permute-done.6
  25.7 2.5 %collective-permute-start.10 = (f32[16,2048]{1,0:T(8,128)S(1)}, f32[16,2048]{1,0:T(8,128)S(1)}, u32[]{:S(2)}, u32[]{:S(2)}) collective-permute-start(f32[16,2048]{1,0:T(8,128)S(1)} %get-tuple-element.63), channel_id=1, source_target_pairs={{0,24},{4,28},{8,16},{12,20},{16,8},{20,12},{24,0},{28,4},{1,25},{... | collective-permute-start | bytes 393224 | tf_op jit(solution)/shard_map/ppermute | solution.py:257
  28.2 0.5 %collective-permute-start.11 = (f32[16,2048]{1,0:T(8,128)S(1)}, f32[16,2048]{1,0:T(8,128)S(1)}, u32[]{:S(2)}, u32[]{:S(2)}) collective-permute-start(f32[16,2048]{1,0:T(8,128)S(1)} %get-tuple-element.63), channel_id=1, source_target_pairs={{0,8},{4,12},{8,0},{12,4},{16,24},{20,28},{24,16},{28,20},{1,9},{5... | collective-permute-start | bytes 393224 | tf_op jit(solution)/shard_map/ppermute | solution.py:257
  28.7 0.0 collective-permute-done.7.refs_1_
  28.7 0.5 %collective-permute-start.12 = (f32[16,2048]{1,0:T(8,128)S(1)}, f32[16,2048]{1,0:T(8,128)S(1)}, u32[]{:S(2)}, u32[]{:S(2)}) collective-permute-start(f32[16,2048]{1,0:T(8,128)S(1)} %get-tuple-element.63), channel_id=1, source_target_pairs={{0,16},{4,20},{8,24},{12,28},{16,0},{20,4},{24,8},{28,12},{1,17},{... | collective-permute-start | bytes 393224 | tf_op jit(solution)/shard_map/ppermute | solution.py:257
  29.2 3.8 %collective-permute-done.8.refs_2_ = f32[264,128]{1,0:T(8,128)S(1)} collective-permute-done((f32[264,128]{1,0:T(8,128)S(1)}, f32[264,128]{1,0:T(8,128)S(1)}, u32[]{:S(2)}, u32[]{:S(2)}) %collective-permute-start.8) | collective-permute-done | bytes 135200 | tf_op jit(solution)/shard_map/ppermute | solution.py:271
  33.0 0.0 collective-permute-done.9.refs_3_
  33.0 0.0 collective-permute-done.10
  33.1 1.5 %collective-permute-done.11 = f32[16,2048]{1,0:T(8,128)S(1)} collective-permute-done((f32[16,2048]{1,0:T(8,128)S(1)}, f32[16,2048]{1,0:T(8,128)S(1)}, u32[]{:S(2)}, u32[]{:S(2)}) %collective-permute-start.11) | collective-permute-done | bytes 131104 | tf_op jit(solution)/shard_map/ppermute | solution.py:257
  34.6 0.0 collective-permute-done.12
  34.7 0.1 collective-permute-start.13
  34.8 1.3 %shard_map.83 = (f32[4,512,128]{2,1,0:T(8,128)}, f32[128,2048]{1,0:T(8,128)}) custom-call(f32[264,128]{1,0:T(8,128)S(1)} %get-tuple-element.55.refs_0_, f32[264,128]{1,0:T(8,128)S(1)} %collective-permute-done.7.refs_1_, f32[264,128]{1,0:T(8,128)S(1)} %collective-permute-done.8.refs_2_, f32[264,128]{1,0:T(8,128)S(1)} %collective-permute-done.9.refs_3_, ...), custom_call_target="tpu_custom_call" | custom-call | flops 268435456 | bytes 1064960 | tf_op jit(solution)/shard_map/pallas_call | solution.py:42
  36.1 0.6 %collective-permute-done.13.other_ref = f32[64,2048]{1,0:T(8,128)S(1)} collective-permute-done((f32[64,2048]{1,0:T(8,128)S(1)}, f32[64,2048]{1,0:T(8,128)S(1)}, u32[]{:S(2)}, u32[]{:S(2)}) %collective-permute-start.13) | collective-permute-done | bytes 524320 | tf_op jit(solution)/shard_map/ppermute | solution.py:283
  36.7 0.8 %shard_map.84 = f32[128,2048]{1,0:T(8,128)} custom-call(f32[128,2048]{1,0:T(8,128)} %get-tuple-element.60._, f32[64,2048]{1,0:T(8,128)S(1)} %collective-permute-done.13.other_ref), custom_call_target="tpu_custom_call", output_to_operand_aliasing={{}: (0, {})} | custom-call | bytes 1572864 | tf_op jit(solution)/shard_map/pallas_call | solution.py:42
  (5 shorter events, 0.1 us)
Async XLA Ops:
  0.6 9.0 %copy-start.1 = (s32[1,1,4]{2,1,0:T(1,128)S(1)}, s32[1,1,4]{2,1,0:T(1,128)}, u32[]{:S(2)}) copy-start(s32[1,1,4]{2,1,0:T(1,128)} %param.11) | copy-start | bytes 52
  0.6 9.0 %copy-start = (s32[1,1,1024]{2,1,0:T(1,128)S(1)}, s32[1,1,1024]{2,1,0:T(1,128)}, u32[]{:S(2)}) copy-start(s32[1,1,1024]{2,1,0:T(1,128)} %param.10) | copy-start | bytes 12292
  3.8 8.1 %collective-permute-start = (f32[1,512]{1,0:T(1,128)S(1)}, f32[1,512]{1,0:T(1,128)S(1)}, u32[]{:S(2)}, u32[]{:S(2)}) collective-permute-start(f32[1,512]{1,0:T(1,128)S(1)} %get-tuple-element.32.refs_3_), channel_id=1, source_target_pairs={{0,3},{1,2},{2,1},{3,0},{4,7},{5,6},{6,5},{7,4},{8,11},{9,10},{10,... | collective-permute-start | bytes 6152 | tf_op jit(solution)/shard_map/ppermute | solution.py:235
  8.9 4.5 %collective-permute-start.1 = (f32[1,512]{1,0:T(1,128)S(1)}, f32[1,512]{1,0:T(1,128)S(1)}, u32[]{:S(2)}, u32[]{:S(2)}) collective-permute-start(f32[1,512]{1,0:T(1,128)S(1)} %get-tuple-element.32.refs_3_), channel_id=1, source_target_pairs={{0,2},{1,3},{2,0},{3,1},{4,6},{5,7},{6,4},{7,5},{8,10},{9,11},{10,... | collective-permute-start | bytes 6152 | tf_op jit(solution)/shard_map/ppermute | solution.py:235
  8.9 4.5 %collective-permute-start.2 = (f32[1,512]{1,0:T(1,128)S(1)}, f32[1,512]{1,0:T(1,128)S(1)}, u32[]{:S(2)}, u32[]{:S(2)}) collective-permute-start(f32[1,512]{1,0:T(1,128)S(1)} %get-tuple-element.32.refs_3_), channel_id=1, source_target_pairs={{0,1},{1,0},{2,3},{3,2},{4,5},{5,4},{6,7},{7,6},{8,9},{9,8},{10,11... | collective-permute-start | bytes 6152 | tf_op jit(solution)/shard_map/ppermute | solution.py:235
  13.9 2.0 %collective-permute-start.3 = (f32[64,2048]{1,0:T(8,128)S(1)}, f32[64,2048]{1,0:T(8,128)S(1)}, u32[]{:S(2)}, u32[]{:S(2)}) collective-permute-start(f32[64,2048]{1,0:T(8,128)S(1)} %get-tuple-element.39), channel_id=1, source_target_pairs={{0,4},{4,0},{8,12},{12,8},{16,20},{20,16},{24,28},{28,24},{1,5},{5... | collective-permute-start | bytes 1572872 | tf_op jit(solution)/shard_map/ppermute | solution.py:253
  16.0 7.3 %collective-permute-start.4 = (f32[16,2048]{1,0:T(8,128)S(1)}, f32[16,2048]{1,0:T(8,128)S(1)}, u32[]{:S(2)}, u32[]{:S(2)}) collective-permute-start(f32[16,2048]{1,0:T(8,128)S(1)} %get-tuple-element.41), channel_id=1, source_target_pairs={{0,24},{4,28},{8,16},{12,20},{16,8},{20,12},{24,0},{28,4},{1,25},{... | collective-permute-start | bytes 393224 | tf_op jit(solution)/shard_map/ppermute | solution.py:257
  18.5 7.1 %collective-permute-start.5 = (f32[16,2048]{1,0:T(8,128)S(1)}, f32[16,2048]{1,0:T(8,128)S(1)}, u32[]{:S(2)}, u32[]{:S(2)}) collective-permute-start(f32[16,2048]{1,0:T(8,128)S(1)} %get-tuple-element.42), channel_id=1, source_target_pairs={{0,8},{4,12},{8,0},{12,4},{16,24},{20,28},{24,16},{28,20},{1,9},{5... | collective-permute-start | bytes 393224 | tf_op jit(solution)/shard_map/ppermute | solution.py:257
  19.0 6.5 %collective-permute-start.6 = (f32[16,2048]{1,0:T(8,128)S(1)}, f32[16,2048]{1,0:T(8,128)S(1)}, u32[]{:S(2)}, u32[]{:S(2)}) collective-permute-start(f32[16,2048]{1,0:T(8,128)S(1)} %get-tuple-element.43), channel_id=1, source_target_pairs={{0,16},{4,20},{8,24},{12,28},{16,0},{20,4},{24,8},{28,12},{1,17},{... | collective-permute-start | bytes 393224 | tf_op jit(solution)/shard_map/ppermute | solution.py:257
  20.0 8.7 %collective-permute-start.7 = (f32[264,128]{1,0:T(8,128)S(1)}, f32[264,128]{1,0:T(8,128)S(1)}, u32[]{:S(2)}, u32[]{:S(2)}) collective-permute-start(f32[264,128]{1,0:T(8,128)S(1)} %get-tuple-element.52), channel_id=1, source_target_pairs={{0,1},{1,0},{2,3},{3,2},{4,5},{5,4},{6,7},{7,6},{8,9},{9,8},{10,11... | collective-permute-start | bytes 405512 | tf_op jit(solution)/shard_map/ppermute | solution.py:271
  20.1 12.9 %collective-permute-start.8 = (f32[264,128]{1,0:T(8,128)S(1)}, f32[264,128]{1,0:T(8,128)S(1)}, u32[]{:S(2)}, u32[]{:S(2)}) collective-permute-start(f32[264,128]{1,0:T(8,128)S(1)} %get-tuple-element.53), channel_id=1, source_target_pairs={{0,2},{1,3},{2,0},{3,1},{4,6},{5,7},{6,4},{7,5},{8,10},{9,11},{10,... | collective-permute-start | bytes 405512 | tf_op jit(solution)/shard_map/ppermute | solution.py:271
  23.3 9.8 %collective-permute-start.9 = (f32[264,128]{1,0:T(8,128)S(1)}, f32[264,128]{1,0:T(8,128)S(1)}, u32[]{:S(2)}, u32[]{:S(2)}) collective-permute-start(f32[264,128]{1,0:T(8,128)S(1)} %get-tuple-element.54), channel_id=1, source_target_pairs={{0,3},{1,2},{2,1},{3,0},{4,7},{5,6},{6,5},{7,4},{8,11},{9,10},{10,... | collective-permute-start | bytes 405512 | tf_op jit(solution)/shard_map/ppermute | solution.py:271
  25.7 7.4 %collective-permute-start.10 = (f32[16,2048]{1,0:T(8,128)S(1)}, f32[16,2048]{1,0:T(8,128)S(1)}, u32[]{:S(2)}, u32[]{:S(2)}) collective-permute-start(f32[16,2048]{1,0:T(8,128)S(1)} %get-tuple-element.63), channel_id=1, source_target_pairs={{0,24},{4,28},{8,16},{12,20},{16,8},{20,12},{24,0},{28,4},{1,25},{... | collective-permute-start | bytes 393224 | tf_op jit(solution)/shard_map/ppermute | solution.py:257
  28.2 6.5 %collective-permute-start.11 = (f32[16,2048]{1,0:T(8,128)S(1)}, f32[16,2048]{1,0:T(8,128)S(1)}, u32[]{:S(2)}, u32[]{:S(2)}) collective-permute-start(f32[16,2048]{1,0:T(8,128)S(1)} %get-tuple-element.63), channel_id=1, source_target_pairs={{0,8},{4,12},{8,0},{12,4},{16,24},{20,28},{24,16},{28,20},{1,9},{5... | collective-permute-start | bytes 393224 | tf_op jit(solution)/shard_map/ppermute | solution.py:257
  28.7 5.9 %collective-permute-start.12 = (f32[16,2048]{1,0:T(8,128)S(1)}, f32[16,2048]{1,0:T(8,128)S(1)}, u32[]{:S(2)}, u32[]{:S(2)}) collective-permute-start(f32[16,2048]{1,0:T(8,128)S(1)} %get-tuple-element.63), channel_id=1, source_target_pairs={{0,16},{4,20},{8,24},{12,28},{16,0},{20,4},{24,8},{28,12},{1,17},{... | collective-permute-start | bytes 393224 | tf_op jit(solution)/shard_map/ppermute | solution.py:257
  34.7 2.0 %collective-permute-start.13 = (f32[64,2048]{1,0:T(8,128)S(1)}, f32[64,2048]{1,0:T(8,128)S(1)}, u32[]{:S(2)}, u32[]{:S(2)}) collective-permute-start(f32[64,2048]{1,0:T(8,128)S(1)} %constant_dynamic-update-slice_fusion.refs_4_), channel_id=1, source_target_pairs={{0,4},{4,0},{8,12},{12,8},{16,20},{20,16},{24,28},{28,24},{1,5},{5... | collective-permute-start | bytes 1572872 | tf_op jit(solution)/shard_map/ppermute | solution.py:283

commit v5 on v4

--- a/solution.py
+++ b/solution.py
@@ -115,19 +115,25 @@
     looks, examples = slots_ref.shape
     cap = width // owners
     me = lax.axis_index("mp")
+    one, zero = jnp.ones((16, 128), BF16), jnp.zeros((16, 128), BF16)
+    wide = {}
+    for l in range(looks):
+        for c in range(0, examples, 128):
+            line = jnp.broadcast_to(slots_ref[l:l + 1, c:c + 128], (16, 128))
+            wide[l, c // 128] = line.astype(jnp.int16)
     for s in range(owners):
         start, count = window(counts_ref, me, s, owners)
         mine = pltpu.roll(ids, lax.rem(width - start, width), 1)[0:1, :cap]
         inside = lax.broadcasted_iota(I32, (1, cap), 1) < count
         targets_ref[s] = jnp.where(inside, mine, -1).astype(F32)
-        for r in range(0, cap, 64):
-            place = lax.broadcasted_iota(I32, (64, 128), 0) + r
-            name = jnp.where(place < count, place + start, -1)
+        for r in range(0, cap, 16):
+            place = lax.broadcasted_iota(I32, (16, 128), 0) + r
+            name = jnp.where(place < count, place + start, -1).astype(jnp.int16)
             for c in range(0, examples, 128):
-                total = jnp.zeros((64, 128), F32)
+                total = jnp.zeros((16, 128), BF16)
                 for l in range(looks):
-                    total = total + jnp.where(slots_ref[l:l + 1, c:c + 128] == name, 1.0, 0.0)
-                named_ref[s * cap + r:s * cap + r + 64, c:c + 128] = total.astype(BF16)
+                    total = total + jnp.where(wide[l, c // 128] == name, one, zero)
+                named_ref[s * cap + r:s * cap + r + 16, c:c + 128] = total
 
 
 def clip_kernel(*refs):
@@ -256,7 +262,7 @@
     def chips(piece, s):
         return lax.ppermute(piece, "dp", [(i, i ^ (2 * s)) for i in range(n_dp)])
 
-    hops = (0, 3, 1, 2)
+    hops = (0, 2, 3, 1)
     if n_dp == 8:
         parts = call(
             functools.partial(split_kernel, hops), [((part, hid), F32)] * 4, half * hid, mine, came

time: 37.6 us -> 37.2 us (0.989)
  waiting for transfers between devices: 9.25 us -> 11 us
  starting transfers between devices: 18.2 us -> 16.7 us
  Pallas kernels: 9.14 us -> 8.42 us
    ppermute x3, starting transfers between devices: 5.18 us -> 3.74 us  [on_device(): unique[s] = lax.ppermute(unique[s], 'mp', steps[s - 1])]
    ppermute x6, waiting for transfers between devices: 1.94 us -> 3.03 us  [chips(): return lax.ppermute(piece, 'dp', [(i, i ^ 2 * s) for i in range(n_dp)])]
    pallas_call x8, Pallas kernels: 9.14 us -> 8.42 us  [call(): pl.pallas_call(kernel, out_shape=[jax.ShapeDtypeStruct(shape, dtype) for...]
    ppermute x3, waiting for transfers between devices: 1.49 us -> 2.21 us  [on_device(): norms = [lax.ppermute(partial, 'mp', r) for r in rounds(owners)]]
  transfers between devices with their start and end apart: 14 -> 14, of which waited for: 6 -> 8; matrix products, arithmetic and copies ran while one was open for 0% -> 0% of each run, Pallas kernels for 12% -> 10%
where the time goes in v5:
time: 37.2 us; the launch traced here: 37 us
  starting transfers between devices  16.7 us (45%)
  waiting for transfers between devices  11 us (30%)
  Pallas kernels  8.42 us (23%)
  between operations  0.75 us (2%)
    pallas_call x8, Pallas kernels, call(): pl.pallas_call(kernel, out_shape=[jax.ShapeDtypeStruct(shape, dtype) for...  8.42 us
    ppermute x6, starting transfers between devices, chips(): return lax.ppermute(piece, 'dp', [(i, i ^ 2 * s) for i in range(n_dp)])  7.11 us
    ppermute x3, starting transfers between devices, on_device(): norms = [lax.ppermute(partial, 'mp', r) for r in rounds(owners)]  5.76 us
    ppermute x3, waiting for transfers between devices, on_device(): unique[s] = lax.ppermute(unique[s], 'mp', steps[s - 1])  3.78 us
    ppermute x3, starting transfers between devices, on_device(): unique[s] = lax.ppermute(unique[s], 'mp', steps[s - 1])  3.74 us
    ppermute x6, waiting for transfers between devices, chips(): return lax.ppermute(piece, 'dp', [(i, i ^ 2 * s) for i in range(n_dp)])  3.03 us
    ppermute x3, waiting for transfers between devices, on_device(): norms = [lax.ppermute(partial, 'mp', r) for r in rounds(owners)]  2.21 us
    ppermute x1, waiting for transfers between devices, on_device(): came = lax.ppermute(theirs, 'dp', swap)  1.42 us
  transfers between devices with their start and end apart: 14, of which 8 were waited for; matrix products, arithmetic and copies ran while one was open for 0% of the time, Pallas kernels for 10%

profile of v5, /device:TPU:0, one launch (start us, length us, event | category | flops | bytes accessed | tf_op | source)
XLA Modules:
  0.0 37.0 jit_solution(7044950067816310573)
XLA Ops:
  0.6 0.0 copy-start.1
  0.6 0.0 copy-start
  0.7 3.2 %shard_map.77 = (f32[128,512]{1,0:T(8,128)S(1)}, bf16[512,2048]{1,0:T(8,128)(2,1)S(1)}, bf16[512,128]{1,0:T(8,128)(2,1)S(1)}, s32[8,512]{1,0:T(8,128)S(1)}, f32[1,512]{1,0:T(1,128)S(1)}) custom-call(bf16[512,2048]{1,0:T(8,128)(2,1)} %delta_hbm.1, bf16[128,2048]{1,0:T(8,128)(2,1)} %w_hbm.1, bf16[512,128]{1,0:T(8,128)(2,1)} %pooled_hbm.1, s32[8,512]{1,0:T(8,128)} %bitcast.8), custom_call_target="tpu_custom_call" | custom-call | flops 268435456 | bytes 2768896 | tf_op jit(solution)/shard_map/pallas_call | solution.py:42
  3.8 5.1 %collective-permute-start = (f32[1,512]{1,0:T(1,128)S(1)}, f32[1,512]{1,0:T(1,128)S(1)}, u32[]{:S(2)}, u32[]{:S(2)}) collective-permute-start(f32[1,512]{1,0:T(1,128)S(1)} %get-tuple-element.32.refs_3_), channel_id=1, source_target_pairs={{0,3},{1,2},{2,1},{3,0},{4,7},{5,6},{6,5},{7,4},{8,11},{9,10},{10,... | collective-permute-start | bytes 6152 | tf_op jit(solution)/shard_map/ppermute | solution.py:241
  8.9 0.0 collective-permute-start.1
  8.9 0.6 %collective-permute-start.2 = (f32[1,512]{1,0:T(1,128)S(1)}, f32[1,512]{1,0:T(1,128)S(1)}, u32[]{:S(2)}, u32[]{:S(2)}) collective-permute-start(f32[1,512]{1,0:T(1,128)S(1)} %get-tuple-element.32.refs_3_), channel_id=1, source_target_pairs={{0,1},{1,0},{2,3},{3,2},{4,5},{5,4},{6,7},{7,6},{8,9},{9,8},{10,11... | collective-permute-start | bytes 6152 | tf_op jit(solution)/shard_map/ppermute | solution.py:241
  9.6 0.0 copy-done.1
  9.6 0.0 copy-done
  9.6 1.6 %shard_map.78 = (bf16[1024,512]{1,0:T(8,128)(2,1)S(1)}, f32[128,512]{1,0:T(8,128)S(1)}, f32[4,1,256]{2,1,0:T(1,128)S(1)}) custom-call(s32[1,4]{1,0:T(1,128)S(1)} %bitcast.7, s32[8,512]{1,0:T(8,128)S(1)} %get-tuple-element.33.slots_ref, bf16[512,128]{1,0:T(8,128)(2,1)S(1)} %get-tuple-element.34.pooled_ref, s32[1,1024]{1,0:T(1,128)S(1)} %bitcast.6), custom_call_target="tpu_custom_call" | custom-call | flops 33554432 | bytes 151568 | tf_op jit(solution)/shard_map/pallas_call | solution.py:42
  11.2 0.0 collective-permute-done.refs_0_
  11.2 2.2 %collective-permute-done.1.refs_1_ = f32[1,512]{1,0:T(1,128)S(1)} collective-permute-done((f32[1,512]{1,0:T(1,128)S(1)}, f32[1,512]{1,0:T(1,128)S(1)}, u32[]{:S(2)}, u32[]{:S(2)}) %collective-permute-start.1) | collective-permute-done | bytes 2080 | tf_op jit(solution)/shard_map/ppermute | solution.py:241
  13.4 0.0 collective-permute-done.2.refs_2_
  13.4 0.5 %shard_map.79 = (f32[1,512]{1,0:T(1,128)S(1)}, bf16[64,512]{1,0:T(8,128)(2,1)S(1)}, f32[64,2048]{1,0:T(8,128)S(1)}) custom-call(f32[1,512]{1,0:T(1,128)S(1)} %collective-permute-done.refs_0_, f32[1,512]{1,0:T(1,128)S(1)} %collective-permute-done.1.refs_1_, f32[1,512]{1,0:T(1,128)S(1)} %collective-permute-done.2.refs_2_, ...), custom_call_target="tpu_custom_call" | custom-call | flops 134217728 | bytes 3416064 | tf_op jit(solution)/shard_map/pallas_call | solution.py:42
  13.9 0.1 collective-permute-start.3
  14.0 0.5 %shard_map.80.mine_ref = f32[64,2048]{1,0:T(8,128)S(1)} custom-call(bf16[64,512]{1,0:T(8,128)(2,1)S(1)} %get-tuple-element.38.scaled_ref, bf16[512,2048]{1,0:T(8,128)(2,1)S(1)} %get-tuple-element.36.refs_5_.delta_ref), custom_call_target="tpu_custom_call" | custom-call | flops 134217728 | bytes 2162688 | tf_op jit(solution)/shard_map/pallas_call | solution.py:42
  14.5 1.4 %collective-permute-done.3.came_ref = f32[64,2048]{1,0:T(8,128)S(1)} collective-permute-done((f32[64,2048]{1,0:T(8,128)S(1)}, f32[64,2048]{1,0:T(8,128)S(1)}, u32[]{:S(2)}, u32[]{:S(2)}) %collective-permute-start.3) | collective-permute-done | bytes 524320 | tf_op jit(solution)/shard_map/ppermute | solution.py:259
  15.9 0.1 shard_map.81
  16.0 1.6 %collective-permute-start.4 = (f32[16,2048]{1,0:T(8,128)S(1)}, f32[16,2048]{1,0:T(8,128)S(1)}, u32[]{:S(2)}, u32[]{:S(2)}) collective-permute-start(f32[16,2048]{1,0:T(8,128)S(1)} %get-tuple-element.41), channel_id=1, source_target_pairs={{0,16},{4,20},{8,24},{12,28},{16,0},{20,4},{24,8},{28,12},{1,17},{... | collective-permute-start | bytes 393224 | tf_op jit(solution)/shard_map/ppermute | solution.py:263
  17.6 1.4 %collective-permute-start.5 = (f32[16,2048]{1,0:T(8,128)S(1)}, f32[16,2048]{1,0:T(8,128)S(1)}, u32[]{:S(2)}, u32[]{:S(2)}) collective-permute-start(f32[16,2048]{1,0:T(8,128)S(1)} %get-tuple-element.42), channel_id=1, source_target_pairs={{0,24},{4,28},{8,16},{12,20},{16,8},{20,12},{24,0},{28,4},{1,25},{... | collective-permute-start | bytes 393224 | tf_op jit(solution)/shard_map/ppermute | solution.py:263
  19.0 0.5 %collective-permute-start.6 = (f32[16,2048]{1,0:T(8,128)S(1)}, f32[16,2048]{1,0:T(8,128)S(1)}, u32[]{:S(2)}, u32[]{:S(2)}) collective-permute-start(f32[16,2048]{1,0:T(8,128)S(1)} %get-tuple-element.43), channel_id=1, source_target_pairs={{0,8},{4,12},{8,0},{12,4},{16,24},{20,28},{24,16},{28,20},{1,9},{5... | collective-permute-start | bytes 393224 | tf_op jit(solution)/shard_map/ppermute | solution.py:263
  19.5 0.5 %shard_map.82 = (f32[264,128]{1,0:T(8,128)S(1)}, f32[264,128]{1,0:T(8,128)S(1)}, f32[264,128]{1,0:T(8,128)S(1)}, f32[264,128]{1,0:T(8,128)S(1)}) custom-call(bf16[1024,512]{1,0:T(8,128)(2,1)S(1)} %get-tuple-element.37.refs_6_.named_ref, f32[128,512]{1,0:T(8,128)S(1)} %get-tuple-element.44.xgrad_ref, f32[1,512]{1,0:T(1,128)S(1)} %get-tuple-element.45.clip_ref, ...), custom_call_target="tpu_custom_call" | custom-call | flops 268435456 | bytes 1447936 | tf_op jit(solution)/shard_map/pallas_call | solution.py:42
  20.0 0.1 collective-permute-start.7
  20.1 2.1 %collective-permute-start.8 = (f32[264,128]{1,0:T(8,128)S(1)}, f32[264,128]{1,0:T(8,128)S(1)}, u32[]{:S(2)}, u32[]{:S(2)}) collective-permute-start(f32[264,128]{1,0:T(8,128)S(1)} %get-tuple-element.53), channel_id=1, source_target_pairs={{0,2},{1,3},{2,0},{3,1},{4,6},{5,7},{6,4},{7,5},{8,10},{9,11},{10,... | collective-permute-start | bytes 405512 | tf_op jit(solution)/shard_map/ppermute | solution.py:277
  22.2 1.7 %collective-permute-done.4 = f32[16,2048]{1,0:T(8,128)S(1)} collective-permute-done((f32[16,2048]{1,0:T(8,128)S(1)}, f32[16,2048]{1,0:T(8,128)S(1)}, u32[]{:S(2)}, u32[]{:S(2)}) %collective-permute-start.4) | collective-permute-done | bytes 131104 | tf_op jit(solution)/shard_map/ppermute | solution.py:263
  23.9 1.6 %collective-permute-start.9 = (f32[264,128]{1,0:T(8,128)S(1)}, f32[264,128]{1,0:T(8,128)S(1)}, u32[]{:S(2)}, u32[]{:S(2)}) collective-permute-start(f32[264,128]{1,0:T(8,128)S(1)} %get-tuple-element.54), channel_id=1, source_target_pairs={{0,3},{1,2},{2,1},{3,0},{4,7},{5,6},{6,5},{7,4},{8,11},{9,10},{10,... | collective-permute-start | bytes 405512 | tf_op jit(solution)/shard_map/ppermute | solution.py:277
  25.5 0.0 collective-permute-done.5
  25.5 0.1 collective-permute-done.6
  25.7 1.9 %collective-permute-start.10 = (f32[16,2048]{1,0:T(8,128)S(1)}, f32[16,2048]{1,0:T(8,128)S(1)}, u32[]{:S(2)}, u32[]{:S(2)}) collective-permute-start(f32[16,2048]{1,0:T(8,128)S(1)} %get-tuple-element.63), channel_id=1, source_target_pairs={{0,16},{4,20},{8,24},{12,28},{16,0},{20,4},{24,8},{28,12},{1,17},{... | collective-permute-start | bytes 393224 | tf_op jit(solution)/shard_map/ppermute | solution.py:263
  27.6 1.1 %collective-permute-start.11 = (f32[16,2048]{1,0:T(8,128)S(1)}, f32[16,2048]{1,0:T(8,128)S(1)}, u32[]{:S(2)}, u32[]{:S(2)}) collective-permute-start(f32[16,2048]{1,0:T(8,128)S(1)} %get-tuple-element.63), channel_id=1, source_target_pairs={{0,24},{4,28},{8,16},{12,20},{16,8},{20,12},{24,0},{28,4},{1,25},{... | collective-permute-start | bytes 393224 | tf_op jit(solution)/shard_map/ppermute | solution.py:263
  28.7 0.0 collective-permute-done.7.refs_1_
  28.7 0.5 %collective-permute-start.12 = (f32[16,2048]{1,0:T(8,128)S(1)}, f32[16,2048]{1,0:T(8,128)S(1)}, u32[]{:S(2)}, u32[]{:S(2)}) collective-permute-start(f32[16,2048]{1,0:T(8,128)S(1)} %get-tuple-element.63), channel_id=1, source_target_pairs={{0,8},{4,12},{8,0},{12,4},{16,24},{20,28},{24,16},{28,20},{1,9},{5... | collective-permute-start | bytes 393224 | tf_op jit(solution)/shard_map/ppermute | solution.py:263
  29.3 3.8 %collective-permute-done.8.refs_2_ = f32[264,128]{1,0:T(8,128)S(1)} collective-permute-done((f32[264,128]{1,0:T(8,128)S(1)}, f32[264,128]{1,0:T(8,128)S(1)}, u32[]{:S(2)}, u32[]{:S(2)}) %collective-permute-start.8) | collective-permute-done | bytes 135200 | tf_op jit(solution)/shard_map/ppermute | solution.py:277
  33.0 0.0 collective-permute-done.9.refs_3_
  33.0 0.0 collective-permute-done.10
  33.1 0.8 %collective-permute-done.11 = f32[16,2048]{1,0:T(8,128)S(1)} collective-permute-done((f32[16,2048]{1,0:T(8,128)S(1)}, f32[16,2048]{1,0:T(8,128)S(1)}, u32[]{:S(2)}, u32[]{:S(2)}) %collective-permute-start.11) | collective-permute-done | bytes 131104 | tf_op jit(solution)/shard_map/ppermute | solution.py:263
  33.9 0.3 collective-permute-done.12
  34.3 0.1 collective-permute-start.13
  34.3 1.3 %shard_map.83 = (f32[4,512,128]{2,1,0:T(8,128)}, f32[128,2048]{1,0:T(8,128)}) custom-call(f32[264,128]{1,0:T(8,128)S(1)} %get-tuple-element.55.refs_0_, f32[264,128]{1,0:T(8,128)S(1)} %collective-permute-done.7.refs_1_, f32[264,128]{1,0:T(8,128)S(1)} %collective-permute-done.8.refs_2_, f32[264,128]{1,0:T(8,128)S(1)} %collective-permute-done.9.refs_3_, ...), custom_call_target="tpu_custom_call" | custom-call | flops 268435456 | bytes 1064960 | tf_op jit(solution)/shard_map/pallas_call | solution.py:42
  35.7 0.6 %collective-permute-done.13.other_ref = f32[64,2048]{1,0:T(8,128)S(1)} collective-permute-done((f32[64,2048]{1,0:T(8,128)S(1)}, f32[64,2048]{1,0:T(8,128)S(1)}, u32[]{:S(2)}, u32[]{:S(2)}) %collective-permute-start.13) | collective-permute-done | bytes 524320 | tf_op jit(solution)/shard_map/ppermute | solution.py:289
  36.2 0.8 %shard_map.84 = f32[128,2048]{1,0:T(8,128)} custom-call(f32[128,2048]{1,0:T(8,128)} %get-tuple-element.60._, f32[64,2048]{1,0:T(8,128)S(1)} %collective-permute-done.13.other_ref), custom_call_target="tpu_custom_call", output_to_operand_aliasing={{}: (0, {})} | custom-call | bytes 1572864 | tf_op jit(solution)/shard_map/pallas_call | solution.py:42
  (5 shorter events, 0.1 us)
Async XLA Ops:
  0.6 9.0 %copy-start.1 = (s32[1,1,4]{2,1,0:T(1,128)S(1)}, s32[1,1,4]{2,1,0:T(1,128)}, u32[]{:S(2)}) copy-start(s32[1,1,4]{2,1,0:T(1,128)} %param.11) | copy-start | bytes 52
  0.6 9.0 %copy-start = (s32[1,1,1024]{2,1,0:T(1,128)S(1)}, s32[1,1,1024]{2,1,0:T(1,128)}, u32[]{:S(2)}) copy-start(s32[1,1,1024]{2,1,0:T(1,128)} %param.10) | copy-start | bytes 12292
  3.8 7.4 %collective-permute-start = (f32[1,512]{1,0:T(1,128)S(1)}, f32[1,512]{1,0:T(1,128)S(1)}, u32[]{:S(2)}, u32[]{:S(2)}) collective-permute-start(f32[1,512]{1,0:T(1,128)S(1)} %get-tuple-element.32.refs_3_), channel_id=1, source_target_pairs={{0,3},{1,2},{2,1},{3,0},{4,7},{5,6},{6,5},{7,4},{8,11},{9,10},{10,... | collective-permute-start | bytes 6152 | tf_op jit(solution)/shard_map/ppermute | solution.py:241
  8.9 4.5 %collective-permute-start.1 = (f32[1,512]{1,0:T(1,128)S(1)}, f32[1,512]{1,0:T(1,128)S(1)}, u32[]{:S(2)}, u32[]{:S(2)}) collective-permute-start(f32[1,512]{1,0:T(1,128)S(1)} %get-tuple-element.32.refs_3_), channel_id=1, source_target_pairs={{0,2},{1,3},{2,0},{3,1},{4,6},{5,7},{6,4},{7,5},{8,10},{9,11},{10,... | collective-permute-start | bytes 6152 | tf_op jit(solution)/shard_map/ppermute | solution.py:241
  8.9 4.5 %collective-permute-start.2 = (f32[1,512]{1,0:T(1,128)S(1)}, f32[1,512]{1,0:T(1,128)S(1)}, u32[]{:S(2)}, u32[]{:S(2)}) collective-permute-start(f32[1,512]{1,0:T(1,128)S(1)} %get-tuple-element.32.refs_3_), channel_id=1, source_target_pairs={{0,1},{1,0},{2,3},{3,2},{4,5},{5,4},{6,7},{7,6},{8,9},{9,8},{10,11... | collective-permute-start | bytes 6152 | tf_op jit(solution)/shard_map/ppermute | solution.py:241
  13.9 2.0 %collective-permute-start.3 = (f32[64,2048]{1,0:T(8,128)S(1)}, f32[64,2048]{1,0:T(8,128)S(1)}, u32[]{:S(2)}, u32[]{:S(2)}) collective-permute-start(f32[64,2048]{1,0:T(8,128)S(1)} %get-tuple-element.39), channel_id=1, source_target_pairs={{0,4},{4,0},{8,12},{12,8},{16,20},{20,16},{24,28},{28,24},{1,5},{5... | collective-permute-start | bytes 1572872 | tf_op jit(solution)/shard_map/ppermute | solution.py:259
  16.0 8.0 %collective-permute-start.4 = (f32[16,2048]{1,0:T(8,128)S(1)}, f32[16,2048]{1,0:T(8,128)S(1)}, u32[]{:S(2)}, u32[]{:S(2)}) collective-permute-start(f32[16,2048]{1,0:T(8,128)S(1)} %get-tuple-element.41), channel_id=1, source_target_pairs={{0,16},{4,20},{8,24},{12,28},{16,0},{20,4},{24,8},{28,12},{1,17},{... | collective-permute-start | bytes 393224 | tf_op jit(solution)/shard_map/ppermute | solution.py:263
  17.6 7.9 %collective-permute-start.5 = (f32[16,2048]{1,0:T(8,128)S(1)}, f32[16,2048]{1,0:T(8,128)S(1)}, u32[]{:S(2)}, u32[]{:S(2)}) collective-permute-start(f32[16,2048]{1,0:T(8,128)S(1)} %get-tuple-element.42), channel_id=1, source_target_pairs={{0,24},{4,28},{8,16},{12,20},{16,8},{20,12},{24,0},{28,4},{1,25},{... | collective-permute-start | bytes 393224 | tf_op jit(solution)/shard_map/ppermute | solution.py:263
  19.0 6.6 %collective-permute-start.6 = (f32[16,2048]{1,0:T(8,128)S(1)}, f32[16,2048]{1,0:T(8,128)S(1)}, u32[]{:S(2)}, u32[]{:S(2)}) collective-permute-start(f32[16,2048]{1,0:T(8,128)S(1)} %get-tuple-element.43), channel_id=1, source_target_pairs={{0,8},{4,12},{8,0},{12,4},{16,24},{20,28},{24,16},{28,20},{1,9},{5... | collective-permute-start | bytes 393224 | tf_op jit(solution)/shard_map/ppermute | solution.py:263
  20.0 8.7 %collective-permute-start.7 = (f32[264,128]{1,0:T(8,128)S(1)}, f32[264,128]{1,0:T(8,128)S(1)}, u32[]{:S(2)}, u32[]{:S(2)}) collective-permute-start(f32[264,128]{1,0:T(8,128)S(1)} %get-tuple-element.52), channel_id=1, source_target_pairs={{0,1},{1,0},{2,3},{3,2},{4,5},{5,4},{6,7},{7,6},{8,9},{9,8},{10,11... | collective-permute-start | bytes 405512 | tf_op jit(solution)/shard_map/ppermute | solution.py:277
  20.1 12.9 %collective-permute-start.8 = (f32[264,128]{1,0:T(8,128)S(1)}, f32[264,128]{1,0:T(8,128)S(1)}, u32[]{:S(2)}, u32[]{:S(2)}) collective-permute-start(f32[264,128]{1,0:T(8,128)S(1)} %get-tuple-element.53), channel_id=1, source_target_pairs={{0,2},{1,3},{2,0},{3,1},{4,6},{5,7},{6,4},{7,5},{8,10},{9,11},{10,... | collective-permute-start | bytes 405512 | tf_op jit(solution)/shard_map/ppermute | solution.py:277
  23.9 9.1 %collective-permute-start.9 = (f32[264,128]{1,0:T(8,128)S(1)}, f32[264,128]{1,0:T(8,128)S(1)}, u32[]{:S(2)}, u32[]{:S(2)}) collective-permute-start(f32[264,128]{1,0:T(8,128)S(1)} %get-tuple-element.54), channel_id=1, source_target_pairs={{0,3},{1,2},{2,1},{3,0},{4,7},{5,6},{6,5},{7,4},{8,11},{9,10},{10,... | collective-permute-start | bytes 405512 | tf_op jit(solution)/shard_map/ppermute | solution.py:277
  25.7 7.3 %collective-permute-start.10 = (f32[16,2048]{1,0:T(8,128)S(1)}, f32[16,2048]{1,0:T(8,128)S(1)}, u32[]{:S(2)}, u32[]{:S(2)}) collective-permute-start(f32[16,2048]{1,0:T(8,128)S(1)} %get-tuple-element.63), channel_id=1, source_target_pairs={{0,16},{4,20},{8,24},{12,28},{16,0},{20,4},{24,8},{28,12},{1,17},{... | collective-permute-start | bytes 393224 | tf_op jit(solution)/shard_map/ppermute | solution.py:263
  27.6 6.2 %collective-permute-start.11 = (f32[16,2048]{1,0:T(8,128)S(1)}, f32[16,2048]{1,0:T(8,128)S(1)}, u32[]{:S(2)}, u32[]{:S(2)}) collective-permute-start(f32[16,2048]{1,0:T(8,128)S(1)} %get-tuple-element.63), channel_id=1, source_target_pairs={{0,24},{4,28},{8,16},{12,20},{16,8},{20,12},{24,0},{28,4},{1,25},{... | collective-permute-start | bytes 393224 | tf_op jit(solution)/shard_map/ppermute | solution.py:263
  28.7 5.5 %collective-permute-start.12 = (f32[16,2048]{1,0:T(8,128)S(1)}, f32[16,2048]{1,0:T(8,128)S(1)}, u32[]{:S(2)}, u32[]{:S(2)}) collective-permute-start(f32[16,2048]{1,0:T(8,128)S(1)} %get-tuple-element.63), channel_id=1, source_target_pairs={{0,8},{4,12},{8,0},{12,4},{16,24},{20,28},{24,16},{28,20},{1,9},{5... | collective-permute-start | bytes 393224 | tf_op jit(solution)/shard_map/ppermute | solution.py:263
  34.3 2.0 %collective-permute-start.13 = (f32[64,2048]{1,0:T(8,128)S(1)}, f32[64,2048]{1,0:T(8,128)S(1)}, u32[]{:S(2)}, u32[]{:S(2)}) collective-permute-start(f32[64,2048]{1,0:T(8,128)S(1)} %constant_dynamic-update-slice_fusion.refs_4_), channel_id=1, source_target_pairs={{0,4},{4,0},{8,12},{12,8},{16,20},{20,16},{24,28},{28,24},{1,5},{5... | collective-permute-start | bytes 1572872 | tf_op jit(solution)/shard_map/ppermute | solution.py:289

commit v6 on v5

--- a/solution.py
+++ b/solution.py
@@ -15,7 +15,7 @@
 SMEM = pl.BlockSpec(memory_space=pltpu.SMEM)
 HBM = pl.BlockSpec(memory_space=pltpu.HBM)
 ANY = pl.BlockSpec(memory_space=pl.ANY)
-CHUNK = 256
+CHUNK = 512
 F32, BF16, I32 = jnp.float32, jnp.bfloat16, jnp.int32
 
 
@@ -26,7 +26,7 @@
 
 
 def rounds(n):
-    return pairings(n)[::-1]
+    return pairings(n)
 
 
 def peer_to(me, s, n):
@@ -64,16 +64,22 @@
 def first_kernel(delta_hbm, w_hbm, pooled_hbm, slots_hbm, *refs):
     xgrad_ref, delta_ref, pooled_ref, slots_ref, partial_ref, w_ref, sems = refs
     examples, emb = pooled_ref.shape
-    hid = delta_ref.shape[1]
     looks = slots_ref.shape[0]
     blocks = list(range(0, examples, CHUNK))
     pairs = [(w_hbm, w_ref)]
     pairs += [(delta_hbm.at[pl.ds(r, CHUNK)], delta_ref.at[pl.ds(r, CHUNK)]) for r in blocks]
     pairs += [(slots_hbm, slots_ref), (pooled_hbm, pooled_ref)]
     copies = [pltpu.make_async_copy(a, b, sems.at[i]) for i, (a, b) in enumerate(pairs)]
-    for copy in copies:
+    for copy in copies[-2:] + copies[:-2]:
         copy.start()
     n = len(blocks)
+    for copy in copies[1 + n:]:
+        copy.wait()
+    slots = slots_ref[...]
+    same = jnp.full(slots.shape, 1.0, F32)
+    for shift in range(1, looks):
+        same = same + jnp.where(slots == pltpu.roll(slots, shift, 0), 1.0, 0.0)
+    repeats = jnp.sum(same, axis=0, keepdims=True)
     copies[0].wait()
     norms = []
     for i, r in enumerate(blocks):
@@ -83,32 +89,23 @@
             preferred_element_type=F32,
         )
         xgrad_ref[:, r:r + CHUNK] = xgrad
-        sums = []
-        for q in range(r, r + CHUNK, 128):
-            total = jnp.zeros((128, 128), F32)
-            for c in range(0, hid, 128):
-                piece = delta_ref[q:q + 128, c:c + 128].astype(F32)
-                total = total + piece * piece
-            sums.append(jnp.sum(total.T, axis=0, keepdims=True))
-        norms.append((jnp.sum(xgrad * xgrad, axis=0, keepdims=True), jnp.concatenate(sums, axis=1)))
-    for copy in copies[1 + n:]:
-        copy.wait()
-    slots = slots_ref[...]
-    same = jnp.full(slots.shape, 1.0, F32)
-    for shift in range(1, looks):
-        same = same + jnp.where(slots == pltpu.roll(slots, shift, 0), 1.0, 0.0)
-    repeats = jnp.sum(same, axis=0, keepdims=True)
+        norms.append(jnp.sum(xgrad * xgrad, axis=0, keepdims=True))
     for i, r in enumerate(blocks):
-        xgrad_sq, delta_sq = norms[i]
         sums = []
         for q in range(r, r + CHUNK, 128):
             piece = pooled_ref[q:q + 128, :].astype(F32)
             sums.append(jnp.sum((piece * piece).T, axis=0, keepdims=True))
-        partial = delta_sq * jnp.concatenate(sums, axis=1) + repeats[:, r:r + CHUNK] * xgrad_sq
-        partial_ref[:, r:r + CHUNK] = partial
-
-
-def named_kernel(owners, counts_ref, slots_ref, pooled_ref, ids_ref, named_ref, turned_ref, targets_ref):
+        partial_ref[0:1, r:r + CHUNK] = jnp.concatenate(sums, axis=1)
+        partial_ref[1:2, r:r + CHUNK] = repeats[:, r:r + CHUNK] * norms[i]
+
+
+def named_kernel(owners, counts_ref, slots_ref, pooled_ref, ids_ref, delta_ref, named_ref, turned_ref, targets_ref, delta_sq_ref):
+    for r in range(0, delta_ref.shape[0], 128):
+        total = jnp.zeros((128, 128), F32)
+        for c in range(0, delta_ref.shape[1], 128):
+            piece = delta_ref[r:r + 128, c:c + 128].astype(F32)
+            total = total + piece * piece
+        delta_sq_ref[:, r:r + 128] = jnp.sum(total.T, axis=0, keepdims=True)
     turned_ref[...] = pooled_ref[...].astype(F32).T
     width = named_ref.shape[0]
     ids = jnp.broadcast_to(ids_ref[...], (8, width))
@@ -137,12 +134,13 @@
 
 
 def clip_kernel(*refs):
-    *messages, turned_ref, delta_ref, _, clip_ref, scaled_ref, theirs_ref, wide_ref = refs
+    *messages, turned_ref, delta_sq_ref, delta_ref, _, clip_ref, scaled_ref, theirs_ref, wide_ref = refs
     half = theirs_ref.shape[0]
     core = lax.rem(lax.axis_index("dp"), 2)
-    norm_sq = messages[0][...]
+    total = messages[0][...]
     for message in messages[1:]:
-        norm_sq = norm_sq + message[...]
+        total = total + message[...]
+    norm_sq = delta_sq_ref[...] * total[0:1, :] + total[1:2, :]
     clip = jnp.minimum(1.0, CLIP_NORM / jnp.sqrt(norm_sq + EPSILON))
     clip_ref[...] = clip
     wide_ref[...] = turned_ref[...] * clip
@@ -181,15 +179,28 @@
             out_refs[s][cap + q:cap + q + 1, :] = targets_ref[s, :, q * emb:(q + 1) * emb]
 
 
-def place_kernel(owners, cap, *refs):
+def place_of(hop, flip, rows, part):
+    me = lax.axis_index("dp")
+    chip, core = me // 2, lax.rem(me, 2)
+    core = 1 - core if flip else core
+    return pl.ds(core * (rows // 2) + ((chip ^ hop) * part if 2 * part < rows else 0), part)
+
+
+def place_kernel(owners, cap, order, *refs):
     pieces = refs[:owners]
-    own_ref, table_ref, dense_ref, rows_ref, sems = refs[owners:]
+    own, ends = refs[owners:owners + len(order)], refs[owners + len(order):-4]
+    table_ref, dense_ref, rows_ref, sems = refs[-4:]
     emb = pieces[0].shape[1]
-    half = own_ref.shape[0]
-    me, core = lax.axis_index("mp"), lax.rem(lax.axis_index("dp"), 2)
-    copy = pltpu.make_async_copy(own_ref, dense_ref.at[pl.ds(core * half, half)], sems.at[owners])
-    copy.start()
-    copies = [copy]
+    part = own[0].shape[0]
+    me = lax.axis_index("mp")
+    places = [(own[i], hop, 0) for i, hop in enumerate(order)]
+    for end in ends:
+        places += [(end.at[pl.ds(i * part, part)], hop, 1) for i, hop in enumerate(order[:len(order) // 2])]
+    copies = []
+    for i, (piece, hop, flip) in enumerate(places):
+        rows = place_of(hop, flip, dense_ref.shape[0], part)
+        copies.append(pltpu.make_async_copy(piece, dense_ref.at[rows], sems.at[owners + i]))
+        copies[-1].start()
     row = lax.broadcasted_iota(I32, (ROWS_DEV, cap), 0).astype(F32)
     for s in range(owners):
         ids = [pieces[s][cap + q:cap + q + 1, :] for q in range(cap // emb)]
@@ -209,12 +220,15 @@
         copy.wait()
 
 
-def finish_kernel(_, other_ref, dense_ref, sem):
-    half = other_ref.shape[0]
-    core = lax.rem(lax.axis_index("dp"), 2)
-    copy = pltpu.make_async_copy(other_ref, dense_ref.at[pl.ds((1 - core) * half, half)], sem)
-    copy.start()
-    copy.wait()
+def finish_kernel(order, _, end_ref, dense_ref, sems):
+    part = end_ref.shape[0] // len(order)
+    copies = []
+    for i, hop in enumerate(order):
+        rows = place_of(hop, 1, dense_ref.shape[0], part)
+        copies.append(pltpu.make_async_copy(end_ref.at[pl.ds(i * part, part)], dense_ref.at[rows], sems.at[i]))
+        copies[-1].start()
+    for copy in copies:
+        copy.wait()
 
 
 def on_device(pooled, delta, w_first, lookup_slot, row_ids, send_counts):
@@ -232,29 +246,29 @@
     xgrad, delta, pooled, slots, partial = call(
         first_kernel,
         [((emb, examples), F32), (delta.shape, BF16), (pooled.shape, BF16), (slots.shape, I32)]
-        + [((1, examples), F32)],
+        + [((2, examples), F32)],
         2 * emb * examples * hid,
         *[pltpu.with_memory_space_constraint(a, pltpu.HBM) for a in (delta, w_first, pooled, slots)],
         specs=[HBM] * 4,
         scratch=[pltpu.VMEM(w_first.shape, BF16), pltpu.SemaphoreType.DMA((3 + examples // CHUNK,))],
     )
     norms = [lax.ppermute(partial, "mp", r) for r in rounds(owners)]
-    named, turned, targets = call(
+    named, turned, targets, delta_sq = call(
         functools.partial(named_kernel, owners),
-        [((width, examples), BF16), ((emb, examples), F32), ((owners, 1, cap), F32)],
-        8 * width * examples * looks, counts, slots, pooled, ids, specs=[SMEM, VMEM, VMEM, VMEM],
+        [((width, examples), BF16), ((emb, examples), F32), ((owners, 1, cap), F32)]
+        + [((1, examples), F32)],
+        8 * width * examples * looks, counts, slots, pooled, ids, delta,
+        specs=[SMEM, VMEM, VMEM, VMEM, VMEM],
     )
     clip, scaled, theirs = call(
         clip_kernel,
         [((1, examples), F32), ((half, examples), BF16), ((half, hid), F32)],
         2 * half * examples * hid,
-        *norms, partial, turned, delta, named,
-        specs=[VMEM] * (len(norms) + 3) + [ANY],
+        *norms, partial, turned, delta_sq, delta, named,
+        specs=[VMEM] * (len(norms) + 4) + [ANY],
         scratch=[pltpu.VMEM((emb, examples), F32)],
     )
     steps = pairings(owners)
-    me = lax.axis_index("dp")
-    chip = me >> 1
     swap = [(i, i ^ 1) for i in range(n_dp)]
     came = lax.ppermute(theirs, "dp", swap)
     (mine,) = call(mine_kernel, [((half, hid), F32)], 2 * half * examples * hid, scaled, delta)
@@ -279,23 +293,28 @@
         got = [chips(piece, s) for piece, s in zip(parts[1:], hops[1:])]
         got, unique[0] = lax.optimization_barrier((got, unique[0]))
         total = parts[0] + got[0] + got[1] + got[2]
-        own = lax.dynamic_update_slice_in_dim(jnp.zeros((half, hid), F32), total, chip * part, 0)
-        own, *unique = lax.optimization_barrier((own, *unique))
-        for s in hops[1:]:
-            own = lax.dynamic_update_slice_in_dim(own, chips(total, s), (chip ^ s) * part, 0)
+        order = (0, 3, 2, 1)
+        own = [total] + [chips(total, s) for s in order[1:]]
+        own[0], *unique = lax.optimization_barrier((own[0], *unique))
+        near = jnp.concatenate(own[:2])
+        ends = [lax.ppermute(half_of, "dp", swap) for half_of in (near, jnp.concatenate(own[2:]))]
     else:
         groups = [list(range(c, n_dp, 2)) for c in (0, 1)]
-        own = lax.psum(parts[0], "dp", axis_index_groups=groups)
-    other = lax.ppermute(own, "dp", swap)
+        order = (0,)
+        own = [lax.psum(parts[0], "dp", axis_index_groups=groups)]
+        ends = [lax.ppermute(own[0], "dp", swap)]
+    writes = len(own) + len(own) // 2
     table_grad, dense_grad = call(
-        functools.partial(place_kernel, owners, cap),
+        functools.partial(place_kernel, owners, cap, order),
         [((owners, ROWS_DEV, emb), F32), ((emb, hid), F32)],
-        4 * owners * ROWS_DEV * cap * emb, *unique, own, out_specs=[HBM, HBM],
-        scratch=[pltpu.VMEM((owners, ROWS_DEV, emb), F32), pltpu.SemaphoreType.DMA((owners + 1,))],
-    )
+        4 * owners * ROWS_DEV * cap * emb, *unique, *own, *ends[:-1], out_specs=[HBM, HBM],
+        scratch=[pltpu.VMEM((owners, ROWS_DEV, emb), F32), pltpu.SemaphoreType.DMA((owners + writes,))],
+    )
+    rest = order[len(order) // 2:]
     (dense_grad,) = call(
-        finish_kernel, [((emb, hid), F32)], 0, dense_grad, other, specs=[HBM, VMEM],
-        out_specs=[HBM], scratch=[pltpu.SemaphoreType.DMA(())], aliases={0: 0},
+        functools.partial(finish_kernel, rest), [((emb, hid), F32)], 0, dense_grad, ends[-1],
+        specs=[HBM, VMEM], out_specs=[HBM], scratch=[pltpu.SemaphoreType.DMA((len(rest),))],
+        aliases={0: 0},
     )
     return (dense_grad, table_grad[None])
 

time: 37.2 us -> 36.6 us (0.984)
  waiting for transfers between devices: 11 us -> 9.69 us
  starting transfers between devices: 16.7 us -> 17.5 us
    ppermute x3, starting transfers between devices: 3.74 us -> 4.4 us  [on_device(): unique[s] = lax.ppermute(unique[s], 'mp', steps[s - 1])]
    ppermute x1 -> x2, waiting for transfers between devices: 0.57 us -> 0.16 us  [on_device(): lax.ppermute(half_of, 'dp', swap)]
  transfers between devices with their start and end apart: 14 -> 15, of which waited for: 8 -> 7; matrix products, arithmetic and copies ran while one was open for 0% -> 0% of each run, Pallas kernels for 10% -> 12%
where the time goes in v6:
time: 36.6 us; the launch traced here: 36.4 us
  starting transfers between devices  17.5 us (48%)
  waiting for transfers between devices  9.69 us (26%)
  Pallas kernels  8.34 us (23%)
  between operations  0.76 us (2%)
    pallas_call x8, Pallas kernels, call(): pl.pallas_call(kernel, out_shape=[jax.ShapeDtypeStruct(shape, dtype) for...  8.34 us
    ppermute x6, starting transfers between devices, chips(): return lax.ppermute(piece, 'dp', [(i, i ^ 2 * s) for i in range(n_dp)])  7.16 us
    ppermute x3, starting transfers between devices, on_device(): norms = [lax.ppermute(partial, 'mp', r) for r in rounds(owners)]  5.75 us
    ppermute x3, starting transfers between devices, on_device(): unique[s] = lax.ppermute(unique[s], 'mp', steps[s - 1])  4.4 us
    ppermute x3, waiting for transfers between devices, on_device(): unique[s] = lax.ppermute(unique[s], 'mp', steps[s - 1])  3.55 us
    ppermute x6, waiting for transfers between devices, chips(): return lax.ppermute(piece, 'dp', [(i, i ^ 2 * s) for i in range(n_dp)])  2.68 us
    ppermute x3, waiting for transfers between devices, on_device(): norms = [lax.ppermute(partial, 'mp', r) for r in rounds(owners)]  1.88 us
    ppermute x1, waiting for transfers between devices, on_device(): came = lax.ppermute(theirs, 'dp', swap)  1.42 us
  transfers between devices with their start and end apart: 15, of which 7 were waited for; matrix products, arithmetic and copies ran while one was open for 0% of the time, Pallas kernels for 12%

profile of v6, /device:TPU:0, one launch (start us, length us, event | category | flops | bytes accessed | tf_op | source)
XLA Modules:
  0.0 36.4 jit_solution(8487775752504740446)
XLA Ops:
  0.6 0.0 copy-start.1
  0.6 0.0 copy-start
  0.7 2.7 %shard_map.77 = (f32[128,512]{1,0:T(8,128)S(1)}, bf16[512,2048]{1,0:T(8,128)(2,1)S(1)}, bf16[512,128]{1,0:T(8,128)(2,1)S(1)}, s32[8,512]{1,0:T(8,128)S(1)}, f32[2,512]{1,0:T(2,128)S(1)}) custom-call(bf16[512,2048]{1,0:T(8,128)(2,1)} %delta_hbm.1, bf16[128,2048]{1,0:T(8,128)(2,1)} %w_hbm.1, bf16[512,128]{1,0:T(8,128)(2,1)} %pooled_hbm.1, s32[8,512]{1,0:T(8,128)} %bitcast.8), custom_call_target="tpu_custom_call" | custom-call | flops 268435456 | bytes 2768896 | tf_op jit(solution)/shard_map/pallas_call | solution.py:42
  3.4 5.1 %collective-permute-start.2 = (f32[2,512]{1,0:T(2,128)S(1)}, f32[2,512]{1,0:T(2,128)S(1)}, u32[]{:S(2)}, u32[]{:S(2)}) collective-permute-start(f32[2,512]{1,0:T(2,128)S(1)} %get-tuple-element.33.refs_3_), channel_id=1, source_target_pairs={{0,3},{1,2},{2,1},{3,0},{4,7},{5,6},{6,5},{7,4},{8,11},{9,10},{10,... | collective-permute-start | bytes 12296 | tf_op jit(solution)/shard_map/ppermute | solution.py:255
  8.5 0.0 collective-permute-start.1
  8.5 0.6 %collective-permute-start = (f32[2,512]{1,0:T(2,128)S(1)}, f32[2,512]{1,0:T(2,128)S(1)}, u32[]{:S(2)}, u32[]{:S(2)}) collective-permute-start(f32[2,512]{1,0:T(2,128)S(1)} %get-tuple-element.33.refs_3_), channel_id=1, source_target_pairs={{0,1},{1,0},{2,3},{3,2},{4,5},{5,4},{6,7},{7,6},{8,9},{9,8},{10,11... | collective-permute-start | bytes 12296 | tf_op jit(solution)/shard_map/ppermute | solution.py:255
  9.1 0.0 copy-done.1
  9.1 0.0 copy-done
  9.2 2.0 %shard_map.78 = (bf16[1024,512]{1,0:T(8,128)(2,1)S(1)}, f32[128,512]{1,0:T(8,128)S(1)}, f32[4,1,256]{2,1,0:T(1,128)S(1)}, f32[1,512]{1,0:T(1,128)S(1)}) custom-call(s32[1,4]{1,0:T(1,128)S(1)} %bitcast.7, s32[8,512]{1,0:T(8,128)S(1)} %get-tuple-element.34.slots_ref, bf16[512,128]{1,0:T(8,128)(2,1)S(1)} %get-tuple-element.35.pooled_ref, ...), custom_call_target="tpu_custom_call" | custom-call | flops 33554432 | bytes 2248720 | tf_op jit(solution)/shard_map/pallas_call | solution.py:42
  11.1 0.0 collective-permute-done.2.refs_2_
  11.1 1.9 %collective-permute-done.1.refs_1_ = f32[2,512]{1,0:T(2,128)S(1)} collective-permute-done((f32[2,512]{1,0:T(2,128)S(1)}, f32[2,512]{1,0:T(2,128)S(1)}, u32[]{:S(2)}, u32[]{:S(2)}) %collective-permute-start.1) | collective-permute-done | bytes 4128 | tf_op jit(solution)/shard_map/ppermute | solution.py:255
  13.0 0.0 collective-permute-done.refs_0_
  13.0 0.5 %shard_map.79 = (f32[1,512]{1,0:T(1,128)S(1)}, bf16[64,512]{1,0:T(8,128)(2,1)S(1)}, f32[64,2048]{1,0:T(8,128)S(1)}) custom-call(f32[2,512]{1,0:T(2,128)S(1)} %collective-permute-done.refs_0_, f32[2,512]{1,0:T(2,128)S(1)} %collective-permute-done.1.refs_1_, f32[2,512]{1,0:T(2,128)S(1)} %collective-permute-done.2.refs_2_, ...), custom_call_target="tpu_custom_call" | custom-call | flops 134217728 | bytes 3426304 | tf_op jit(solution)/shard_map/pallas_call | solution.py:42
  13.5 0.1 collective-permute-start.3
  13.6 0.5 %shard_map.80.mine_ref = f32[64,2048]{1,0:T(8,128)S(1)} custom-call(bf16[64,512]{1,0:T(8,128)(2,1)S(1)} %get-tuple-element.40.scaled_ref, bf16[512,2048]{1,0:T(8,128)(2,1)S(1)} %get-tuple-element.36.delta_ref.refs_6_), custom_call_target="tpu_custom_call" | custom-call | flops 134217728 | bytes 2162688 | tf_op jit(solution)/shard_map/pallas_call | solution.py:42
  14.1 1.4 %collective-permute-done.3.came_ref = f32[64,2048]{1,0:T(8,128)S(1)} collective-permute-done((f32[64,2048]{1,0:T(8,128)S(1)}, f32[64,2048]{1,0:T(8,128)S(1)}, u32[]{:S(2)}, u32[]{:S(2)}) %collective-permute-start.3) | collective-permute-done | bytes 524320 | tf_op jit(solution)/shard_map/ppermute | solution.py:273
  15.5 0.1 shard_map.81
  15.6 1.6 %collective-permute-start.4 = (f32[16,2048]{1,0:T(8,128)S(1)}, f32[16,2048]{1,0:T(8,128)S(1)}, u32[]{:S(2)}, u32[]{:S(2)}) collective-permute-start(f32[16,2048]{1,0:T(8,128)S(1)} %get-tuple-element.43), channel_id=1, source_target_pairs={{0,16},{4,20},{8,24},{12,28},{16,0},{20,4},{24,8},{28,12},{1,17},{... | collective-permute-start | bytes 393224 | tf_op jit(solution)/shard_map/ppermute | solution.py:277
  17.1 1.4 %collective-permute-start.5 = (f32[16,2048]{1,0:T(8,128)S(1)}, f32[16,2048]{1,0:T(8,128)S(1)}, u32[]{:S(2)}, u32[]{:S(2)}) collective-permute-start(f32[16,2048]{1,0:T(8,128)S(1)} %get-tuple-element.44), channel_id=1, source_target_pairs={{0,24},{4,28},{8,16},{12,20},{16,8},{20,12},{24,0},{28,4},{1,25},{... | collective-permute-start | bytes 393224 | tf_op jit(solution)/shard_map/ppermute | solution.py:277
  18.6 0.5 %collective-permute-start.6 = (f32[16,2048]{1,0:T(8,128)S(1)}, f32[16,2048]{1,0:T(8,128)S(1)}, u32[]{:S(2)}, u32[]{:S(2)}) collective-permute-start(f32[16,2048]{1,0:T(8,128)S(1)} %get-tuple-element.45), channel_id=1, source_target_pairs={{0,8},{4,12},{8,0},{12,4},{16,24},{20,28},{24,16},{28,20},{1,9},{5... | collective-permute-start | bytes 393224 | tf_op jit(solution)/shard_map/ppermute | solution.py:277
  19.1 0.5 %shard_map.82 = (f32[264,128]{1,0:T(8,128)S(1)}, f32[264,128]{1,0:T(8,128)S(1)}, f32[264,128]{1,0:T(8,128)S(1)}, f32[264,128]{1,0:T(8,128)S(1)}) custom-call(bf16[1024,512]{1,0:T(8,128)(2,1)S(1)} %get-tuple-element.39.refs_7_.named_ref, f32[128,512]{1,0:T(8,128)S(1)} %get-tuple-element.46.xgrad_ref, f32[1,512]{1,0:T(1,128)S(1)} %get-tuple-element.47.clip_ref, ...), custom_call_target="tpu_custom_call" | custom-call | flops 268435456 | bytes 1447936 | tf_op jit(solution)/shard_map/pallas_call | solution.py:42
  19.6 0.1 collective-permute-start.7
  19.7 2.4 %collective-permute-start.8 = (f32[264,128]{1,0:T(8,128)S(1)}, f32[264,128]{1,0:T(8,128)S(1)}, u32[]{:S(2)}, u32[]{:S(2)}) collective-permute-start(f32[264,128]{1,0:T(8,128)S(1)} %get-tuple-element.55), channel_id=1, source_target_pairs={{0,2},{1,3},{2,0},{3,1},{4,6},{5,7},{6,4},{7,5},{8,10},{9,11},{10,... | collective-permute-start | bytes 405512 | tf_op jit(solution)/shard_map/ppermute | solution.py:291
  22.1 1.4 %collective-permute-done.4 = f32[16,2048]{1,0:T(8,128)S(1)} collective-permute-done((f32[16,2048]{1,0:T(8,128)S(1)}, f32[16,2048]{1,0:T(8,128)S(1)}, u32[]{:S(2)}, u32[]{:S(2)}) %collective-permute-start.4) | collective-permute-done | bytes 131104 | tf_op jit(solution)/shard_map/ppermute | solution.py:277
  23.5 1.9 %collective-permute-start.9 = (f32[264,128]{1,0:T(8,128)S(1)}, f32[264,128]{1,0:T(8,128)S(1)}, u32[]{:S(2)}, u32[]{:S(2)}) collective-permute-start(f32[264,128]{1,0:T(8,128)S(1)} %get-tuple-element.56), channel_id=1, source_target_pairs={{0,3},{1,2},{2,1},{3,0},{4,7},{5,6},{6,5},{7,4},{8,11},{9,10},{10,... | collective-permute-start | bytes 405512 | tf_op jit(solution)/shard_map/ppermute | solution.py:291
  25.4 0.0 collective-permute-done.5
  25.4 0.0 collective-permute-done.6
  25.5 3.0 %collective-permute-start.10 = (f32[16,2048]{1,0:T(8,128)S(1)}, f32[16,2048]{1,0:T(8,128)S(1)}, u32[]{:S(2)}, u32[]{:S(2)}) collective-permute-start(f32[16,2048]{1,0:T(8,128)S(1)} %add_add_fusion.refs_4_), channel_id=1, source_target_pairs={{0,24},{4,28},{8,16},{12,20},{16,8},{20,12},{24,0},{28,4},{1,25},{... | collective-permute-start | bytes 393224 | tf_op jit(solution)/shard_map/ppermute | solution.py:277
  28.4 0.5 %collective-permute-start.12 = (f32[16,2048]{1,0:T(8,128)S(1)}, f32[16,2048]{1,0:T(8,128)S(1)}, u32[]{:S(2)}, u32[]{:S(2)}) collective-permute-start(f32[16,2048]{1,0:T(8,128)S(1)} %add_add_fusion.refs_4_), channel_id=1, source_target_pairs={{0,8},{4,12},{8,0},{12,4},{16,24},{20,28},{24,16},{28,20},{1,9},{5... | collective-permute-start | bytes 393224 | tf_op jit(solution)/shard_map/ppermute | solution.py:277
  29.0 0.0 collective-permute-done.7.refs_1_
  29.0 0.1 collective-permute-start.11
  29.1 3.5 %collective-permute-done.8.refs_2_ = f32[264,128]{1,0:T(8,128)S(1)} collective-permute-done((f32[264,128]{1,0:T(8,128)S(1)}, f32[264,128]{1,0:T(8,128)S(1)}, u32[]{:S(2)}, u32[]{:S(2)}) %collective-permute-start.8) | collective-permute-done | bytes 135200 | tf_op jit(solution)/shard_map/ppermute | solution.py:291
  32.6 0.0 collective-permute-done.9.refs_3_
  32.6 0.0 collective-permute-done.10.refs_5_
  32.6 0.1 collective-permute-start.13
  32.7 1.2 %collective-permute-done.12.refs_7_ = f32[16,2048]{1,0:T(8,128)S(1)} collective-permute-done((f32[16,2048]{1,0:T(8,128)S(1)}, f32[16,2048]{1,0:T(8,128)S(1)}, u32[]{:S(2)}, u32[]{:S(2)}) %collective-permute-start.12) | collective-permute-done | bytes 131104 | tf_op jit(solution)/shard_map/ppermute | solution.py:277
  33.9 0.1 collective-permute-done.11.refs_6_
  34.0 0.1 collective-permute-start.14
  34.1 0.2 collective-permute-done.13.refs_8_
  34.2 1.4 %shard_map.83 = (f32[4,512,128]{2,1,0:T(8,128)}, f32[128,2048]{1,0:T(8,128)}) custom-call(f32[264,128]{1,0:T(8,128)S(1)} %get-tuple-element.57.refs_0_, f32[264,128]{1,0:T(8,128)S(1)} %collective-permute-done.7.refs_1_, f32[264,128]{1,0:T(8,128)S(1)} %collective-permute-done.8.refs_2_, f32[264,128]{1,0:T(8,128)S(1)} %collective-permute-done.9.refs_3_, ...), custom_call_target="tpu_custom_call" | custom-call | flops 268435456 | bytes 1327104 | tf_op jit(solution)/shard_map/pallas_call | solution.py:42
  35.7 0.0 collective-permute-done.14.end_ref
  35.7 0.7 %shard_map.84 = f32[128,2048]{1,0:T(8,128)} custom-call(f32[128,2048]{1,0:T(8,128)} %get-tuple-element.62._, f32[32,2048]{1,0:T(8,128)S(1)} %collective-permute-done.14.end_ref), custom_call_target="tpu_custom_call", output_to_operand_aliasing={{}: (0, {})} | custom-call | bytes 1310720 | tf_op jit(solution)/shard_map/pallas_call | solution.py:42
  (3 shorter events, 0.1 us)
Async XLA Ops:
  0.6 8.5 %copy-start.1 = (s32[1,1,4]{2,1,0:T(1,128)S(1)}, s32[1,1,4]{2,1,0:T(1,128)}, u32[]{:S(2)}) copy-start(s32[1,1,4]{2,1,0:T(1,128)} %param.11) | copy-start | bytes 52
  0.6 8.5 %copy-start = (s32[1,1,1024]{2,1,0:T(1,128)S(1)}, s32[1,1,1024]{2,1,0:T(1,128)}, u32[]{:S(2)}) copy-start(s32[1,1,1024]{2,1,0:T(1,128)} %param.10) | copy-start | bytes 12292
  3.4 7.7 %collective-permute-start.2 = (f32[2,512]{1,0:T(2,128)S(1)}, f32[2,512]{1,0:T(2,128)S(1)}, u32[]{:S(2)}, u32[]{:S(2)}) collective-permute-start(f32[2,512]{1,0:T(2,128)S(1)} %get-tuple-element.33.refs_3_), channel_id=1, source_target_pairs={{0,3},{1,2},{2,1},{3,0},{4,7},{5,6},{6,5},{7,4},{8,11},{9,10},{10,... | collective-permute-start | bytes 12296 | tf_op jit(solution)/shard_map/ppermute | solution.py:255
  8.5 4.5 %collective-permute-start.1 = (f32[2,512]{1,0:T(2,128)S(1)}, f32[2,512]{1,0:T(2,128)S(1)}, u32[]{:S(2)}, u32[]{:S(2)}) collective-permute-start(f32[2,512]{1,0:T(2,128)S(1)} %get-tuple-element.33.refs_3_), channel_id=1, source_target_pairs={{0,2},{1,3},{2,0},{3,1},{4,6},{5,7},{6,4},{7,5},{8,10},{9,11},{10,... | collective-permute-start | bytes 12296 | tf_op jit(solution)/shard_map/ppermute | solution.py:255
  8.5 4.5 %collective-permute-start = (f32[2,512]{1,0:T(2,128)S(1)}, f32[2,512]{1,0:T(2,128)S(1)}, u32[]{:S(2)}, u32[]{:S(2)}) collective-permute-start(f32[2,512]{1,0:T(2,128)S(1)} %get-tuple-element.33.refs_3_), channel_id=1, source_target_pairs={{0,1},{1,0},{2,3},{3,2},{4,5},{5,4},{6,7},{7,6},{8,9},{9,8},{10,11... | collective-permute-start | bytes 12296 | tf_op jit(solution)/shard_map/ppermute | solution.py:255
  13.5 2.0 %collective-permute-start.3 = (f32[64,2048]{1,0:T(8,128)S(1)}, f32[64,2048]{1,0:T(8,128)S(1)}, u32[]{:S(2)}, u32[]{:S(2)}) collective-permute-start(f32[64,2048]{1,0:T(8,128)S(1)} %get-tuple-element.41), channel_id=1, source_target_pairs={{0,4},{4,0},{8,12},{12,8},{16,20},{20,16},{24,28},{28,24},{1,5},{5... | collective-permute-start | bytes 1572872 | tf_op jit(solution)/shard_map/ppermute | solution.py:273
  15.6 8.0 %collective-permute-start.4 = (f32[16,2048]{1,0:T(8,128)S(1)}, f32[16,2048]{1,0:T(8,128)S(1)}, u32[]{:S(2)}, u32[]{:S(2)}) collective-permute-start(f32[16,2048]{1,0:T(8,128)S(1)} %get-tuple-element.43), channel_id=1, source_target_pairs={{0,16},{4,20},{8,24},{12,28},{16,0},{20,4},{24,8},{28,12},{1,17},{... | collective-permute-start | bytes 393224 | tf_op jit(solution)/shard_map/ppermute | solution.py:277
  17.1 8.3 %collective-permute-start.5 = (f32[16,2048]{1,0:T(8,128)S(1)}, f32[16,2048]{1,0:T(8,128)S(1)}, u32[]{:S(2)}, u32[]{:S(2)}) collective-permute-start(f32[16,2048]{1,0:T(8,128)S(1)} %get-tuple-element.44), channel_id=1, source_target_pairs={{0,24},{4,28},{8,16},{12,20},{16,8},{20,12},{24,0},{28,4},{1,25},{... | collective-permute-start | bytes 393224 | tf_op jit(solution)/shard_map/ppermute | solution.py:277
  18.6 6.8 %collective-permute-start.6 = (f32[16,2048]{1,0:T(8,128)S(1)}, f32[16,2048]{1,0:T(8,128)S(1)}, u32[]{:S(2)}, u32[]{:S(2)}) collective-permute-start(f32[16,2048]{1,0:T(8,128)S(1)} %get-tuple-element.45), channel_id=1, source_target_pairs={{0,8},{4,12},{8,0},{12,4},{16,24},{20,28},{24,16},{28,20},{1,9},{5... | collective-permute-start | bytes 393224 | tf_op jit(solution)/shard_map/ppermute | solution.py:277
  19.6 9.4 %collective-permute-start.7 = (f32[264,128]{1,0:T(8,128)S(1)}, f32[264,128]{1,0:T(8,128)S(1)}, u32[]{:S(2)}, u32[]{:S(2)}) collective-permute-start(f32[264,128]{1,0:T(8,128)S(1)} %get-tuple-element.54), channel_id=1, source_target_pairs={{0,1},{1,0},{2,3},{3,2},{4,5},{5,4},{6,7},{7,6},{8,9},{9,8},{10,11... | collective-permute-start | bytes 405512 | tf_op jit(solution)/shard_map/ppermute | solution.py:291
  19.7 12.9 %collective-permute-start.8 = (f32[264,128]{1,0:T(8,128)S(1)}, f32[264,128]{1,0:T(8,128)S(1)}, u32[]{:S(2)}, u32[]{:S(2)}) collective-permute-start(f32[264,128]{1,0:T(8,128)S(1)} %get-tuple-element.55), channel_id=1, source_target_pairs={{0,2},{1,3},{2,0},{3,1},{4,6},{5,7},{6,4},{7,5},{8,10},{9,11},{10,... | collective-permute-start | bytes 405512 | tf_op jit(solution)/shard_map/ppermute | solution.py:291
  23.5 9.1 %collective-permute-start.9 = (f32[264,128]{1,0:T(8,128)S(1)}, f32[264,128]{1,0:T(8,128)S(1)}, u32[]{:S(2)}, u32[]{:S(2)}) collective-permute-start(f32[264,128]{1,0:T(8,128)S(1)} %get-tuple-element.56), channel_id=1, source_target_pairs={{0,3},{1,2},{2,1},{3,0},{4,7},{5,6},{6,5},{7,4},{8,11},{9,10},{10,... | collective-permute-start | bytes 405512 | tf_op jit(solution)/shard_map/ppermute | solution.py:291
  25.5 7.2 %collective-permute-start.10 = (f32[16,2048]{1,0:T(8,128)S(1)}, f32[16,2048]{1,0:T(8,128)S(1)}, u32[]{:S(2)}, u32[]{:S(2)}) collective-permute-start(f32[16,2048]{1,0:T(8,128)S(1)} %add_add_fusion.refs_4_), channel_id=1, source_target_pairs={{0,24},{4,28},{8,16},{12,20},{16,8},{20,12},{24,0},{28,4},{1,25},{... | collective-permute-start | bytes 393224 | tf_op jit(solution)/shard_map/ppermute | solution.py:277
  28.4 5.5 %collective-permute-start.12 = (f32[16,2048]{1,0:T(8,128)S(1)}, f32[16,2048]{1,0:T(8,128)S(1)}, u32[]{:S(2)}, u32[]{:S(2)}) collective-permute-start(f32[16,2048]{1,0:T(8,128)S(1)} %add_add_fusion.refs_4_), channel_id=1, source_target_pairs={{0,8},{4,12},{8,0},{12,4},{16,24},{20,28},{24,16},{28,20},{1,9},{5... | collective-permute-start | bytes 393224 | tf_op jit(solution)/shard_map/ppermute | solution.py:277
  29.0 5.0 %collective-permute-start.11 = (f32[16,2048]{1,0:T(8,128)S(1)}, f32[16,2048]{1,0:T(8,128)S(1)}, u32[]{:S(2)}, u32[]{:S(2)}) collective-permute-start(f32[16,2048]{1,0:T(8,128)S(1)} %add_add_fusion.refs_4_), channel_id=1, source_target_pairs={{0,16},{4,20},{8,24},{12,28},{16,0},{20,4},{24,8},{28,12},{1,17},{... | collective-permute-start | bytes 393224 | tf_op jit(solution)/shard_map/ppermute | solution.py:277
  32.6 1.6 %collective-permute-start.13 = (f32[32,2048]{1,0:T(8,128)S(1)}, f32[32,2048]{1,0:T(8,128)S(1)}, u32[]{:S(2)}, u32[]{:S(2)}) collective-permute-start(f32[32,2048]{1,0:T(8,128)S(1)} %pad_maximum_fusion), channel_id=1, source_target_pairs={{0,4},{4,0},{8,12},{12,8},{16,20},{20,16},{24,28},{28,24},{1,5},{5... | collective-permute-start | bytes 786440 | tf_op jit(solution)/shard_map/ppermute | solution.py:300
  34.0 1.6 %collective-permute-start.14 = (f32[32,2048]{1,0:T(8,128)S(1)}, f32[32,2048]{1,0:T(8,128)S(1)}, u32[]{:S(2)}, u32[]{:S(2)}) collective-permute-start(f32[32,2048]{1,0:T(8,128)S(1)} %pad_maximum_fusion.1), channel_id=1, source_target_pairs={{0,4},{4,0},{8,12},{12,8},{16,20},{20,16},{24,28},{28,24},{1,5},{5... | collective-permute-start | bytes 786440 | tf_op jit(solution)/shard_map/ppermute | solution.py:300

commit v7 on v6

--- a/solution.py
+++ b/solution.py
@@ -153,7 +153,7 @@
     mine_ref[...] = jnp.dot(scaled_ref[...], delta_ref[...], preferred_element_type=F32)
 
 
-def split_kernel(steps, mine_ref, came_ref, *part_refs):
+def split_kernel(steps, mine_ref, came_ref, _, *part_refs):
     part = part_refs[0].shape[0]
     chip = lax.axis_index("dp") // 2
     for step, out_ref in zip(steps, part_refs):
@@ -276,17 +276,18 @@
     def chips(piece, s):
         return lax.ppermute(piece, "dp", [(i, i ^ (2 * s)) for i in range(n_dp)])
 
+    unique = call(
+        functools.partial(unique_kernel, owners), [((cap + tail, emb), F32)] * owners,
+        4 * width * examples * emb, named, xgrad, clip, targets, mine, specs=[VMEM] * 4 + [ANY],
+    )
     hops = (0, 2, 3, 1)
     if n_dp == 8:
         parts = call(
-            functools.partial(split_kernel, hops), [((part, hid), F32)] * 4, half * hid, mine, came
+            functools.partial(split_kernel, hops), [((part, hid), F32)] * 4, half * hid, mine, came,
+            unique[0], specs=[VMEM, VMEM, ANY],
         )
     else:
         parts = [mine + came]
-    unique = call(
-        functools.partial(unique_kernel, owners), [((cap + tail, emb), F32)] * owners,
-        4 * width * examples * emb, named, xgrad, clip, targets, parts[0], specs=[VMEM] * 4 + [ANY],
-    )
     for s in range(1, owners):
         unique[s] = lax.ppermute(unique[s], "mp", steps[s - 1])
     if n_dp == 8:

time: 36.6 us -> 36.5 us (level)
    ppermute x6, waiting for transfers between devices: 2.68 us -> 3.99 us  [chips(): return lax.ppermute(piece, 'dp', [(i, i ^ 2 * s) for i in range(n_dp)])]
    ppermute x3, waiting for transfers between devices: 3.55 us -> 2.78 us  [on_device(): unique[s] = lax.ppermute(unique[s], 'mp', steps[s - 1])]
    ppermute x1, waiting for transfers between devices: 1.42 us -> 0.94 us  [on_device(): came = lax.ppermute(theirs, 'dp', swap)]
  transfers between devices with their start and end apart: 15 -> 15, of which waited for: 7 -> 8; matrix products, arithmetic and copies ran while one was open for 0% -> 0% of each run, Pallas kernels for 12% -> 12%
where the time goes in v7:
time: 36.5 us; the launch traced here: 36.3 us
  starting transfers between devices  17.5 us (48%)
  waiting for transfers between devices  9.69 us (27%)
  Pallas kernels  8.33 us (23%)
  between operations  0.75 us (2%)
    pallas_call x8, Pallas kernels, call(): pl.pallas_call(kernel, out_shape=[jax.ShapeDtypeStruct(shape, dtype) for...  8.33 us
    ppermute x6, starting transfers between devices, chips(): return lax.ppermute(piece, 'dp', [(i, i ^ 2 * s) for i in range(n_dp)])  7.16 us
    ppermute x3, starting transfers between devices, on_device(): norms = [lax.ppermute(partial, 'mp', r) for r in rounds(owners)]  5.75 us
    ppermute x3, starting transfers between devices, on_device(): unique[s] = lax.ppermute(unique[s], 'mp', steps[s - 1])  4.34 us
    ppermute x6, waiting for transfers between devices, chips(): return lax.ppermute(piece, 'dp', [(i, i ^ 2 * s) for i in range(n_dp)])  3.99 us
    ppermute x3, waiting for transfers between devices, on_device(): unique[s] = lax.ppermute(unique[s], 'mp', steps[s - 1])  2.78 us
    ppermute x3, waiting for transfers between devices, on_device(): norms = [lax.ppermute(partial, 'mp', r) for r in rounds(owners)]  1.88 us
    ppermute x1, waiting for transfers between devices, on_device(): came = lax.ppermute(theirs, 'dp', swap)  0.94 us
  transfers between devices with their start and end apart: 15, of which 8 were waited for; matrix products, arithmetic and copies ran while one was open for 0% of the time, Pallas kernels for 12%

profile of v7, /device:TPU:0, one launch (start us, length us, event | category | flops | bytes accessed | tf_op | source)
XLA Modules:
  0.0 36.3 jit_solution(6602385024616895938)
XLA Ops:
  0.6 0.0 copy-start.1
  0.6 0.0 copy-start
  0.7 2.7 %shard_map.77 = (f32[128,512]{1,0:T(8,128)S(1)}, bf16[512,2048]{1,0:T(8,128)(2,1)S(1)}, bf16[512,128]{1,0:T(8,128)(2,1)S(1)}, s32[8,512]{1,0:T(8,128)S(1)}, f32[2,512]{1,0:T(2,128)S(1)}) custom-call(bf16[512,2048]{1,0:T(8,128)(2,1)} %delta_hbm.1, bf16[128,2048]{1,0:T(8,128)(2,1)} %w_hbm.1, bf16[512,128]{1,0:T(8,128)(2,1)} %pooled_hbm.1, s32[8,512]{1,0:T(8,128)} %bitcast.8), custom_call_target="tpu_custom_call" | custom-call | flops 268435456 | bytes 2768896 | tf_op jit(solution)/shard_map/pallas_call | solution.py:42
  3.4 5.1 %collective-permute-start.2 = (f32[2,512]{1,0:T(2,128)S(1)}, f32[2,512]{1,0:T(2,128)S(1)}, u32[]{:S(2)}, u32[]{:S(2)}) collective-permute-start(f32[2,512]{1,0:T(2,128)S(1)} %get-tuple-element.33.refs_3_), channel_id=1, source_target_pairs={{0,3},{1,2},{2,1},{3,0},{4,7},{5,6},{6,5},{7,4},{8,11},{9,10},{10,... | collective-permute-start | bytes 12296 | tf_op jit(solution)/shard_map/ppermute | solution.py:255
  8.5 0.0 collective-permute-start.1
  8.5 0.6 %collective-permute-start = (f32[2,512]{1,0:T(2,128)S(1)}, f32[2,512]{1,0:T(2,128)S(1)}, u32[]{:S(2)}, u32[]{:S(2)}) collective-permute-start(f32[2,512]{1,0:T(2,128)S(1)} %get-tuple-element.33.refs_3_), channel_id=1, source_target_pairs={{0,1},{1,0},{2,3},{3,2},{4,5},{5,4},{6,7},{7,6},{8,9},{9,8},{10,11... | collective-permute-start | bytes 12296 | tf_op jit(solution)/shard_map/ppermute | solution.py:255
  9.1 0.0 copy-done.1
  9.1 0.0 copy-done
  9.2 2.0 %shard_map.78 = (bf16[1024,512]{1,0:T(8,128)(2,1)S(1)}, f32[128,512]{1,0:T(8,128)S(1)}, f32[4,1,256]{2,1,0:T(1,128)S(1)}, f32[1,512]{1,0:T(1,128)S(1)}) custom-call(s32[1,4]{1,0:T(1,128)S(1)} %bitcast.7, s32[8,512]{1,0:T(8,128)S(1)} %get-tuple-element.34.slots_ref, bf16[512,128]{1,0:T(8,128)(2,1)S(1)} %get-tuple-element.35.pooled_ref, ...), custom_call_target="tpu_custom_call" | custom-call | flops 33554432 | bytes 2248720 | tf_op jit(solution)/shard_map/pallas_call | solution.py:42
  11.1 0.0 collective-permute-done.2.refs_2_
  11.1 1.9 %collective-permute-done.1.refs_1_ = f32[2,512]{1,0:T(2,128)S(1)} collective-permute-done((f32[2,512]{1,0:T(2,128)S(1)}, f32[2,512]{1,0:T(2,128)S(1)}, u32[]{:S(2)}, u32[]{:S(2)}) %collective-permute-start.1) | collective-permute-done | bytes 4128 | tf_op jit(solution)/shard_map/ppermute | solution.py:255
  13.0 0.0 collective-permute-done.refs_0_
  13.0 0.5 %shard_map.79 = (f32[1,512]{1,0:T(1,128)S(1)}, bf16[64,512]{1,0:T(8,128)(2,1)S(1)}, f32[64,2048]{1,0:T(8,128)S(1)}) custom-call(f32[2,512]{1,0:T(2,128)S(1)} %collective-permute-done.refs_0_, f32[2,512]{1,0:T(2,128)S(1)} %collective-permute-done.1.refs_1_, f32[2,512]{1,0:T(2,128)S(1)} %collective-permute-done.2.refs_2_, ...), custom_call_target="tpu_custom_call" | custom-call | flops 134217728 | bytes 3426304 | tf_op jit(solution)/shard_map/pallas_call | solution.py:42
  13.5 0.1 collective-permute-start.3
  13.6 0.5 %shard_map.80._.mine_ref = f32[64,2048]{1,0:T(8,128)S(1)} custom-call(bf16[64,512]{1,0:T(8,128)(2,1)S(1)} %get-tuple-element.40.scaled_ref, bf16[512,2048]{1,0:T(8,128)(2,1)S(1)} %get-tuple-element.36.delta_ref.refs_6_), custom_call_target="tpu_custom_call" | custom-call | flops 134217728 | bytes 2162688 | tf_op jit(solution)/shard_map/pallas_call | solution.py:42
  14.1 0.5 %shard_map.81 = (f32[264,128]{1,0:T(8,128)S(1)}, f32[264,128]{1,0:T(8,128)S(1)}, f32[264,128]{1,0:T(8,128)S(1)}, f32[264,128]{1,0:T(8,128)S(1)}) custom-call(bf16[1024,512]{1,0:T(8,128)(2,1)S(1)} %get-tuple-element.39.refs_7_.named_ref, f32[128,512]{1,0:T(8,128)S(1)} %get-tuple-element.42.xgrad_ref, f32[1,512]{1,0:T(1,128)S(1)} %get-tuple-element.43.clip_ref, ...), custom_call_target="tpu_custom_call" | custom-call | flops 268435456 | bytes 1841152 | tf_op jit(solution)/shard_map/pallas_call | solution.py:42
  14.6 0.9 %collective-permute-done.3.came_ref = f32[64,2048]{1,0:T(8,128)S(1)} collective-permute-done((f32[64,2048]{1,0:T(8,128)S(1)}, f32[64,2048]{1,0:T(8,128)S(1)}, u32[]{:S(2)}, u32[]{:S(2)}) %collective-permute-start.3) | collective-permute-done | bytes 524320 | tf_op jit(solution)/shard_map/ppermute | solution.py:273
  15.5 0.1 shard_map.82
  15.6 1.6 %collective-permute-start.4 = (f32[16,2048]{1,0:T(8,128)S(1)}, f32[16,2048]{1,0:T(8,128)S(1)}, u32[]{:S(2)}, u32[]{:S(2)}) collective-permute-start(f32[16,2048]{1,0:T(8,128)S(1)} %get-tuple-element.47), channel_id=1, source_target_pairs={{0,16},{4,20},{8,24},{12,28},{16,0},{20,4},{24,8},{28,12},{1,17},{... | collective-permute-start | bytes 393224 | tf_op jit(solution)/shard_map/ppermute | solution.py:277
  17.1 1.4 %collective-permute-start.5 = (f32[16,2048]{1,0:T(8,128)S(1)}, f32[16,2048]{1,0:T(8,128)S(1)}, u32[]{:S(2)}, u32[]{:S(2)}) collective-permute-start(f32[16,2048]{1,0:T(8,128)S(1)} %get-tuple-element.48), channel_id=1, source_target_pairs={{0,24},{4,28},{8,16},{12,20},{16,8},{20,12},{24,0},{28,4},{1,25},{... | collective-permute-start | bytes 393224 | tf_op jit(solution)/shard_map/ppermute | solution.py:277
  18.6 0.5 %collective-permute-start.6 = (f32[16,2048]{1,0:T(8,128)S(1)}, f32[16,2048]{1,0:T(8,128)S(1)}, u32[]{:S(2)}, u32[]{:S(2)}) collective-permute-start(f32[16,2048]{1,0:T(8,128)S(1)} %get-tuple-element.49), channel_id=1, source_target_pairs={{0,8},{4,12},{8,0},{12,4},{16,24},{20,28},{24,16},{28,20},{1,9},{5... | collective-permute-start | bytes 393224 | tf_op jit(solution)/shard_map/ppermute | solution.py:277
  19.1 0.0 collective-permute-start.7
  19.1 2.4 %collective-permute-start.8 = (f32[264,128]{1,0:T(8,128)S(1)}, f32[264,128]{1,0:T(8,128)S(1)}, u32[]{:S(2)}, u32[]{:S(2)}) collective-permute-start(f32[264,128]{1,0:T(8,128)S(1)} %get-tuple-element.55), channel_id=1, source_target_pairs={{0,2},{1,3},{2,0},{3,1},{4,6},{5,7},{6,4},{7,5},{8,10},{9,11},{10,... | collective-permute-start | bytes 405512 | tf_op jit(solution)/shard_map/ppermute | solution.py:292
  21.6 1.9 %collective-permute-done.4 = f32[16,2048]{1,0:T(8,128)S(1)} collective-permute-done((f32[16,2048]{1,0:T(8,128)S(1)}, f32[16,2048]{1,0:T(8,128)S(1)}, u32[]{:S(2)}, u32[]{:S(2)}) %collective-permute-start.4) | collective-permute-done | bytes 131104 | tf_op jit(solution)/shard_map/ppermute | solution.py:277
  23.5 1.9 %collective-permute-start.9 = (f32[264,128]{1,0:T(8,128)S(1)}, f32[264,128]{1,0:T(8,128)S(1)}, u32[]{:S(2)}, u32[]{:S(2)}) collective-permute-start(f32[264,128]{1,0:T(8,128)S(1)} %get-tuple-element.56), channel_id=1, source_target_pairs={{0,3},{1,2},{2,1},{3,0},{4,7},{5,6},{6,5},{7,4},{8,11},{9,10},{10,... | collective-permute-start | bytes 405512 | tf_op jit(solution)/shard_map/ppermute | solution.py:292
  25.4 0.0 collective-permute-done.5
  25.4 0.0 collective-permute-done.6
  25.5 3.0 %collective-permute-start.10 = (f32[16,2048]{1,0:T(8,128)S(1)}, f32[16,2048]{1,0:T(8,128)S(1)}, u32[]{:S(2)}, u32[]{:S(2)}) collective-permute-start(f32[16,2048]{1,0:T(8,128)S(1)} %add_add_fusion.refs_4_), channel_id=1, source_target_pairs={{0,24},{4,28},{8,16},{12,20},{16,8},{20,12},{24,0},{28,4},{1,25},{... | collective-permute-start | bytes 393224 | tf_op jit(solution)/shard_map/ppermute | solution.py:277
  28.4 0.5 %collective-permute-start.12 = (f32[16,2048]{1,0:T(8,128)S(1)}, f32[16,2048]{1,0:T(8,128)S(1)}, u32[]{:S(2)}, u32[]{:S(2)}) collective-permute-start(f32[16,2048]{1,0:T(8,128)S(1)} %add_add_fusion.refs_4_), channel_id=1, source_target_pairs={{0,8},{4,12},{8,0},{12,4},{16,24},{20,28},{24,16},{28,20},{1,9},{5... | collective-permute-start | bytes 393224 | tf_op jit(solution)/shard_map/ppermute | solution.py:277
  29.0 0.0 collective-permute-done.7.refs_1_
  29.0 0.1 collective-permute-start.11
  29.1 2.8 %collective-permute-done.8.refs_2_ = f32[264,128]{1,0:T(8,128)S(1)} collective-permute-done((f32[264,128]{1,0:T(8,128)S(1)}, f32[264,128]{1,0:T(8,128)S(1)}, u32[]{:S(2)}, u32[]{:S(2)}) %collective-permute-start.8) | collective-permute-done | bytes 135200 | tf_op jit(solution)/shard_map/ppermute | solution.py:292
  31.8 0.0 collective-permute-done.9.refs_3_
  31.8 0.5 %collective-permute-done.10.refs_5_ = f32[16,2048]{1,0:T(8,128)S(1)} collective-permute-done((f32[16,2048]{1,0:T(8,128)S(1)}, f32[16,2048]{1,0:T(8,128)S(1)}, u32[]{:S(2)}, u32[]{:S(2)}) %collective-permute-start.10) | collective-permute-done | bytes 131104 | tf_op jit(solution)/shard_map/ppermute | solution.py:277
  32.4 0.1 collective-permute-start.13
  32.5 1.4 %collective-permute-done.12.refs_7_ = f32[16,2048]{1,0:T(8,128)S(1)} collective-permute-done((f32[16,2048]{1,0:T(8,128)S(1)}, f32[16,2048]{1,0:T(8,128)S(1)}, u32[]{:S(2)}, u32[]{:S(2)}) %collective-permute-start.12) | collective-permute-done | bytes 131104 | tf_op jit(solution)/shard_map/ppermute | solution.py:277
  33.9 0.1 collective-permute-done.11.refs_6_
  34.0 0.1 collective-permute-start.14
  34.1 0.0 collective-permute-done.13.refs_8_
  34.1 1.4 %shard_map.83 = (f32[4,512,128]{2,1,0:T(8,128)}, f32[128,2048]{1,0:T(8,128)}) custom-call(f32[264,128]{1,0:T(8,128)S(1)} %get-tuple-element.57._.refs_0_, f32[264,128]{1,0:T(8,128)S(1)} %collective-permute-done.7.refs_1_, f32[264,128]{1,0:T(8,128)S(1)} %collective-permute-done.8.refs_2_, f32[264,128]{1,0:T(8,128)S(1)} %collective-permute-done.9.refs_3_, ...), custom_call_target="tpu_custom_call" | custom-call | flops 268435456 | bytes 1327104 | tf_op jit(solution)/shard_map/pallas_call | solution.py:42
  35.5 0.1 collective-permute-done.14.end_ref
  35.6 0.7 %shard_map.84 = f32[128,2048]{1,0:T(8,128)} custom-call(f32[128,2048]{1,0:T(8,128)} %get-tuple-element.62._, f32[32,2048]{1,0:T(8,128)S(1)} %collective-permute-done.14.end_ref), custom_call_target="tpu_custom_call", output_to_operand_aliasing={{}: (0, {})} | custom-call | bytes 1310720 | tf_op jit(solution)/shard_map/pallas_call | solution.py:42
  (3 shorter events, 0.1 us)
Async XLA Ops:
  0.6 8.5 %copy-start.1 = (s32[1,1,4]{2,1,0:T(1,128)S(1)}, s32[1,1,4]{2,1,0:T(1,128)}, u32[]{:S(2)}) copy-start(s32[1,1,4]{2,1,0:T(1,128)} %param.11) | copy-start | bytes 52
  0.6 8.5 %copy-start = (s32[1,1,1024]{2,1,0:T(1,128)S(1)}, s32[1,1,1024]{2,1,0:T(1,128)}, u32[]{:S(2)}) copy-start(s32[1,1,1024]{2,1,0:T(1,128)} %param.10) | copy-start | bytes 12292
  3.4 7.7 %collective-permute-start.2 = (f32[2,512]{1,0:T(2,128)S(1)}, f32[2,512]{1,0:T(2,128)S(1)}, u32[]{:S(2)}, u32[]{:S(2)}) collective-permute-start(f32[2,512]{1,0:T(2,128)S(1)} %get-tuple-element.33.refs_3_), channel_id=1, source_target_pairs={{0,3},{1,2},{2,1},{3,0},{4,7},{5,6},{6,5},{7,4},{8,11},{9,10},{10,... | collective-permute-start | bytes 12296 | tf_op jit(solution)/shard_map/ppermute | solution.py:255
  8.5 4.5 %collective-permute-start.1 = (f32[2,512]{1,0:T(2,128)S(1)}, f32[2,512]{1,0:T(2,128)S(1)}, u32[]{:S(2)}, u32[]{:S(2)}) collective-permute-start(f32[2,512]{1,0:T(2,128)S(1)} %get-tuple-element.33.refs_3_), channel_id=1, source_target_pairs={{0,2},{1,3},{2,0},{3,1},{4,6},{5,7},{6,4},{7,5},{8,10},{9,11},{10,... | collective-permute-start | bytes 12296 | tf_op jit(solution)/shard_map/ppermute | solution.py:255
  8.5 4.5 %collective-permute-start = (f32[2,512]{1,0:T(2,128)S(1)}, f32[2,512]{1,0:T(2,128)S(1)}, u32[]{:S(2)}, u32[]{:S(2)}) collective-permute-start(f32[2,512]{1,0:T(2,128)S(1)} %get-tuple-element.33.refs_3_), channel_id=1, source_target_pairs={{0,1},{1,0},{2,3},{3,2},{4,5},{5,4},{6,7},{7,6},{8,9},{9,8},{10,11... | collective-permute-start | bytes 12296 | tf_op jit(solution)/shard_map/ppermute | solution.py:255
  13.5 2.0 %collective-permute-start.3 = (f32[64,2048]{1,0:T(8,128)S(1)}, f32[64,2048]{1,0:T(8,128)S(1)}, u32[]{:S(2)}, u32[]{:S(2)}) collective-permute-start(f32[64,2048]{1,0:T(8,128)S(1)} %get-tuple-element.41), channel_id=1, source_target_pairs={{0,4},{4,0},{8,12},{12,8},{16,20},{20,16},{24,28},{28,24},{1,5},{5... | collective-permute-start | bytes 1572872 | tf_op jit(solution)/shard_map/ppermute | solution.py:273
  15.6 8.0 %collective-permute-start.4 = (f32[16,2048]{1,0:T(8,128)S(1)}, f32[16,2048]{1,0:T(8,128)S(1)}, u32[]{:S(2)}, u32[]{:S(2)}) collective-permute-start(f32[16,2048]{1,0:T(8,128)S(1)} %get-tuple-element.47), channel_id=1, source_target_pairs={{0,16},{4,20},{8,24},{12,28},{16,0},{20,4},{24,8},{28,12},{1,17},{... | collective-permute-start | bytes 393224 | tf_op jit(solution)/shard_map/ppermute | solution.py:277
  17.1 8.3 %collective-permute-start.5 = (f32[16,2048]{1,0:T(8,128)S(1)}, f32[16,2048]{1,0:T(8,128)S(1)}, u32[]{:S(2)}, u32[]{:S(2)}) collective-permute-start(f32[16,2048]{1,0:T(8,128)S(1)} %get-tuple-element.48), channel_id=1, source_target_pairs={{0,24},{4,28},{8,16},{12,20},{16,8},{20,12},{24,0},{28,4},{1,25},{... | collective-permute-start | bytes 393224 | tf_op jit(solution)/shard_map/ppermute | solution.py:277
  18.6 6.8 %collective-permute-start.6 = (f32[16,2048]{1,0:T(8,128)S(1)}, f32[16,2048]{1,0:T(8,128)S(1)}, u32[]{:S(2)}, u32[]{:S(2)}) collective-permute-start(f32[16,2048]{1,0:T(8,128)S(1)} %get-tuple-element.49), channel_id=1, source_target_pairs={{0,8},{4,12},{8,0},{12,4},{16,24},{20,28},{24,16},{28,20},{1,9},{5... | collective-permute-start | bytes 393224 | tf_op jit(solution)/shard_map/ppermute | solution.py:277
  19.1 9.8 %collective-permute-start.7 = (f32[264,128]{1,0:T(8,128)S(1)}, f32[264,128]{1,0:T(8,128)S(1)}, u32[]{:S(2)}, u32[]{:S(2)}) collective-permute-start(f32[264,128]{1,0:T(8,128)S(1)} %get-tuple-element.54), channel_id=1, source_target_pairs={{0,1},{1,0},{2,3},{3,2},{4,5},{5,4},{6,7},{7,6},{8,9},{9,8},{10,11... | collective-permute-start | bytes 405512 | tf_op jit(solution)/shard_map/ppermute | solution.py:292
  19.1 12.7 %collective-permute-start.8 = (f32[264,128]{1,0:T(8,128)S(1)}, f32[264,128]{1,0:T(8,128)S(1)}, u32[]{:S(2)}, u32[]{:S(2)}) collective-permute-start(f32[264,128]{1,0:T(8,128)S(1)} %get-tuple-element.55), channel_id=1, source_target_pairs={{0,2},{1,3},{2,0},{3,1},{4,6},{5,7},{6,4},{7,5},{8,10},{9,11},{10,... | collective-permute-start | bytes 405512 | tf_op jit(solution)/shard_map/ppermute | solution.py:292
  23.5 8.3 %collective-permute-start.9 = (f32[264,128]{1,0:T(8,128)S(1)}, f32[264,128]{1,0:T(8,128)S(1)}, u32[]{:S(2)}, u32[]{:S(2)}) collective-permute-start(f32[264,128]{1,0:T(8,128)S(1)} %get-tuple-element.56), channel_id=1, source_target_pairs={{0,3},{1,2},{2,1},{3,0},{4,7},{5,6},{6,5},{7,4},{8,11},{9,10},{10,... | collective-permute-start | bytes 405512 | tf_op jit(solution)/shard_map/ppermute | solution.py:292
  25.5 6.9 %collective-permute-start.10 = (f32[16,2048]{1,0:T(8,128)S(1)}, f32[16,2048]{1,0:T(8,128)S(1)}, u32[]{:S(2)}, u32[]{:S(2)}) collective-permute-start(f32[16,2048]{1,0:T(8,128)S(1)} %add_add_fusion.refs_4_), channel_id=1, source_target_pairs={{0,24},{4,28},{8,16},{12,20},{16,8},{20,12},{24,0},{28,4},{1,25},{... | collective-permute-start | bytes 393224 | tf_op jit(solution)/shard_map/ppermute | solution.py:277
  28.4 5.5 %collective-permute-start.12 = (f32[16,2048]{1,0:T(8,128)S(1)}, f32[16,2048]{1,0:T(8,128)S(1)}, u32[]{:S(2)}, u32[]{:S(2)}) collective-permute-start(f32[16,2048]{1,0:T(8,128)S(1)} %add_add_fusion.refs_4_), channel_id=1, source_target_pairs={{0,8},{4,12},{8,0},{12,4},{16,24},{20,28},{24,16},{28,20},{1,9},{5... | collective-permute-start | bytes 393224 | tf_op jit(solution)/shard_map/ppermute | solution.py:277
  29.0 5.0 %collective-permute-start.11 = (f32[16,2048]{1,0:T(8,128)S(1)}, f32[16,2048]{1,0:T(8,128)S(1)}, u32[]{:S(2)}, u32[]{:S(2)}) collective-permute-start(f32[16,2048]{1,0:T(8,128)S(1)} %add_add_fusion.refs_4_), channel_id=1, source_target_pairs={{0,16},{4,20},{8,24},{12,28},{16,0},{20,4},{24,8},{28,12},{1,17},{... | collective-permute-start | bytes 393224 | tf_op jit(solution)/shard_map/ppermute | solution.py:277
  32.4 1.7 %collective-permute-start.13 = (f32[32,2048]{1,0:T(8,128)S(1)}, f32[32,2048]{1,0:T(8,128)S(1)}, u32[]{:S(2)}, u32[]{:S(2)}) collective-permute-start(f32[32,2048]{1,0:T(8,128)S(1)} %pad_maximum_fusion), channel_id=1, source_target_pairs={{0,4},{4,0},{8,12},{12,8},{16,20},{20,16},{24,28},{28,24},{1,5},{5... | collective-permute-start | bytes 786440 | tf_op jit(solution)/shard_map/ppermute | solution.py:301
  34.0 1.6 %collective-permute-start.14 = (f32[32,2048]{1,0:T(8,128)S(1)}, f32[32,2048]{1,0:T(8,128)S(1)}, u32[]{:S(2)}, u32[]{:S(2)}) collective-permute-start(f32[32,2048]{1,0:T(8,128)S(1)} %pad_maximum_fusion.1), channel_id=1, source_target_pairs={{0,4},{4,0},{8,12},{12,8},{16,20},{20,16},{24,28},{28,24},{1,5},{5... | collective-permute-start | bytes 786440 | tf_op jit(solution)/shard_map/ppermute | solution.py:301

commit v8 on v7

--- a/solution.py
+++ b/solution.py
@@ -80,6 +80,9 @@
     for shift in range(1, looks):
         same = same + jnp.where(slots == pltpu.roll(slots, shift, 0), 1.0, 0.0)
     repeats = jnp.sum(same, axis=0, keepdims=True)
+    for q in range(0, examples, 128):
+        piece = pooled_ref[q:q + 128, :].astype(F32)
+        partial_ref[0:1, q:q + 128] = jnp.sum((piece * piece).T, axis=0, keepdims=True)
     copies[0].wait()
     norms = []
     for i, r in enumerate(blocks):
@@ -91,11 +94,6 @@
         xgrad_ref[:, r:r + CHUNK] = xgrad
         norms.append(jnp.sum(xgrad * xgrad, axis=0, keepdims=True))
     for i, r in enumerate(blocks):
-        sums = []
-        for q in range(r, r + CHUNK, 128):
-            piece = pooled_ref[q:q + 128, :].astype(F32)
-            sums.append(jnp.sum((piece * piece).T, axis=0, keepdims=True))
-        partial_ref[0:1, r:r + CHUNK] = jnp.concatenate(sums, axis=1)
         partial_ref[1:2, r:r + CHUNK] = repeats[:, r:r + CHUNK] * norms[i]
 
 

time: 36.5 us -> 36.5 us (level)
  no operation moved by 1% of the time
where the time goes in v8:
time: 36.5 us; the launch traced here: 36.3 us
  starting transfers between devices  17.5 us (48%)
  waiting for transfers between devices  9.69 us (27%)
  Pallas kernels  8.33 us (23%)
  between operations  0.75 us (2%)
    pallas_call x8, Pallas kernels, call(): pl.pallas_call(kernel, out_shape=[jax.ShapeDtypeStruct(shape, dtype) for...  8.33 us
    ppermute x6, starting transfers between devices, chips(): return lax.ppermute(piece, 'dp', [(i, i ^ 2 * s) for i in range(n_dp)])  7.16 us
    ppermute x3, starting transfers between devices, on_device(): norms = [lax.ppermute(partial, 'mp', r) for r in rounds(owners)]  5.75 us
    ppermute x3, starting transfers between devices, on_device(): unique[s] = lax.ppermute(unique[s], 'mp', steps[s - 1])  4.34 us
    ppermute x6, waiting for transfers between devices, chips(): return lax.ppermute(piece, 'dp', [(i, i ^ 2 * s) for i in range(n_dp)])  3.99 us
    ppermute x3, waiting for transfers between devices, on_device(): unique[s] = lax.ppermute(unique[s], 'mp', steps[s - 1])  2.78 us
    ppermute x3, waiting for transfers between devices, on_device(): norms = [lax.ppermute(partial, 'mp', r) for r in rounds(owners)]  1.88 us
    ppermute x1, waiting for transfers between devices, on_device(): came = lax.ppermute(theirs, 'dp', swap)  0.94 us
  transfers between devices with their start and end apart: 15, of which 8 were waited for; matrix products, arithmetic and copies ran while one was open for 0% of the time, Pallas kernels for 12%

profile of v8, /device:TPU:0, one launch (start us, length us, event | category | flops | bytes accessed | tf_op | source)
XLA Modules:
  0.0 36.3 jit_solution(15548749133756219210)
XLA Ops:
  0.6 0.0 copy-start.1
  0.6 0.0 copy-start
  0.7 2.7 %shard_map.77 = (f32[128,512]{1,0:T(8,128)S(1)}, bf16[512,2048]{1,0:T(8,128)(2,1)S(1)}, bf16[512,128]{1,0:T(8,128)(2,1)S(1)}, s32[8,512]{1,0:T(8,128)S(1)}, f32[2,512]{1,0:T(2,128)S(1)}) custom-call(bf16[512,2048]{1,0:T(8,128)(2,1)} %delta_hbm.1, bf16[128,2048]{1,0:T(8,128)(2,1)} %w_hbm.1, bf16[512,128]{1,0:T(8,128)(2,1)} %pooled_hbm.1, s32[8,512]{1,0:T(8,128)} %bitcast.8), custom_call_target="tpu_custom_call" | custom-call | flops 268435456 | bytes 2768896 | tf_op jit(solution)/shard_map/pallas_call | solution.py:42
  3.4 5.1 %collective-permute-start.2 = (f32[2,512]{1,0:T(2,128)S(1)}, f32[2,512]{1,0:T(2,128)S(1)}, u32[]{:S(2)}, u32[]{:S(2)}) collective-permute-start(f32[2,512]{1,0:T(2,128)S(1)} %get-tuple-element.33.refs_3_), channel_id=1, source_target_pairs={{0,3},{1,2},{2,1},{3,0},{4,7},{5,6},{6,5},{7,4},{8,11},{9,10},{10,... | collective-permute-start | bytes 12296 | tf_op jit(solution)/shard_map/ppermute | solution.py:253
  8.5 0.0 collective-permute-start.1
  8.5 0.6 %collective-permute-start = (f32[2,512]{1,0:T(2,128)S(1)}, f32[2,512]{1,0:T(2,128)S(1)}, u32[]{:S(2)}, u32[]{:S(2)}) collective-permute-start(f32[2,512]{1,0:T(2,128)S(1)} %get-tuple-element.33.refs_3_), channel_id=1, source_target_pairs={{0,1},{1,0},{2,3},{3,2},{4,5},{5,4},{6,7},{7,6},{8,9},{9,8},{10,11... | collective-permute-start | bytes 12296 | tf_op jit(solution)/shard_map/ppermute | solution.py:253
  9.1 0.0 copy-done.1
  9.1 0.0 copy-done
  9.1 2.0 %shard_map.78 = (bf16[1024,512]{1,0:T(8,128)(2,1)S(1)}, f32[128,512]{1,0:T(8,128)S(1)}, f32[4,1,256]{2,1,0:T(1,128)S(1)}, f32[1,512]{1,0:T(1,128)S(1)}) custom-call(s32[1,4]{1,0:T(1,128)S(1)} %bitcast.7, s32[8,512]{1,0:T(8,128)S(1)} %get-tuple-element.34.slots_ref, bf16[512,128]{1,0:T(8,128)(2,1)S(1)} %get-tuple-element.35.pooled_ref, ...), custom_call_target="tpu_custom_call" | custom-call | flops 33554432 | bytes 2248720 | tf_op jit(solution)/shard_map/pallas_call | solution.py:42
  11.1 0.0 collective-permute-done.2.refs_2_
  11.1 1.9 %collective-permute-done.1.refs_1_ = f32[2,512]{1,0:T(2,128)S(1)} collective-permute-done((f32[2,512]{1,0:T(2,128)S(1)}, f32[2,512]{1,0:T(2,128)S(1)}, u32[]{:S(2)}, u32[]{:S(2)}) %collective-permute-start.1) | collective-permute-done | bytes 4128 | tf_op jit(solution)/shard_map/ppermute | solution.py:253
  13.0 0.0 collective-permute-done.refs_0_
  13.0 0.5 %shard_map.79 = (f32[1,512]{1,0:T(1,128)S(1)}, bf16[64,512]{1,0:T(8,128)(2,1)S(1)}, f32[64,2048]{1,0:T(8,128)S(1)}) custom-call(f32[2,512]{1,0:T(2,128)S(1)} %collective-permute-done.refs_0_, f32[2,512]{1,0:T(2,128)S(1)} %collective-permute-done.1.refs_1_, f32[2,512]{1,0:T(2,128)S(1)} %collective-permute-done.2.refs_2_, ...), custom_call_target="tpu_custom_call" | custom-call | flops 134217728 | bytes 3426304 | tf_op jit(solution)/shard_map/pallas_call | solution.py:42
  13.5 0.1 collective-permute-start.3
  13.6 0.5 %shard_map.80._.mine_ref = f32[64,2048]{1,0:T(8,128)S(1)} custom-call(bf16[64,512]{1,0:T(8,128)(2,1)S(1)} %get-tuple-element.40.scaled_ref, bf16[512,2048]{1,0:T(8,128)(2,1)S(1)} %get-tuple-element.36.delta_ref.refs_6_), custom_call_target="tpu_custom_call" | custom-call | flops 134217728 | bytes 2162688 | tf_op jit(solution)/shard_map/pallas_call | solution.py:42
  14.1 0.5 %shard_map.81 = (f32[264,128]{1,0:T(8,128)S(1)}, f32[264,128]{1,0:T(8,128)S(1)}, f32[264,128]{1,0:T(8,128)S(1)}, f32[264,128]{1,0:T(8,128)S(1)}) custom-call(bf16[1024,512]{1,0:T(8,128)(2,1)S(1)} %get-tuple-element.39.refs_7_.named_ref, f32[128,512]{1,0:T(8,128)S(1)} %get-tuple-element.42.xgrad_ref, f32[1,512]{1,0:T(1,128)S(1)} %get-tuple-element.43.clip_ref, ...), custom_call_target="tpu_custom_call" | custom-call | flops 268435456 | bytes 1841152 | tf_op jit(solution)/shard_map/pallas_call | solution.py:42
  14.6 0.9 %collective-permute-done.3.came_ref = f32[64,2048]{1,0:T(8,128)S(1)} collective-permute-done((f32[64,2048]{1,0:T(8,128)S(1)}, f32[64,2048]{1,0:T(8,128)S(1)}, u32[]{:S(2)}, u32[]{:S(2)}) %collective-permute-start.3) | collective-permute-done | bytes 524320 | tf_op jit(solution)/shard_map/ppermute | solution.py:271
  15.5 0.1 shard_map.82
  15.6 1.6 %collective-permute-start.4 = (f32[16,2048]{1,0:T(8,128)S(1)}, f32[16,2048]{1,0:T(8,128)S(1)}, u32[]{:S(2)}, u32[]{:S(2)}) collective-permute-start(f32[16,2048]{1,0:T(8,128)S(1)} %get-tuple-element.47), channel_id=1, source_target_pairs={{0,16},{4,20},{8,24},{12,28},{16,0},{20,4},{24,8},{28,12},{1,17},{... | collective-permute-start | bytes 393224 | tf_op jit(solution)/shard_map/ppermute | solution.py:275
  17.1 1.4 %collective-permute-start.5 = (f32[16,2048]{1,0:T(8,128)S(1)}, f32[16,2048]{1,0:T(8,128)S(1)}, u32[]{:S(2)}, u32[]{:S(2)}) collective-permute-start(f32[16,2048]{1,0:T(8,128)S(1)} %get-tuple-element.48), channel_id=1, source_target_pairs={{0,24},{4,28},{8,16},{12,20},{16,8},{20,12},{24,0},{28,4},{1,25},{... | collective-permute-start | bytes 393224 | tf_op jit(solution)/shard_map/ppermute | solution.py:275
  18.6 0.5 %collective-permute-start.6 = (f32[16,2048]{1,0:T(8,128)S(1)}, f32[16,2048]{1,0:T(8,128)S(1)}, u32[]{:S(2)}, u32[]{:S(2)}) collective-permute-start(f32[16,2048]{1,0:T(8,128)S(1)} %get-tuple-element.49), channel_id=1, source_target_pairs={{0,8},{4,12},{8,0},{12,4},{16,24},{20,28},{24,16},{28,20},{1,9},{5... | collective-permute-start | bytes 393224 | tf_op jit(solution)/shard_map/ppermute | solution.py:275
  19.1 0.0 collective-permute-start.7
  19.1 2.4 %collective-permute-start.8 = (f32[264,128]{1,0:T(8,128)S(1)}, f32[264,128]{1,0:T(8,128)S(1)}, u32[]{:S(2)}, u32[]{:S(2)}) collective-permute-start(f32[264,128]{1,0:T(8,128)S(1)} %get-tuple-element.55), channel_id=1, source_target_pairs={{0,2},{1,3},{2,0},{3,1},{4,6},{5,7},{6,4},{7,5},{8,10},{9,11},{10,... | collective-permute-start | bytes 405512 | tf_op jit(solution)/shard_map/ppermute | solution.py:290
  21.6 1.9 %collective-permute-done.4 = f32[16,2048]{1,0:T(8,128)S(1)} collective-permute-done((f32[16,2048]{1,0:T(8,128)S(1)}, f32[16,2048]{1,0:T(8,128)S(1)}, u32[]{:S(2)}, u32[]{:S(2)}) %collective-permute-start.4) | collective-permute-done | bytes 131104 | tf_op jit(solution)/shard_map/ppermute | solution.py:275
  23.5 1.9 %collective-permute-start.9 = (f32[264,128]{1,0:T(8,128)S(1)}, f32[264,128]{1,0:T(8,128)S(1)}, u32[]{:S(2)}, u32[]{:S(2)}) collective-permute-start(f32[264,128]{1,0:T(8,128)S(1)} %get-tuple-element.56), channel_id=1, source_target_pairs={{0,3},{1,2},{2,1},{3,0},{4,7},{5,6},{6,5},{7,4},{8,11},{9,10},{10,... | collective-permute-start | bytes 405512 | tf_op jit(solution)/shard_map/ppermute | solution.py:290
  25.4 0.0 collective-permute-done.5
  25.4 0.0 collective-permute-done.6
  25.5 3.0 %collective-permute-start.10 = (f32[16,2048]{1,0:T(8,128)S(1)}, f32[16,2048]{1,0:T(8,128)S(1)}, u32[]{:S(2)}, u32[]{:S(2)}) collective-permute-start(f32[16,2048]{1,0:T(8,128)S(1)} %add_add_fusion.refs_4_), channel_id=1, source_target_pairs={{0,24},{4,28},{8,16},{12,20},{16,8},{20,12},{24,0},{28,4},{1,25},{... | collective-permute-start | bytes 393224 | tf_op jit(solution)/shard_map/ppermute | solution.py:275
  28.4 0.5 %collective-permute-start.12 = (f32[16,2048]{1,0:T(8,128)S(1)}, f32[16,2048]{1,0:T(8,128)S(1)}, u32[]{:S(2)}, u32[]{:S(2)}) collective-permute-start(f32[16,2048]{1,0:T(8,128)S(1)} %add_add_fusion.refs_4_), channel_id=1, source_target_pairs={{0,8},{4,12},{8,0},{12,4},{16,24},{20,28},{24,16},{28,20},{1,9},{5... | collective-permute-start | bytes 393224 | tf_op jit(solution)/shard_map/ppermute | solution.py:275
  29.0 0.0 collective-permute-done.7.refs_1_
  29.0 0.1 collective-permute-start.11
  29.1 2.8 %collective-permute-done.8.refs_2_ = f32[264,128]{1,0:T(8,128)S(1)} collective-permute-done((f32[264,128]{1,0:T(8,128)S(1)}, f32[264,128]{1,0:T(8,128)S(1)}, u32[]{:S(2)}, u32[]{:S(2)}) %collective-permute-start.8) | collective-permute-done | bytes 135200 | tf_op jit(solution)/shard_map/ppermute | solution.py:290
  31.8 0.0 collective-permute-done.9.refs_3_
  31.8 0.5 %collective-permute-done.10.refs_5_ = f32[16,2048]{1,0:T(8,128)S(1)} collective-permute-done((f32[16,2048]{1,0:T(8,128)S(1)}, f32[16,2048]{1,0:T(8,128)S(1)}, u32[]{:S(2)}, u32[]{:S(2)}) %collective-permute-start.10) | collective-permute-done | bytes 131104 | tf_op jit(solution)/shard_map/ppermute | solution.py:275
  32.4 0.1 collective-permute-start.13
  32.5 1.4 %collective-permute-done.12.refs_7_ = f32[16,2048]{1,0:T(8,128)S(1)} collective-permute-done((f32[16,2048]{1,0:T(8,128)S(1)}, f32[16,2048]{1,0:T(8,128)S(1)}, u32[]{:S(2)}, u32[]{:S(2)}) %collective-permute-start.12) | collective-permute-done | bytes 131104 | tf_op jit(solution)/shard_map/ppermute | solution.py:275
  33.9 0.1 collective-permute-done.11.refs_6_
  34.0 0.1 collective-permute-start.14
  34.1 0.0 collective-permute-done.13.refs_8_
  34.1 1.4 %shard_map.83 = (f32[4,512,128]{2,1,0:T(8,128)}, f32[128,2048]{1,0:T(8,128)}) custom-call(f32[264,128]{1,0:T(8,128)S(1)} %get-tuple-element.57._.refs_0_, f32[264,128]{1,0:T(8,128)S(1)} %collective-permute-done.7.refs_1_, f32[264,128]{1,0:T(8,128)S(1)} %collective-permute-done.8.refs_2_, f32[264,128]{1,0:T(8,128)S(1)} %collective-permute-done.9.refs_3_, ...), custom_call_target="tpu_custom_call" | custom-call | flops 268435456 | bytes 1327104 | tf_op jit(solution)/shard_map/pallas_call | solution.py:42
  35.5 0.1 collective-permute-done.14.end_ref
  35.6 0.7 %shard_map.84 = f32[128,2048]{1,0:T(8,128)} custom-call(f32[128,2048]{1,0:T(8,128)} %get-tuple-element.62._, f32[32,2048]{1,0:T(8,128)S(1)} %collective-permute-done.14.end_ref), custom_call_target="tpu_custom_call", output_to_operand_aliasing={{}: (0, {})} | custom-call | bytes 1310720 | tf_op jit(solution)/shard_map/pallas_call | solution.py:42
  (3 shorter events, 0.1 us)
Async XLA Ops:
  0.6 8.5 %copy-start.1 = (s32[1,1,4]{2,1,0:T(1,128)S(1)}, s32[1,1,4]{2,1,0:T(1,128)}, u32[]{:S(2)}) copy-start(s32[1,1,4]{2,1,0:T(1,128)} %param.11) | copy-start | bytes 52
  0.6 8.5 %copy-start = (s32[1,1,1024]{2,1,0:T(1,128)S(1)}, s32[1,1,1024]{2,1,0:T(1,128)}, u32[]{:S(2)}) copy-start(s32[1,1,1024]{2,1,0:T(1,128)} %param.10) | copy-start | bytes 12292
  3.4 7.7 %collective-permute-start.2 = (f32[2,512]{1,0:T(2,128)S(1)}, f32[2,512]{1,0:T(2,128)S(1)}, u32[]{:S(2)}, u32[]{:S(2)}) collective-permute-start(f32[2,512]{1,0:T(2,128)S(1)} %get-tuple-element.33.refs_3_), channel_id=1, source_target_pairs={{0,3},{1,2},{2,1},{3,0},{4,7},{5,6},{6,5},{7,4},{8,11},{9,10},{10,... | collective-permute-start | bytes 12296 | tf_op jit(solution)/shard_map/ppermute | solution.py:253
  8.5 4.5 %collective-permute-start.1 = (f32[2,512]{1,0:T(2,128)S(1)}, f32[2,512]{1,0:T(2,128)S(1)}, u32[]{:S(2)}, u32[]{:S(2)}) collective-permute-start(f32[2,512]{1,0:T(2,128)S(1)} %get-tuple-element.33.refs_3_), channel_id=1, source_target_pairs={{0,2},{1,3},{2,0},{3,1},{4,6},{5,7},{6,4},{7,5},{8,10},{9,11},{10,... | collective-permute-start | bytes 12296 | tf_op jit(solution)/shard_map/ppermute | solution.py:253
  8.5 4.5 %collective-permute-start = (f32[2,512]{1,0:T(2,128)S(1)}, f32[2,512]{1,0:T(2,128)S(1)}, u32[]{:S(2)}, u32[]{:S(2)}) collective-permute-start(f32[2,512]{1,0:T(2,128)S(1)} %get-tuple-element.33.refs_3_), channel_id=1, source_target_pairs={{0,1},{1,0},{2,3},{3,2},{4,5},{5,4},{6,7},{7,6},{8,9},{9,8},{10,11... | collective-permute-start | bytes 12296 | tf_op jit(solution)/shard_map/ppermute | solution.py:253
  13.5 2.0 %collective-permute-start.3 = (f32[64,2048]{1,0:T(8,128)S(1)}, f32[64,2048]{1,0:T(8,128)S(1)}, u32[]{:S(2)}, u32[]{:S(2)}) collective-permute-start(f32[64,2048]{1,0:T(8,128)S(1)} %get-tuple-element.41), channel_id=1, source_target_pairs={{0,4},{4,0},{8,12},{12,8},{16,20},{20,16},{24,28},{28,24},{1,5},{5... | collective-permute-start | bytes 1572872 | tf_op jit(solution)/shard_map/ppermute | solution.py:271
  15.6 8.0 %collective-permute-start.4 = (f32[16,2048]{1,0:T(8,128)S(1)}, f32[16,2048]{1,0:T(8,128)S(1)}, u32[]{:S(2)}, u32[]{:S(2)}) collective-permute-start(f32[16,2048]{1,0:T(8,128)S(1)} %get-tuple-element.47), channel_id=1, source_target_pairs={{0,16},{4,20},{8,24},{12,28},{16,0},{20,4},{24,8},{28,12},{1,17},{... | collective-permute-start | bytes 393224 | tf_op jit(solution)/shard_map/ppermute | solution.py:275
  17.1 8.3 %collective-permute-start.5 = (f32[16,2048]{1,0:T(8,128)S(1)}, f32[16,2048]{1,0:T(8,128)S(1)}, u32[]{:S(2)}, u32[]{:S(2)}) collective-permute-start(f32[16,2048]{1,0:T(8,128)S(1)} %get-tuple-element.48), channel_id=1, source_target_pairs={{0,24},{4,28},{8,16},{12,20},{16,8},{20,12},{24,0},{28,4},{1,25},{... | collective-permute-start | bytes 393224 | tf_op jit(solution)/shard_map/ppermute | solution.py:275
  18.6 6.8 %collective-permute-start.6 = (f32[16,2048]{1,0:T(8,128)S(1)}, f32[16,2048]{1,0:T(8,128)S(1)}, u32[]{:S(2)}, u32[]{:S(2)}) collective-permute-start(f32[16,2048]{1,0:T(8,128)S(1)} %get-tuple-element.49), channel_id=1, source_target_pairs={{0,8},{4,12},{8,0},{12,4},{16,24},{20,28},{24,16},{28,20},{1,9},{5... | collective-permute-start | bytes 393224 | tf_op jit(solution)/shard_map/ppermute | solution.py:275
  19.1 9.8 %collective-permute-start.7 = (f32[264,128]{1,0:T(8,128)S(1)}, f32[264,128]{1,0:T(8,128)S(1)}, u32[]{:S(2)}, u32[]{:S(2)}) collective-permute-start(f32[264,128]{1,0:T(8,128)S(1)} %get-tuple-element.54), channel_id=1, source_target_pairs={{0,1},{1,0},{2,3},{3,2},{4,5},{5,4},{6,7},{7,6},{8,9},{9,8},{10,11... | collective-permute-start | bytes 405512 | tf_op jit(solution)/shard_map/ppermute | solution.py:290
  19.1 12.7 %collective-permute-start.8 = (f32[264,128]{1,0:T(8,128)S(1)}, f32[264,128]{1,0:T(8,128)S(1)}, u32[]{:S(2)}, u32[]{:S(2)}) collective-permute-start(f32[264,128]{1,0:T(8,128)S(1)} %get-tuple-element.55), channel_id=1, source_target_pairs={{0,2},{1,3},{2,0},{3,1},{4,6},{5,7},{6,4},{7,5},{8,10},{9,11},{10,... | collective-permute-start | bytes 405512 | tf_op jit(solution)/shard_map/ppermute | solution.py:290
  23.5 8.3 %collective-permute-start.9 = (f32[264,128]{1,0:T(8,128)S(1)}, f32[264,128]{1,0:T(8,128)S(1)}, u32[]{:S(2)}, u32[]{:S(2)}) collective-permute-start(f32[264,128]{1,0:T(8,128)S(1)} %get-tuple-element.56), channel_id=1, source_target_pairs={{0,3},{1,2},{2,1},{3,0},{4,7},{5,6},{6,5},{7,4},{8,11},{9,10},{10,... | collective-permute-start | bytes 405512 | tf_op jit(solution)/shard_map/ppermute | solution.py:290
  25.5 6.9 %collective-permute-start.10 = (f32[16,2048]{1,0:T(8,128)S(1)}, f32[16,2048]{1,0:T(8,128)S(1)}, u32[]{:S(2)}, u32[]{:S(2)}) collective-permute-start(f32[16,2048]{1,0:T(8,128)S(1)} %add_add_fusion.refs_4_), channel_id=1, source_target_pairs={{0,24},{4,28},{8,16},{12,20},{16,8},{20,12},{24,0},{28,4},{1,25},{... | collective-permute-start | bytes 393224 | tf_op jit(solution)/shard_map/ppermute | solution.py:275
  28.4 5.5 %collective-permute-start.12 = (f32[16,2048]{1,0:T(8,128)S(1)}, f32[16,2048]{1,0:T(8,128)S(1)}, u32[]{:S(2)}, u32[]{:S(2)}) collective-permute-start(f32[16,2048]{1,0:T(8,128)S(1)} %add_add_fusion.refs_4_), channel_id=1, source_target_pairs={{0,8},{4,12},{8,0},{12,4},{16,24},{20,28},{24,16},{28,20},{1,9},{5... | collective-permute-start | bytes 393224 | tf_op jit(solution)/shard_map/ppermute | solution.py:275
  29.0 5.0 %collective-permute-start.11 = (f32[16,2048]{1,0:T(8,128)S(1)}, f32[16,2048]{1,0:T(8,128)S(1)}, u32[]{:S(2)}, u32[]{:S(2)}) collective-permute-start(f32[16,2048]{1,0:T(8,128)S(1)} %add_add_fusion.refs_4_), channel_id=1, source_target_pairs={{0,16},{4,20},{8,24},{12,28},{16,0},{20,4},{24,8},{28,12},{1,17},{... | collective-permute-start | bytes 393224 | tf_op jit(solution)/shard_map/ppermute | solution.py:275
  32.4 1.7 %collective-permute-start.13 = (f32[32,2048]{1,0:T(8,128)S(1)}, f32[32,2048]{1,0:T(8,128)S(1)}, u32[]{:S(2)}, u32[]{:S(2)}) collective-permute-start(f32[32,2048]{1,0:T(8,128)S(1)} %pad_maximum_fusion), channel_id=1, source_target_pairs={{0,4},{4,0},{8,12},{12,8},{16,20},{20,16},{24,28},{28,24},{1,5},{5... | collective-permute-start | bytes 786440 | tf_op jit(solution)/shard_map/ppermute | solution.py:299
  34.0 1.6 %collective-permute-start.14 = (f32[32,2048]{1,0:T(8,128)S(1)}, f32[32,2048]{1,0:T(8,128)S(1)}, u32[]{:S(2)}, u32[]{:S(2)}) collective-permute-start(f32[32,2048]{1,0:T(8,128)S(1)} %pad_maximum_fusion.1), channel_id=1, source_target_pairs={{0,4},{4,0},{8,12},{12,8},{16,20},{20,16},{24,28},{28,24},{1,5},{5... | collective-permute-start | bytes 786440 | tf_op jit(solution)/shard_map/ppermute | solution.py:299

commit v9 on v7

--- a/solution.py
+++ b/solution.py
@@ -294,7 +294,7 @@
         got = [chips(piece, s) for piece, s in zip(parts[1:], hops[1:])]
         got, unique[0] = lax.optimization_barrier((got, unique[0]))
         total = parts[0] + got[0] + got[1] + got[2]
-        order = (0, 3, 2, 1)
+        order = (0, 3, 1, 2)
         own = [total] + [chips(total, s) for s in order[1:]]
         own[0], *unique = lax.optimization_barrier((own[0], *unique))
         near = jnp.concatenate(own[:2])

time: 36.5 us -> 36.4 us (level)
  no operation moved by 1% of the time
where the time goes in v9:
time: 36.4 us; the launch traced here: 36.3 us
  starting transfers between devices  17.5 us (48%)
  waiting for transfers between devices  9.62 us (26%)
  Pallas kernels  8.33 us (23%)
  between operations  0.75 us (2%)
    pallas_call x8, Pallas kernels, call(): pl.pallas_call(kernel, out_shape=[jax.ShapeDtypeStruct(shape, dtype) for...  8.33 us
    ppermute x6, starting transfers between devices, chips(): return lax.ppermute(piece, 'dp', [(i, i ^ 2 * s) for i in range(n_dp)])  7.16 us
    ppermute x3, starting transfers between devices, on_device(): norms = [lax.ppermute(partial, 'mp', r) for r in rounds(owners)]  5.75 us
    ppermute x3, starting transfers between devices, on_device(): unique[s] = lax.ppermute(unique[s], 'mp', steps[s - 1])  4.34 us
    ppermute x6, waiting for transfers between devices, chips(): return lax.ppermute(piece, 'dp', [(i, i ^ 2 * s) for i in range(n_dp)])  3.93 us
    ppermute x3, waiting for transfers between devices, on_device(): unique[s] = lax.ppermute(unique[s], 'mp', steps[s - 1])  2.78 us
    ppermute x3, waiting for transfers between devices, on_device(): norms = [lax.ppermute(partial, 'mp', r) for r in rounds(owners)]  1.88 us
    ppermute x1, waiting for transfers between devices, on_device(): came = lax.ppermute(theirs, 'dp', swap)  0.94 us
  transfers between devices with their start and end apart: 15, of which 8 were waited for; matrix products, arithmetic and copies ran while one was open for 0% of the time, Pallas kernels for 12%

profile of v9, /device:TPU:0, one launch (start us, length us, event | category | flops | bytes accessed | tf_op | source)
XLA Modules:
  0.0 36.3 jit_solution(1400701902436132794)
XLA Ops:
  0.6 0.0 copy-start.1
  0.6 0.0 copy-start
  0.7 2.7 %shard_map.77 = (f32[128,512]{1,0:T(8,128)S(1)}, bf16[512,2048]{1,0:T(8,128)(2,1)S(1)}, bf16[512,128]{1,0:T(8,128)(2,1)S(1)}, s32[8,512]{1,0:T(8,128)S(1)}, f32[2,512]{1,0:T(2,128)S(1)}) custom-call(bf16[512,2048]{1,0:T(8,128)(2,1)} %delta_hbm.1, bf16[128,2048]{1,0:T(8,128)(2,1)} %w_hbm.1, bf16[512,128]{1,0:T(8,128)(2,1)} %pooled_hbm.1, s32[8,512]{1,0:T(8,128)} %bitcast.8), custom_call_target="tpu_custom_call" | custom-call | flops 268435456 | bytes 2768896 | tf_op jit(solution)/shard_map/pallas_call | solution.py:42
  3.4 5.1 %collective-permute-start.2 = (f32[2,512]{1,0:T(2,128)S(1)}, f32[2,512]{1,0:T(2,128)S(1)}, u32[]{:S(2)}, u32[]{:S(2)}) collective-permute-start(f32[2,512]{1,0:T(2,128)S(1)} %get-tuple-element.33.refs_3_), channel_id=1, source_target_pairs={{0,3},{1,2},{2,1},{3,0},{4,7},{5,6},{6,5},{7,4},{8,11},{9,10},{10,... | collective-permute-start | bytes 12296 | tf_op jit(solution)/shard_map/ppermute | solution.py:255
  8.5 0.0 collective-permute-start.1
  8.5 0.6 %collective-permute-start = (f32[2,512]{1,0:T(2,128)S(1)}, f32[2,512]{1,0:T(2,128)S(1)}, u32[]{:S(2)}, u32[]{:S(2)}) collective-permute-start(f32[2,512]{1,0:T(2,128)S(1)} %get-tuple-element.33.refs_3_), channel_id=1, source_target_pairs={{0,1},{1,0},{2,3},{3,2},{4,5},{5,4},{6,7},{7,6},{8,9},{9,8},{10,11... | collective-permute-start | bytes 12296 | tf_op jit(solution)/shard_map/ppermute | solution.py:255
  9.1 0.0 copy-done.1
  9.1 0.0 copy-done
  9.2 2.0 %shard_map.78 = (bf16[1024,512]{1,0:T(8,128)(2,1)S(1)}, f32[128,512]{1,0:T(8,128)S(1)}, f32[4,1,256]{2,1,0:T(1,128)S(1)}, f32[1,512]{1,0:T(1,128)S(1)}) custom-call(s32[1,4]{1,0:T(1,128)S(1)} %bitcast.7, s32[8,512]{1,0:T(8,128)S(1)} %get-tuple-element.34.slots_ref, bf16[512,128]{1,0:T(8,128)(2,1)S(1)} %get-tuple-element.35.pooled_ref, ...), custom_call_target="tpu_custom_call" | custom-call | flops 33554432 | bytes 2248720 | tf_op jit(solution)/shard_map/pallas_call | solution.py:42
  11.1 0.0 collective-permute-done.2.refs_2_
  11.1 1.9 %collective-permute-done.1.refs_1_ = f32[2,512]{1,0:T(2,128)S(1)} collective-permute-done((f32[2,512]{1,0:T(2,128)S(1)}, f32[2,512]{1,0:T(2,128)S(1)}, u32[]{:S(2)}, u32[]{:S(2)}) %collective-permute-start.1) | collective-permute-done | bytes 4128 | tf_op jit(solution)/shard_map/ppermute | solution.py:255
  13.0 0.0 collective-permute-done.refs_0_
  13.0 0.5 %shard_map.79 = (f32[1,512]{1,0:T(1,128)S(1)}, bf16[64,512]{1,0:T(8,128)(2,1)S(1)}, f32[64,2048]{1,0:T(8,128)S(1)}) custom-call(f32[2,512]{1,0:T(2,128)S(1)} %collective-permute-done.refs_0_, f32[2,512]{1,0:T(2,128)S(1)} %collective-permute-done.1.refs_1_, f32[2,512]{1,0:T(2,128)S(1)} %collective-permute-done.2.refs_2_, ...), custom_call_target="tpu_custom_call" | custom-call | flops 134217728 | bytes 3426304 | tf_op jit(solution)/shard_map/pallas_call | solution.py:42
  13.5 0.1 collective-permute-start.3
  13.6 0.5 %shard_map.80._.mine_ref = f32[64,2048]{1,0:T(8,128)S(1)} custom-call(bf16[64,512]{1,0:T(8,128)(2,1)S(1)} %get-tuple-element.40.scaled_ref, bf16[512,2048]{1,0:T(8,128)(2,1)S(1)} %get-tuple-element.36.delta_ref.refs_6_), custom_call_target="tpu_custom_call" | custom-call | flops 134217728 | bytes 2162688 | tf_op jit(solution)/shard_map/pallas_call | solution.py:42
  14.1 0.5 %shard_map.81 = (f32[264,128]{1,0:T(8,128)S(1)}, f32[264,128]{1,0:T(8,128)S(1)}, f32[264,128]{1,0:T(8,128)S(1)}, f32[264,128]{1,0:T(8,128)S(1)}) custom-call(bf16[1024,512]{1,0:T(8,128)(2,1)S(1)} %get-tuple-element.39.refs_7_.named_ref, f32[128,512]{1,0:T(8,128)S(1)} %get-tuple-element.42.xgrad_ref, f32[1,512]{1,0:T(1,128)S(1)} %get-tuple-element.43.clip_ref, ...), custom_call_target="tpu_custom_call" | custom-call | flops 268435456 | bytes 1841152 | tf_op jit(solution)/shard_map/pallas_call | solution.py:42
  14.6 0.9 %collective-permute-done.3.came_ref = f32[64,2048]{1,0:T(8,128)S(1)} collective-permute-done((f32[64,2048]{1,0:T(8,128)S(1)}, f32[64,2048]{1,0:T(8,128)S(1)}, u32[]{:S(2)}, u32[]{:S(2)}) %collective-permute-start.3) | collective-permute-done | bytes 524320 | tf_op jit(solution)/shard_map/ppermute | solution.py:273
  15.5 0.1 shard_map.82
  15.6 1.6 %collective-permute-start.4 = (f32[16,2048]{1,0:T(8,128)S(1)}, f32[16,2048]{1,0:T(8,128)S(1)}, u32[]{:S(2)}, u32[]{:S(2)}) collective-permute-start(f32[16,2048]{1,0:T(8,128)S(1)} %get-tuple-element.47), channel_id=1, source_target_pairs={{0,16},{4,20},{8,24},{12,28},{16,0},{20,4},{24,8},{28,12},{1,17},{... | collective-permute-start | bytes 393224 | tf_op jit(solution)/shard_map/ppermute | solution.py:277
  17.1 1.4 %collective-permute-start.5 = (f32[16,2048]{1,0:T(8,128)S(1)}, f32[16,2048]{1,0:T(8,128)S(1)}, u32[]{:S(2)}, u32[]{:S(2)}) collective-permute-start(f32[16,2048]{1,0:T(8,128)S(1)} %get-tuple-element.48), channel_id=1, source_target_pairs={{0,24},{4,28},{8,16},{12,20},{16,8},{20,12},{24,0},{28,4},{1,25},{... | collective-permute-start | bytes 393224 | tf_op jit(solution)/shard_map/ppermute | solution.py:277
  18.6 0.5 %collective-permute-start.6 = (f32[16,2048]{1,0:T(8,128)S(1)}, f32[16,2048]{1,0:T(8,128)S(1)}, u32[]{:S(2)}, u32[]{:S(2)}) collective-permute-start(f32[16,2048]{1,0:T(8,128)S(1)} %get-tuple-element.49), channel_id=1, source_target_pairs={{0,8},{4,12},{8,0},{12,4},{16,24},{20,28},{24,16},{28,20},{1,9},{5... | collective-permute-start | bytes 393224 | tf_op jit(solution)/shard_map/ppermute | solution.py:277
  19.1 0.0 collective-permute-start.7
  19.1 2.4 %collective-permute-start.8 = (f32[264,128]{1,0:T(8,128)S(1)}, f32[264,128]{1,0:T(8,128)S(1)}, u32[]{:S(2)}, u32[]{:S(2)}) collective-permute-start(f32[264,128]{1,0:T(8,128)S(1)} %get-tuple-element.55), channel_id=1, source_target_pairs={{0,2},{1,3},{2,0},{3,1},{4,6},{5,7},{6,4},{7,5},{8,10},{9,11},{10,... | collective-permute-start | bytes 405512 | tf_op jit(solution)/shard_map/ppermute | solution.py:292
  21.6 1.9 %collective-permute-done.4 = f32[16,2048]{1,0:T(8,128)S(1)} collective-permute-done((f32[16,2048]{1,0:T(8,128)S(1)}, f32[16,2048]{1,0:T(8,128)S(1)}, u32[]{:S(2)}, u32[]{:S(2)}) %collective-permute-start.4) | collective-permute-done | bytes 131104 | tf_op jit(solution)/shard_map/ppermute | solution.py:277
  23.5 1.9 %collective-permute-start.9 = (f32[264,128]{1,0:T(8,128)S(1)}, f32[264,128]{1,0:T(8,128)S(1)}, u32[]{:S(2)}, u32[]{:S(2)}) collective-permute-start(f32[264,128]{1,0:T(8,128)S(1)} %get-tuple-element.56), channel_id=1, source_target_pairs={{0,3},{1,2},{2,1},{3,0},{4,7},{5,6},{6,5},{7,4},{8,11},{9,10},{10,... | collective-permute-start | bytes 405512 | tf_op jit(solution)/shard_map/ppermute | solution.py:292
  25.4 0.0 collective-permute-done.5
  25.4 0.0 collective-permute-done.6
  25.5 3.0 %collective-permute-start.10 = (f32[16,2048]{1,0:T(8,128)S(1)}, f32[16,2048]{1,0:T(8,128)S(1)}, u32[]{:S(2)}, u32[]{:S(2)}) collective-permute-start(f32[16,2048]{1,0:T(8,128)S(1)} %add_add_fusion.refs_4_), channel_id=1, source_target_pairs={{0,24},{4,28},{8,16},{12,20},{16,8},{20,12},{24,0},{28,4},{1,25},{... | collective-permute-start | bytes 393224 | tf_op jit(solution)/shard_map/ppermute | solution.py:277
  28.4 0.1 collective-permute-start.12
  28.5 0.0 collective-permute-done.7.refs_1_
  28.5 0.6 %collective-permute-start.11 = (f32[16,2048]{1,0:T(8,128)S(1)}, f32[16,2048]{1,0:T(8,128)S(1)}, u32[]{:S(2)}, u32[]{:S(2)}) collective-permute-start(f32[16,2048]{1,0:T(8,128)S(1)} %add_add_fusion.refs_4_), channel_id=1, source_target_pairs={{0,8},{4,12},{8,0},{12,4},{16,24},{20,28},{24,16},{28,20},{1,9},{5... | collective-permute-start | bytes 393224 | tf_op jit(solution)/shard_map/ppermute | solution.py:277
  29.1 2.8 %collective-permute-done.8.refs_2_ = f32[264,128]{1,0:T(8,128)S(1)} collective-permute-done((f32[264,128]{1,0:T(8,128)S(1)}, f32[264,128]{1,0:T(8,128)S(1)}, u32[]{:S(2)}, u32[]{:S(2)}) %collective-permute-start.8) | collective-permute-done | bytes 135200 | tf_op jit(solution)/shard_map/ppermute | solution.py:292
  31.8 0.0 collective-permute-done.9.refs_3_
  31.8 0.3 collective-permute-done.10.refs_5_
  32.2 0.1 collective-permute-start.13
  32.2 1.5 %collective-permute-done.12.refs_7_ = f32[16,2048]{1,0:T(8,128)S(1)} collective-permute-done((f32[16,2048]{1,0:T(8,128)S(1)}, f32[16,2048]{1,0:T(8,128)S(1)}, u32[]{:S(2)}, u32[]{:S(2)}) %collective-permute-start.12) | collective-permute-done | bytes 131104 | tf_op jit(solution)/shard_map/ppermute | solution.py:277
  33.7 0.2 collective-permute-done.11.refs_6_
  33.9 0.1 collective-permute-start.14
  34.0 0.0 collective-permute-done.13.refs_8_
  34.0 1.4 %shard_map.83 = (f32[4,512,128]{2,1,0:T(8,128)}, f32[128,2048]{1,0:T(8,128)}) custom-call(f32[264,128]{1,0:T(8,128)S(1)} %get-tuple-element.57._.refs_0_, f32[264,128]{1,0:T(8,128)S(1)} %collective-permute-done.7.refs_1_, f32[264,128]{1,0:T(8,128)S(1)} %collective-permute-done.8.refs_2_, f32[264,128]{1,0:T(8,128)S(1)} %collective-permute-done.9.refs_3_, ...), custom_call_target="tpu_custom_call" | custom-call | flops 268435456 | bytes 1327104 | tf_op jit(solution)/shard_map/pallas_call | solution.py:42
  35.4 0.1 collective-permute-done.14.end_ref
  35.5 0.7 %shard_map.84 = f32[128,2048]{1,0:T(8,128)} custom-call(f32[128,2048]{1,0:T(8,128)} %get-tuple-element.62._, f32[32,2048]{1,0:T(8,128)S(1)} %collective-permute-done.14.end_ref), custom_call_target="tpu_custom_call", output_to_operand_aliasing={{}: (0, {})} | custom-call | bytes 1310720 | tf_op jit(solution)/shard_map/pallas_call | solution.py:42
  (3 shorter events, 0.1 us)
Async XLA Ops:
  0.6 8.5 %copy-start.1 = (s32[1,1,4]{2,1,0:T(1,128)S(1)}, s32[1,1,4]{2,1,0:T(1,128)}, u32[]{:S(2)}) copy-start(s32[1,1,4]{2,1,0:T(1,128)} %param.11) | copy-start | bytes 52
  0.6 8.5 %copy-start = (s32[1,1,1024]{2,1,0:T(1,128)S(1)}, s32[1,1,1024]{2,1,0:T(1,128)}, u32[]{:S(2)}) copy-start(s32[1,1,1024]{2,1,0:T(1,128)} %param.10) | copy-start | bytes 12292
  3.4 7.7 %collective-permute-start.2 = (f32[2,512]{1,0:T(2,128)S(1)}, f32[2,512]{1,0:T(2,128)S(1)}, u32[]{:S(2)}, u32[]{:S(2)}) collective-permute-start(f32[2,512]{1,0:T(2,128)S(1)} %get-tuple-element.33.refs_3_), channel_id=1, source_target_pairs={{0,3},{1,2},{2,1},{3,0},{4,7},{5,6},{6,5},{7,4},{8,11},{9,10},{10,... | collective-permute-start | bytes 12296 | tf_op jit(solution)/shard_map/ppermute | solution.py:255
  8.5 4.5 %collective-permute-start.1 = (f32[2,512]{1,0:T(2,128)S(1)}, f32[2,512]{1,0:T(2,128)S(1)}, u32[]{:S(2)}, u32[]{:S(2)}) collective-permute-start(f32[2,512]{1,0:T(2,128)S(1)} %get-tuple-element.33.refs_3_), channel_id=1, source_target_pairs={{0,2},{1,3},{2,0},{3,1},{4,6},{5,7},{6,4},{7,5},{8,10},{9,11},{10,... | collective-permute-start | bytes 12296 | tf_op jit(solution)/shard_map/ppermute | solution.py:255
  8.5 4.5 %collective-permute-start = (f32[2,512]{1,0:T(2,128)S(1)}, f32[2,512]{1,0:T(2,128)S(1)}, u32[]{:S(2)}, u32[]{:S(2)}) collective-permute-start(f32[2,512]{1,0:T(2,128)S(1)} %get-tuple-element.33.refs_3_), channel_id=1, source_target_pairs={{0,1},{1,0},{2,3},{3,2},{4,5},{5,4},{6,7},{7,6},{8,9},{9,8},{10,11... | collective-permute-start | bytes 12296 | tf_op jit(solution)/shard_map/ppermute | solution.py:255
  13.5 2.0 %collective-permute-start.3 = (f32[64,2048]{1,0:T(8,128)S(1)}, f32[64,2048]{1,0:T(8,128)S(1)}, u32[]{:S(2)}, u32[]{:S(2)}) collective-permute-start(f32[64,2048]{1,0:T(8,128)S(1)} %get-tuple-element.41), channel_id=1, source_target_pairs={{0,4},{4,0},{8,12},{12,8},{16,20},{20,16},{24,28},{28,24},{1,5},{5... | collective-permute-start | bytes 1572872 | tf_op jit(solution)/shard_map/ppermute | solution.py:273
  15.6 8.0 %collective-permute-start.4 = (f32[16,2048]{1,0:T(8,128)S(1)}, f32[16,2048]{1,0:T(8,128)S(1)}, u32[]{:S(2)}, u32[]{:S(2)}) collective-permute-start(f32[16,2048]{1,0:T(8,128)S(1)} %get-tuple-element.47), channel_id=1, source_target_pairs={{0,16},{4,20},{8,24},{12,28},{16,0},{20,4},{24,8},{28,12},{1,17},{... | collective-permute-start | bytes 393224 | tf_op jit(solution)/shard_map/ppermute | solution.py:277
  17.1 8.3 %collective-permute-start.5 = (f32[16,2048]{1,0:T(8,128)S(1)}, f32[16,2048]{1,0:T(8,128)S(1)}, u32[]{:S(2)}, u32[]{:S(2)}) collective-permute-start(f32[16,2048]{1,0:T(8,128)S(1)} %get-tuple-element.48), channel_id=1, source_target_pairs={{0,24},{4,28},{8,16},{12,20},{16,8},{20,12},{24,0},{28,4},{1,25},{... | collective-permute-start | bytes 393224 | tf_op jit(solution)/shard_map/ppermute | solution.py:277
  18.6 6.8 %collective-permute-start.6 = (f32[16,2048]{1,0:T(8,128)S(1)}, f32[16,2048]{1,0:T(8,128)S(1)}, u32[]{:S(2)}, u32[]{:S(2)}) collective-permute-start(f32[16,2048]{1,0:T(8,128)S(1)} %get-tuple-element.49), channel_id=1, source_target_pairs={{0,8},{4,12},{8,0},{12,4},{16,24},{20,28},{24,16},{28,20},{1,9},{5... | collective-permute-start | bytes 393224 | tf_op jit(solution)/shard_map/ppermute | solution.py:277
  19.1 9.4 %collective-permute-start.7 = (f32[264,128]{1,0:T(8,128)S(1)}, f32[264,128]{1,0:T(8,128)S(1)}, u32[]{:S(2)}, u32[]{:S(2)}) collective-permute-start(f32[264,128]{1,0:T(8,128)S(1)} %get-tuple-element.54), channel_id=1, source_target_pairs={{0,1},{1,0},{2,3},{3,2},{4,5},{5,4},{6,7},{7,6},{8,9},{9,8},{10,11... | collective-permute-start | bytes 405512 | tf_op jit(solution)/shard_map/ppermute | solution.py:292
  19.1 12.7 %collective-permute-start.8 = (f32[264,128]{1,0:T(8,128)S(1)}, f32[264,128]{1,0:T(8,128)S(1)}, u32[]{:S(2)}, u32[]{:S(2)}) collective-permute-start(f32[264,128]{1,0:T(8,128)S(1)} %get-tuple-element.55), channel_id=1, source_target_pairs={{0,2},{1,3},{2,0},{3,1},{4,6},{5,7},{6,4},{7,5},{8,10},{9,11},{10,... | collective-permute-start | bytes 405512 | tf_op jit(solution)/shard_map/ppermute | solution.py:292
  23.5 8.3 %collective-permute-start.9 = (f32[264,128]{1,0:T(8,128)S(1)}, f32[264,128]{1,0:T(8,128)S(1)}, u32[]{:S(2)}, u32[]{:S(2)}) collective-permute-start(f32[264,128]{1,0:T(8,128)S(1)} %get-tuple-element.56), channel_id=1, source_target_pairs={{0,3},{1,2},{2,1},{3,0},{4,7},{5,6},{6,5},{7,4},{8,11},{9,10},{10,... | collective-permute-start | bytes 405512 | tf_op jit(solution)/shard_map/ppermute | solution.py:292
  25.5 6.7 %collective-permute-start.10 = (f32[16,2048]{1,0:T(8,128)S(1)}, f32[16,2048]{1,0:T(8,128)S(1)}, u32[]{:S(2)}, u32[]{:S(2)}) collective-permute-start(f32[16,2048]{1,0:T(8,128)S(1)} %add_add_fusion.refs_4_), channel_id=1, source_target_pairs={{0,24},{4,28},{8,16},{12,20},{16,8},{20,12},{24,0},{28,4},{1,25},{... | collective-permute-start | bytes 393224 | tf_op jit(solution)/shard_map/ppermute | solution.py:277
  28.4 5.3 %collective-permute-start.12 = (f32[16,2048]{1,0:T(8,128)S(1)}, f32[16,2048]{1,0:T(8,128)S(1)}, u32[]{:S(2)}, u32[]{:S(2)}) collective-permute-start(f32[16,2048]{1,0:T(8,128)S(1)} %add_add_fusion.refs_4_), channel_id=1, source_target_pairs={{0,16},{4,20},{8,24},{12,28},{16,0},{20,4},{24,8},{28,12},{1,17},{... | collective-permute-start | bytes 393224 | tf_op jit(solution)/shard_map/ppermute | solution.py:277
  28.5 5.4 %collective-permute-start.11 = (f32[16,2048]{1,0:T(8,128)S(1)}, f32[16,2048]{1,0:T(8,128)S(1)}, u32[]{:S(2)}, u32[]{:S(2)}) collective-permute-start(f32[16,2048]{1,0:T(8,128)S(1)} %add_add_fusion.refs_4_), channel_id=1, source_target_pairs={{0,8},{4,12},{8,0},{12,4},{16,24},{20,28},{24,16},{28,20},{1,9},{5... | collective-permute-start | bytes 393224 | tf_op jit(solution)/shard_map/ppermute | solution.py:277
  32.2 1.9 %collective-permute-start.13 = (f32[32,2048]{1,0:T(8,128)S(1)}, f32[32,2048]{1,0:T(8,128)S(1)}, u32[]{:S(2)}, u32[]{:S(2)}) collective-permute-start(f32[32,2048]{1,0:T(8,128)S(1)} %pad_maximum_fusion), channel_id=1, source_target_pairs={{0,4},{4,0},{8,12},{12,8},{16,20},{20,16},{24,28},{28,24},{1,5},{5... | collective-permute-start | bytes 786440 | tf_op jit(solution)/shard_map/ppermute | solution.py:301
  33.9 1.6 %collective-permute-start.14 = (f32[32,2048]{1,0:T(8,128)S(1)}, f32[32,2048]{1,0:T(8,128)S(1)}, u32[]{:S(2)}, u32[]{:S(2)}) collective-permute-start(f32[32,2048]{1,0:T(8,128)S(1)} %pad_maximum_fusion.1), channel_id=1, source_target_pairs={{0,4},{4,0},{8,12},{12,8},{16,20},{20,16},{24,28},{28,24},{1,5},{5... | collective-permute-start | bytes 786440 | tf_op jit(solution)/shard_map/ppermute | solution.py:301
